TPU v7x, 256 devices: a whole 4x4x8 slice. The times are simulated.
256 devices in a mesh: inst: 4 (over y), batch: 8 (over z), tensor: 8 (over x, core).
Axes of the slice: x: 4, y: 4, z: 8, core: 2. Of those that a mesh axis runs over, the one named last changes fastest.
Arguments:
- queries: bfloat16 [256, 8192], P(('inst', 'batch'), 'tensor'), may hold values from -100 to 100
- current_key_value: bfloat16 [256, 2048], P(('inst', 'batch'), 'tensor'), may hold values from -6 to 6
- key_value_pages: bfloat16 [2048, 128, 2048], P(('inst', 'batch'), None, 'tensor'), may hold values from -6 to 6
- transfer_pages: int32 [32, 32], P(('inst', 'batch')), may hold values from -1 to 63, as said below
- request_pages: int32 [256, 8], P(('inst', 'batch')), may hold values from 0 to 95, as said below
- lengths: int32 [256], P(('inst', 'batch')), may hold values from 512 to 1024, as said below
- request_adapter: int32 [256], P('inst'), may hold values from 0 to 7
- residual_input: bfloat16 [256, 8192], P(('inst', 'tensor'), 'batch'), may hold values from -3 to 3
- wo: bfloat16 [8192, 8192], P('tensor', 'batch'), may hold values from -0.0625 to 0.0625
- down_weight: bfloat16 [8192, 512], P('tensor'), may hold values from -0.0625 to 0.0625
- up_weight: bfloat16 [512, 8192], P(None, 'batch'), may hold values from -0.75 to 0.75
Outputs:
- mixed: bfloat16 [256, 8192], P(('inst', 'tensor'), 'batch')
Inputs may be any that keep to these rules, and one draw needn't show every extreme that they name: `transfer_pages`: row s gives, for each device p of inst+batch in turn, 1 slots: a page of device s's pool that s sends to p, or -1 for an empty slot. The filled slots of one row name distinct pages and none is addressed to s itself; some row fills all 1 slots toward some device. `request_pages`: an entry e names a page as stated in the first step; an entry of 64 or more names a filled slot of the migration list. Every filled slot is named exactly once among the rows of the device it is sent to, at page positions below 4. `lengths`: some request holds 1024 tokens.
All inputs are finite; a program needn't handle non-finite values.
Results may differ from a plain program's by a relative error of at most 0.014.
Values may be sent and summed in bfloat16 or wider, within the bound.
No kernel may reach another device: no remote copies, remote signals or barrier semaphores. Data moves between devices by JAX's collectives and lax.ppermute only.
A program may use at most 64 MiB of HBM per device.

v0:
```python
import math

import jax
import jax.numpy as jnp
from jax import lax
from jax.sharding import PartitionSpec as P

HEAD_DIM = 128
GROUP = 8
ADAPTER_RANK = 64


def page_terms(query_heads, pages, counts):
    keys_part = pages[..., 0, :]
    values_part = pages[..., 1, :]
    scores = jnp.einsum(
        "nkgd,npskd->npkgs", query_heads, keys_part, preferred_element_type=jnp.float32
    ) / math.sqrt(HEAD_DIM)
    positions = jnp.arange(pages.shape[2], dtype=jnp.int32)
    live = (positions[None, None, :] < counts[:, :, None])[:, :, None, None, :]
    masked = jnp.where(live, scores, -1e30)
    page_max = jnp.max(masked, axis=-1)
    probs = jnp.where(live, jnp.exp(masked - page_max[..., None]), 0.0).astype(jnp.bfloat16)
    page_sum = jnp.sum(probs.astype(jnp.float32), axis=-1)
    page_out = jnp.einsum(
        "npkgs,npskd->npkgd", probs, values_part, preferred_element_type=jnp.float32
    )
    return (page_max, page_sum, page_out)


def combine(page_max, page_sum, page_out, own_score, new_values):
    peak = jnp.maximum(jnp.max(page_max, axis=1), own_score)
    scales = jnp.exp(page_max - peak[:, None])
    self_weight = jnp.exp(own_score - peak)
    numer = (
        jnp.sum(scales[..., None] * page_out, axis=1)
        + self_weight[..., None] * new_values[:, :, None, :]
    )
    denom = jnp.sum(scales * page_sum, axis=1) + self_weight
    return numer / denom[..., None]


def body(
    queries,
    current_key_value,
    key_value_pages,
    transfer_pages,
    request_pages,
    lengths,
    request_adapter,
    residual_input,
    wo,
    down_weight,
    up_weight,
):
    slots, pages_per = request_pages.shape
    pool_size, page_len, pool_width = key_value_pages.shape
    kv_local = pool_width // (2 * HEAD_DIM)
    query_heads = queries.reshape(slots, kv_local, GROUP, HEAD_DIM)
    fresh_kv = current_key_value.reshape(slots, kv_local, 2, HEAD_DIM)
    counts = jnp.clip(
        lengths[:, None] - jnp.arange(pages_per, dtype=jnp.int32)[None, :] * page_len, 0, page_len
    )
    outgoing = key_value_pages[jnp.maximum(transfer_pages[0], 0)]
    arrived = lax.all_to_all(outgoing, ("inst", "batch"), split_axis=0, concat_axis=0, tiled=True)
    all_pages = jnp.concatenate([key_value_pages, arrived], 0)
    chosen = all_pages[request_pages].reshape(slots, pages_per, page_len, kv_local, 2, HEAD_DIM)
    page_max, page_sum, page_out = page_terms(query_heads, chosen, counts)
    own_score = jnp.einsum(
        "nkgd,nkd->nkg", query_heads, fresh_kv[:, :, 0], preferred_element_type=jnp.float32
    ) / math.sqrt(HEAD_DIM)
    attention_output = combine(
        page_max, page_sum, page_out, own_score, fresh_kv[:, :, 1].astype(jnp.float32)
    )
    attention_output = attention_output.reshape(slots, -1).astype(jnp.bfloat16)
    out_cols = wo.shape[1]
    row_portion = lax.all_gather(attention_output, "batch", axis=0, tiled=True)
    base_piece = jnp.dot(row_portion, wo, preferred_element_type=jnp.float32)
    reduced_portion = jnp.dot(row_portion, down_weight, preferred_element_type=jnp.float32)
    products = jnp.concatenate([base_piece, reduced_portion], 1)
    base_part = products[:, :out_cols]
    reduced_total = products[:, out_cols:]
    rows_all = products.shape[0]
    adapter_choice = up_weight.shape[0] // ADAPTER_RANK
    onehot = (
        request_adapter[:, None] == jnp.arange(adapter_choice, dtype=jnp.int32)[None, :]
    ).astype(jnp.float32)
    selected = jnp.sum(
        reduced_total.reshape(rows_all, adapter_choice, ADAPTER_RANK) * onehot[:, :, None], axis=1
    )
    adapter_wide = up_weight.astype(jnp.float32)
    own_rows = rows_all // lax.axis_size("tensor")
    summed_shrink = lax.psum(selected, "tensor")
    first_own = lax.axis_index("tensor") * own_rows
    mine_shrink = lax.dynamic_slice_in_dim(summed_shrink, first_own, own_rows, 0)
    mine_onehot = lax.dynamic_slice_in_dim(onehot, first_own, own_rows, 0)
    spread_values = (mine_onehot[:, :, None] * mine_shrink[:, None, :]).reshape(
        own_rows, adapter_choice * ADAPTER_RANK
    )
    additional_rows = jnp.dot(spread_values, adapter_wide, precision=lax.Precision.HIGHEST)
    summed = lax.psum_scatter(
        base_part.astype(jnp.bfloat16), "tensor", scatter_dimension=0, tiled=True
    ).astype(jnp.float32)
    return (residual_input.astype(jnp.float32) + summed + additional_rows).astype(jnp.bfloat16)


def solution(mesh):
    return jax.shard_map(
        body,
        mesh=mesh,
        in_specs=(
            P(("inst", "batch"), "tensor"),
            P(("inst", "batch"), "tensor"),
            P(("inst", "batch"), None, "tensor"),
            P(("inst", "batch"), None),
            P(("inst", "batch"), None),
            P(("inst", "batch")),
            P("inst"),
            P(("inst", "tensor"), "batch"),
            P("tensor", "batch"),
            P("tensor", None),
            P(None, "batch"),
        ),
        out_specs=P(("inst", "tensor"), "batch"),
        check_vma=False,
    )
```

profile of v0, /device:TPU:1, one launch (start us, length us, event | category | flops | bytes accessed | tf_op | source)
XLA Modules:
  0.0 186.5 jit_solution(6440699801110881569)
XLA Ops:
  6.5 0.0 copy-start
  6.5 0.8 maximum_bitcast_fusion
  7.4 0.0 copy-start.5
  7.4 0.0 copy-start.7
  7.4 0.0 copy-start.8
  7.4 0.0 copy-start.6
  7.4 0.0 copy-start.9
  7.4 4.2 %gather_fusion = bf16[32,128,256]{2,1,0:T(8,128)(2,1)} fusion(bf16[64,128,256]{2,1,0:T(8,128)(2,1)} %param.13, s32[1024]{0:T(1024)S(1)} %pad_clamp_fusion.1), kind=kCustom, calls=%fused_computation | custom fusion | bytes 4194432 | tf_op jit(solution)/shard_map/gather | solution.py:64
  11.6 12.2 %all-to-all-start = ((bf16[32,128,256]{2,1,0:T(8,128)(2,1)}), bf16[32,128,256]{2,1,0:T(8,128)(2,1)}, u32[]{:S(2)}, u32[]{:S(2)}) async-start(bf16[32,128,256]{2,1,0:T(8,128)(2,1)} %gather_fusion), calls=%async_computation | async-start | bytes 4194304 | tf_op jit(solution)/shard_map/all_to_all | solution.py:65
  23.8 0.0 reduce-scatter.2.cloned.1.call-start
  23.9 0.0 copy-done.5
  23.9 0.1 reshape.201
  24.0 0.0 copy-done.7
  24.0 0.1 fusion.10
  24.1 0.0 copy-start.3
  24.1 0.6 copy-done.3
  24.7 0.6 constant_dynamic-slice_fusion.1
  25.3 0.0 copy-done.8
  25.3 0.1 subtract_clamp_fusion
  25.3 0.0 copy-done.6
  25.3 0.1 iota_compare_fusion.1
  25.4 0.0 copy-done.9
  25.4 0.1 fusion.13
  25.6 47.1 %all-to-all-done = bf16[32,128,256]{2,1,0:T(8,128)(2,1)} async-done(((bf16[32,128,256]{2,1,0:T(8,128)(2,1)}), bf16[32,128,256]{2,1,0:T(8,128)(2,1)}, u32[]{:S(2)}, u32[]{:S(2)}) %all-to-all-start) | async-done | bytes 2097184 | tf_op jit(solution)/shard_map/all_to_all | solution.py:65
  72.7 6.0 %pad_maximum_fusion = bf16[96,128,256]{2,1,0:T(8,128)(2,1)} fusion(bf16[32,128,256]{2,1,0:T(8,128)(2,1)} %all-to-all-done, bf16[64,128,256]{2,1,0:T(8,128)(2,1)} %param.13), kind=kLoop, calls=%fused_computation.2 | loop fusion | flops 3145728 | bytes 12582912 | tf_op jit(solution)/shard_map/concatenate | solution.py:66
  78.7 5.6 %gather_fusion.1 = bf16[64,128,256]{2,1,0:T(8,128)(2,1)} fusion(bf16[96,128,256]{2,1,0:T(8,128)(2,1)} %pad_maximum_fusion, s32[1024]{0:T(1024)S(1)} %pad_clamp_fusion), kind=kCustom, calls=%fused_computation.1 | custom fusion | bytes 8388864 | tf_op jit(solution)/shard_map/gather | solution.py:67
  84.3 6.4 %copy.16 = bf16[64,128,256]{1,2,0:T(8,128)(2,1)} copy(bf16[64,128,256]{2,1,0:T(8,128)(2,1)} %gather_fusion.1) | data formatting | bytes 8388608 | tf_op jit(solution)/shard_map/gather | solution.py:67
  90.7 0.0 copy-start.1
  90.7 2.2 %fusion.19 = (f32[8,8,8]{2,1,0:T(8,128)S(1)}, f32[8,8,1,8,128]{4,3,1,0,2:T(8,128)S(1)}) fusion(bf16[8,8,128]{2,0,1:T(8,128)(2,1)S(1)} %bitcast.74, bf16[8,8,128,1,2,128]{2,5,4,1,0,3:T(8,128)(2,1)} %bitcast.67, pred[8,8,128]{2,1,0:T(8,128)(4,1)S(1)} %iota_compare_fusion.1), kind=kOutput, calls=%fused_computation.48 | convolution fusion | flops 16973312 | bytes 2385920 | tf_op jit(solution)/shard_map/nkgd,npskd->npkgs/dot_general | solution.py:16
  92.9 0.0 copy-start.2
  92.9 0.0 copy-start.4
  92.9 0.3 convert_reduce_fusion
  93.3 2.8 %fusion.5 = f32[8,8,128]{2,1,0:T(8,128)S(1)} fusion(bf16[8,8,128,1,2,128]{2,5,4,1,0,3:T(8,128)(2,1)} %bitcast.68, f32[8,8,8]{2,1,0:T(8,128)S(1)} %get-tuple-element.10, f32[8,8,1,8,128]{4,3,1,0,2:T(8,128)S(1)} %get-tuple-element.14, f32[8,8,8]{2,1,0:T(8,128)S(1)} %get-tuple-element.13, pred[8,8,128]{2,1,0:T(8,128)(4,1)S(1)} %iota_compare_fusion.1), kind=kOutput, calls=%fused_computation.11 | convolution fusion | flops 17096704 | bytes 2404352 | tf_op jit(solution)/shard_map/npkgs,npskd->npkgd/dot_general | solution.py:25
  96.1 0.1 fusion.12
  96.2 19.4 %all_gather.3 = bf16[64,1024]{1,0:T(8,128)(2,1)S(1)} all-gather(bf16[8,1024]{1,0:T(8,128)(2,1)S(1)} %bitcast.69), channel_id=1, replica_groups=mesh['inst'=4,'batch'=8,'tensor'=8] {'batch'}, dimensions={0}, use_global_device_ids=true | all-gather | bytes 147456 | tf_op jit(solution)/shard_map/all_gather | solution.py:77
  115.6 0.0 copy-done.1
  115.6 0.9 fusion.20
  116.6 1.0 reshape.189
  117.6 1.5 multiply_reduce_fusion
  119.1 28.2 %psum.7 = f32[64,64]{1,0:T(8,128)S(1)} all-reduce(f32[64,64]{1,0:T(8,128)} %multiply_reduce_fusion), channel_id=1, replica_groups=mesh['inst'=4,'batch'=8,'tensor'=8] {'tensor'}, use_global_device_ids=true, to_apply=%region_7.8 | all-reduce | flops 4096 | bytes 32768 | tf_op jit(solution)/shard_map/psum | solution.py:93
  147.2 0.0 copy-done
  147.2 1.1 convolution_convert_fusion
  148.4 0.0 reduce-scatter.2.cloned.1.call-update
  148.4 0.8 broadcast_multiply_fusion
  149.2 0.1 mul.89
  149.2 28.5 %reduce-scatter.2.cloned.1.call-done = bf16[8,1024]{1,0:T(8,128)(2,1)} async-done(((bf16[64,1024]{1,0:T(8,128)(2,1)}), bf16[8,1024]{1,0:T(8,128)(2,1)}) %reduce-scatter.2.cloned.1.call-update) | async-done | bytes 16400 | tf_op jit(solution)/shard_map/reduce_scatter | solution.py:101
  177.8 0.0 copy-done.2
  177.8 0.0 copy-done.4
  177.8 1.8 fusion.8
  (10 shorter events, 0.1 us)
Async XLA Ops:
  6.5 140.7 %copy-start = (bf16[1024,1024]{1,0:T(8,128)(2,1)S(1)}, bf16[1024,1024]{1,0:T(8,128)(2,1)}, u32[]{:S(2)}) copy-start(bf16[1024,1024]{1,0:T(8,128)(2,1)} %param.19) | copy-start | bytes 6291460
  7.4 16.5 %copy-start.5 = (s32[8,8]{1,0:T(8,128)S(1)}, s32[8,8]{1,0:T(8,128)}, u32[]{:S(2)}) copy-start(s32[8,8]{1,0:T(8,128)} %param.15) | copy-start | bytes 772
  7.4 16.6 %copy-start.7 = (s32[64]{0:T(128)S(1)}, s32[64]{0:T(128)}, u32[]{:S(2)}) copy-start(s32[64]{0:T(128)} %param.17) | copy-start | bytes 772
  7.4 17.9 %copy-start.8 = (s32[8]{0:T(128)S(1)}, s32[8]{0:T(128)}, u32[]{:S(2)}) copy-start(s32[8]{0:T(128)} %param.16) | copy-start | bytes 100
  7.4 18.0 %copy-start.6 = (bf16[8,256]{1,0:T(8,128)(2,1)S(1)}, bf16[8,256]{1,0:T(8,128)(2,1)}, u32[]{:S(2)}) copy-start(bf16[8,256]{1,0:T(8,128)(2,1)} %param.12) | copy-start | bytes 12292
  7.4 18.0 %copy-start.9 = (bf16[8,1024]{1,0:T(8,128)(2,1)S(1)}, bf16[8,1024]{1,0:T(8,128)(2,1)}, u32[]{:S(2)}) copy-start(bf16[8,1024]{1,0:T(8,128)(2,1)} %param.11) | copy-start | bytes 49156
  11.6 61.0 %all-to-all-start = ((bf16[32,128,256]{2,1,0:T(8,128)(2,1)}), bf16[32,128,256]{2,1,0:T(8,128)(2,1)}, u32[]{:S(2)}, u32[]{:S(2)}) async-start(bf16[32,128,256]{2,1,0:T(8,128)(2,1)} %gather_fusion), calls=%async_computation | async-start | bytes 4194304 | tf_op jit(solution)/shard_map/all_to_all | solution.py:65
  23.8 153.9 %reduce-scatter.2.cloned.1.call-start = ((), (), s32[]{:S(2)}) async-start(), calls=%async_computation.2 | async-start | bytes 147456 | tf_op jit(solution)/shard_map/reduce_scatter | solution.py:101
  24.1 0.6 copy-start.3
  90.7 24.9 %copy-start.1 = (bf16[1024,512]{1,0:T(8,128)(2,1)S(1)}, bf16[1024,512]{1,0:T(8,128)(2,1)}, u32[]{:S(2)}) copy-start(bf16[1024,512]{1,0:T(8,128)(2,1)} %param.20) | copy-start | bytes 3145732
  92.9 84.9 %copy-start.2 = (bf16[512,1024]{1,0:T(8,128)(2,1)S(1)}, bf16[512,1024]{1,0:T(8,128)(2,1)}, u32[]{:S(2)}) copy-start(bf16[512,1024]{1,0:T(8,128)(2,1)} %param.21) | copy-start | bytes 3145732
  92.9 84.9 %copy-start.4 = (bf16[8,1024]{1,0:T(8,128)(2,1)S(1)}, bf16[8,1024]{1,0:T(8,128)(2,1)}, u32[]{:S(2)}) copy-start(bf16[8,1024]{1,0:T(8,128)(2,1)} %param.18) | copy-start | bytes 49156
Sparse Core Ops, SparseCore 0:
  148.5 29.2 reduce-scatter.1
where the time goes:
time: 188 us; the launch traced here: 186 us
  waiting for transfers between devices  75.7 us (40%)
  blocking collectives  47.6 us (25%)
  local copies, waits for them, and re-layouts  18.7 us (10%)
  between operations  13.6 us (7%)
  starting transfers between devices  12.2 us (6%)
  other arithmetic  9.77 us (5%)
  matrix products  9.02 us (5%)
    all_to_all x1, waiting for transfers between devices, body(): lax.all_to_all(outgoing, ('inst', 'batch'), split_axis=0, concat_axis=0,...  47.1 us
    reduce_scatter x1, waiting for transfers between devices, body(): lax.psum_scatter(base_part.astype(jnp.bfloat16), 'tensor', scatter_dimens...  28.5 us
    psum x1, blocking collectives, body(): summed_shrink = lax.psum(selected, 'tensor')  28.2 us
    all_gather x1, blocking collectives, body(): row_portion = lax.all_gather(attention_output, 'batch', axis=0, tiled=True)  19.4 us
    all_to_all x1, starting transfers between devices, body(): lax.all_to_all(outgoing, ('inst', 'batch'), split_axis=0, concat_axis=0,...  12.2 us
    gather x2, local copies, waits for them, and re-layouts, body(): all_pages[request_pages]  12 us
    concatenate x1, other arithmetic, body(): all_pages = jnp.concatenate([key_value_pages, arrived], 0)  6.02 us
    gather x1, local copies, waits for them, and re-layouts, body(): outgoing = key_value_pages[jnp.maximum(transfer_pages[0], 0)]  4.24 us
  transfers between devices with their start and end apart: 2, of which 2 were waited for; matrix products, arithmetic and copies ran while one was open for 1% of the time, Pallas kernels for 0%

commit v1 on v0

v1 whole, which is shorter than its diff:
```python
import math

import jax
import jax.numpy as jnp
from jax import lax
from jax.sharding import PartitionSpec as P

HEAD_DIM = 128
GROUP = 8
ADAPTER_RANK = 64


def body(
    queries,
    current_key_value,
    key_value_pages,
    transfer_pages,
    request_pages,
    lengths,
    request_adapter,
    residual_input,
    wo,
    down_weight,
    up_weight,
):
    slots, pages_per = request_pages.shape
    pool, page_len, _ = key_value_pages.shape
    peers = transfer_pages.shape[1]
    scale = 1.0 / math.sqrt(HEAD_DIM)
    q = queries.reshape(slots, GROUP, HEAD_DIM)
    named = request_pages[None] == pool + jnp.arange(peers, dtype=jnp.int32)[:, None, None]
    picks = jnp.any(named, axis=2)
    out_q = jnp.dot(picks.astype(jnp.bfloat16), queries, preferred_element_type=jnp.float32)
    out_q = out_q.astype(jnp.bfloat16).reshape(peers, GROUP, HEAD_DIM)
    in_q = lax.all_to_all(out_q, ("inst", "batch"), 0, 0, tiled=True)
    mine = request_pages < pool
    chosen = key_value_pages[jnp.where(mine, request_pages, 0)]
    chosen = chosen.reshape(slots, pages_per * page_len, 2 * HEAD_DIM)
    live = jnp.arange(pages_per * page_len, dtype=jnp.int32)[None] < lengths[:, None]
    live = live & jnp.repeat(mine, page_len, axis=1)
    scores = jnp.einsum(
        "ngd,nsd->ngs", q, chosen[..., :HEAD_DIM], preferred_element_type=jnp.float32
    ) * scale
    own = jnp.einsum(
        "ngd,nd->ng", q, current_key_value[:, :HEAD_DIM], preferred_element_type=jnp.float32
    ) * scale
    scores = jnp.where(live[:, None], scores, -1e30)
    top = jnp.maximum(jnp.max(scores, axis=-1), own)
    probs = jnp.where(live[:, None], jnp.exp(scores - top[..., None]), 0.0).astype(jnp.bfloat16)
    self_weight = jnp.exp(own - top)
    total = jnp.sum(probs.astype(jnp.float32), axis=-1) + self_weight
    numer = jnp.einsum(
        "ngs,nsd->ngd", probs, chosen[..., HEAD_DIM:], preferred_element_type=jnp.float32
    ) + self_weight[..., None] * current_key_value[:, None, HEAD_DIM:].astype(jnp.float32)
    sent = key_value_pages[jnp.maximum(transfer_pages[0], 0)]
    far_scores = jnp.einsum(
        "pgd,psd->pgs", in_q, sent[..., :HEAD_DIM], preferred_element_type=jnp.float32
    ) * scale
    far_top = jnp.max(far_scores, axis=-1)
    far_probs = jnp.exp(far_scores - far_top[..., None]).astype(jnp.bfloat16)
    far_total = jnp.sum(far_probs.astype(jnp.float32), axis=-1)
    far_out = jnp.einsum(
        "pgs,psd->pgd", far_probs, sent[..., HEAD_DIM:], preferred_element_type=jnp.float32
    ) / far_total[..., None]
    stats = jnp.concatenate([far_top[:, None], far_total[:, None]], 1)
    back_out = lax.all_to_all(
        far_out.astype(jnp.bfloat16), ("inst", "batch"), 0, 0, tiled=True
    )
    back_stats = lax.all_to_all(stats, ("inst", "batch"), 0, 0, tiled=True)
    back_top = back_stats[:, 0]
    back_total = back_stats[:, 1]
    reach = jnp.where(picks.T[:, :, None], back_top[None], -1e30)
    peak = jnp.maximum(jnp.max(reach, axis=1), top)
    weights = jnp.where(
        picks.T[:, :, None], jnp.exp(reach - peak[:, None]) * back_total[None], 0.0
    )
    keep = jnp.exp(top - peak)
    denom = keep * total + jnp.sum(weights, axis=1)
    numer = keep[..., None] * numer + jnp.einsum(
        "nsg,sgd->ngd", weights, back_out.astype(jnp.float32), precision=lax.Precision.HIGHEST
    )
    attended = (numer / denom[..., None]).astype(jnp.bfloat16).reshape(slots, -1)
    copies = jnp.broadcast_to(attended[None], (lax.axis_size("batch"),) + attended.shape)
    rows = lax.all_to_all(copies, "batch", 0, 0, tiled=True).reshape(-1, attended.shape[1])
    base = jnp.dot(rows, wo, preferred_element_type=jnp.float32)
    shrink = jnp.dot(rows, down_weight, preferred_element_type=jnp.float32)
    adapter_of = jnp.arange(down_weight.shape[1], dtype=jnp.int32) // ADAPTER_RANK
    shrink = jnp.where(request_adapter[:, None] == adapter_of[None], shrink, 0.0)
    high = shrink.astype(jnp.bfloat16)
    low = (shrink - high.astype(jnp.float32)).astype(jnp.bfloat16)
    both = jnp.dot(
        jnp.concatenate([high, low], 0), up_weight, preferred_element_type=jnp.float32
    )
    count = rows.shape[0]
    part = (base + both[:count] + both[count:]).astype(jnp.bfloat16)
    parts = lax.all_to_all(
        part.reshape(lax.axis_size("tensor"), -1, part.shape[1]), "tensor", 0, 0, tiled=True
    )
    summed = jnp.sum(parts.astype(jnp.float32), axis=0)
    return (residual_input.astype(jnp.float32) + summed).astype(jnp.bfloat16)


def solution(mesh):
    return jax.shard_map(
        body,
        mesh=mesh,
        in_specs=(
            P(("inst", "batch"), "tensor"),
            P(("inst", "batch"), "tensor"),
            P(("inst", "batch"), None, "tensor"),
            P(("inst", "batch"), None),
            P(("inst", "batch"), None),
            P(("inst", "batch")),
            P("inst"),
            P(("inst", "tensor"), "batch"),
            P("tensor", "batch"),
            P("tensor", None),
            P(None, "batch"),
        ),
        out_specs=P(("inst", "tensor"), "batch"),
        check_vma=False,
    )
```

time: 188 us -> 96.9 us (0.52)
  waiting for transfers between devices: 75.7 us -> 21.6 us
  blocking collectives: 47.6 us -> 14.4 us
  starting transfers between devices: 12.2 us -> 28.5 us
  between operations: 13.6 us -> 0.17 us
  local copies, waits for them, and re-layouts: 18.7 us -> 11.6 us
  matrix products: 9.02 us -> 13.4 us
  other arithmetic: 9.77 us -> 6.37 us
    reduce_scatter x1 -> x0, waiting for transfers between devices: 28.5 us -> none  [body(): lax.psum_scatter(base_part.astype(jnp.bfloat16), 'tensor', scatter_dimens...]
    psum x1 -> x0, blocking collectives: 28.2 us -> none  [body(): summed_shrink = lax.psum(selected, 'tensor')]
    all_to_all x1 -> x4, waiting for transfers between devices: 47.1 us -> 21.6 us  [the longest x1 7.82 us: body(): lax.all_to_all(copies, 'batch', 0, 0, tiled=True)]
    all_gather x1 -> x0, blocking collectives: 19.4 us -> none  [body(): row_portion = lax.all_gather(attention_output, 'batch', axis=0, tiled=True)]
    all_to_all x1 -> x4, starting transfers between devices: 12.2 us -> 28.5 us  [the longest x1 12 us: body(): in_q = lax.all_to_all(out_q, ('inst', 'batch'), 0, 0, tiled=True)]
    all_to_all x0 -> x1, blocking collectives: none -> 14.4 us  [body(): lax.all_to_all(part.reshape(lax.axis_size('tensor'), -1, part.shape[1]),...]
    gather x3 -> x2, local copies, waits for them, and re-layouts: 16.3 us -> 9.14 us  [the longest x1 4.95 us: body(): chosen = key_value_pages[jnp.where(mine, request_pages, 0)]]
    concatenate x1, other arithmetic: 6.02 us -> 0.01 us  [body(): stats = jnp.concatenate([far_top[:, None], far_total[:, None]], 1)]
  transfers between devices with their start and end apart: 2 -> 4, of which waited for: 2 -> 3; matrix products, arithmetic and copies ran while one was open for 1% -> 20% of each run, Pallas kernels for 0% -> 0%
where the time goes in v1:
time: 96.9 us; the launch traced here: 96.1 us
  starting transfers between devices  28.5 us (29%)
  waiting for transfers between devices  21.6 us (22%)
  blocking collectives  14.4 us (15%)
  matrix products  13.4 us (14%)
  local copies, waits for them, and re-layouts  11.6 us (12%)
  other arithmetic  6.37 us (7%)
    all_to_all x1, blocking collectives, body(): lax.all_to_all(part.reshape(lax.axis_size('tensor'), -1, part.shape[1]),...  14.4 us
    all_to_all x1, starting transfers between devices, body(): in_q = lax.all_to_all(out_q, ('inst', 'batch'), 0, 0, tiled=True)  12 us
    all_to_all x1, starting transfers between devices, body(): back_stats = lax.all_to_all(stats, ('inst', 'batch'), 0, 0, tiled=True)  9.22 us
    all_to_all x1, waiting for transfers between devices, body(): lax.all_to_all(copies, 'batch', 0, 0, tiled=True)  7.82 us
    all_to_all x1, waiting for transfers between devices, body(): lax.all_to_all(far_out.astype(jnp.bfloat16), ('inst', 'batch'), 0, 0, til...  7.3 us
    all_to_all x1, waiting for transfers between devices, body(): back_stats = lax.all_to_all(stats, ('inst', 'batch'), 0, 0, tiled=True)  6.47 us
    gather x1, local copies, waits for them, and re-layouts, body(): chosen = key_value_pages[jnp.where(mine, request_pages, 0)]  4.95 us
    gather x1, local copies, waits for them, and re-layouts, body(): sent = key_value_pages[jnp.maximum(transfer_pages[0], 0)]  4.2 us
  transfers between devices with their start and end apart: 4, of which 3 were waited for; matrix products, arithmetic and copies ran while one was open for 20% of the time, Pallas kernels for 0%

profile of v1, /device:TPU:1, one launch (start us, length us, event | category | flops | bytes accessed | tf_op | source)
XLA Modules:
  0.0 96.1 jit_solution(16298496349327485969)
XLA Ops:
  0.0 0.0 copy-start
  0.0 0.9 compare_reduce_fusion
  0.9 0.9 fusion.17
  1.9 0.6 copy.56
  2.5 12.0 %all-to-all-start = ((bf16[32,8,128]{2,1,0:T(8,128)(2,1)}), bf16[32,8,128]{2,1,0:T(8,128)(2,1)S(1)}, u32[]{:S(2)}, u32[]{:S(2)}) async-start(bf16[32,8,128]{2,1,0:T(8,128)(2,1)} %bitcast.17), calls=%async_computation | async-start | bytes 131072 | tf_op jit(solution)/shard_map/all_to_all | solution.py:35
  14.5 0.7 broadcast_compare_fusion
  15.2 0.7 compare_select_fusion
  15.9 0.7 maximum_bitcast_fusion
  16.6 0.1 copy.44
  16.7 0.1 reshape.93
  16.8 1.3 %slice_convert_fusion = (f32[8,128]{1,0:T(8,128)}, bf16[8,128,1]{1,0,2:T(8,128)(2,1)S(1)}) fusion(bf16[8,256]{1,0:T(8,128)(2,1)} %param.12), kind=kLoop, calls=%fused_computation.76 | loop fusion | flops 1024 | bytes 10240 | tf_op jit(solution)/shard_map/convert_element_type | solution.py:54
  18.1 4.2 %gather_fusion.1 = bf16[32,128,256]{2,1,0:T(8,128)(2,1)} fusion(bf16[64,128,256]{2,1,0:T(8,128)(2,1)} %param.13, s32[1024]{0:T(1024)S(1)} %pad_clamp_fusion), kind=kCustom, calls=%fused_computation.1 | custom fusion | bytes 4194432 | tf_op jit(solution)/shard_map/gather | solution.py:55
  22.2 0.0 copy-start.4
  22.3 0.0 copy-start.2
  22.3 4.9 %gather_fusion = bf16[64,128,256]{2,1,0:T(8,128)(2,1)} fusion(bf16[64,128,256]{2,1,0:T(8,128)(2,1)} %param.13, s32[1024]{0:T(1024)S(1)} %pad_clamp_fusion.1), kind=kCustom, calls=%fused_computation | custom fusion | bytes 8388864 | tf_op jit(solution)/shard_map/gather | solution.py:37
  27.2 0.0 copy-done.4
  27.2 0.1 fusion.51
  27.3 0.0 copy-done.2
  27.3 2.9 %fusion.72 = (f32[8,8]{1,0:T(8,128)}, f32[8,8,1024]{2,1,0:T(8,128)S(1)}) fusion(bf16[8,8,128]{2,0,1:T(8,128)(2,1)S(1)} %bitcast.49, bf16[8,1024,256]{2,1,0:T(8,128)(2,1)} %bitcast.42, pred[8,1024]{1,0:T(8,128)(4,1)S(1)} %fusion.51), kind=kOutput, calls=%fused_computation.89 | convolution fusion | flops 16973760 | bytes 2384128 | tf_op jit(solution)/shard_map/ngd,nsd->ngs/dot_general | solution.py:41
  30.2 0.1 fusion.58
  30.3 0.0 all-to-all-done
  30.3 1.9 %fusion.71 = (f32[32,8]{1,0:T(8,128)S(1)}, f32[32,8,128]{2,1,0:T(8,128)S(1)}) fusion(bf16[32,8,128]{2,1,0:T(8,128)(2,1)S(1)} %all-to-all-done, bf16[32,128,256]{2,1,0:T(8,128)(2,1)} %gather_fusion.1), kind=kOutput, calls=%fused_computation.88 | convolution fusion | flops 8453888 | bytes 1246208 | tf_op jit(solution)/shard_map/pgd,psd->pgs/dot_general | solution.py:56
  32.3 0.2 convert_reduce_fusion.2
  32.5 0.6 copy.46
  33.1 9.2 %all-to-all-start.1 = ((f32[32,2,8]{2,1,0:T(2,128)}), f32[32,2,8]{2,1,0:T(2,128)S(1)}, u32[]{:S(2)}, u32[]{:S(2)}) async-start(f32[32,2,8]{2,1,0:T(2,128)} %copy.46), calls=%async_computation.1 | async-start | bytes 65536 | tf_op jit(solution)/shard_map/all_to_all | solution.py:69
  42.4 2.3 %fusion.16 = bf16[32,8,128]{2,1,0:T(8,128)(2,1)} fusion(bf16[32,128,256]{2,1,0:T(8,128)(2,1)} %gather_fusion.1, f32[32,8]{1,0:T(8,128)S(1)} %convert_reduce_fusion.2, f32[32,8,128]{2,1,0:T(8,128)S(1)} %get-tuple-element.17, f32[32,8]{1,0:T(8,128)S(1)} %get-tuple-element.16), kind=kOutput, calls=%fused_computation.16 | convolution fusion | flops 8519680 | bytes 1247232 | tf_op jit(solution)/shard_map/pgs,psd->pgd/dot_general | solution.py:62
  44.7 0.0 copy-start.1
  44.7 6.5 %all-to-all-done.1 = f32[32,2,8]{2,1,0:T(2,128)S(1)} async-done(((f32[32,2,8]{2,1,0:T(2,128)}), f32[32,2,8]{2,1,0:T(2,128)S(1)}, u32[]{:S(2)}, u32[]{:S(2)}) %all-to-all-start.1) | async-done | bytes 2080 | tf_op jit(solution)/shard_map/all_to_all | solution.py:69
  51.1 3.9 %all-to-all-start.2 = ((bf16[32,8,128]{2,1,0:T(8,128)(2,1)}), bf16[32,8,128]{2,1,0:T(8,128)(2,1)S(1)}, u32[]{:S(2)}, u32[]{:S(2)}) async-start(bf16[32,8,128]{2,1,0:T(8,128)(2,1)} %fusion.16), calls=%async_computation.2 | async-start | bytes 131072 | tf_op jit(solution)/shard_map/all_to_all | solution.py:66
  55.0 0.1 copy.47
  55.1 0.1 copy.50
  55.2 0.1 select_reduce_fusion
  55.2 0.1 copy.48
  55.3 0.7 fusion.69
  56.0 0.1 copy.49
  56.1 0.2 fusion.49
  56.3 0.1 copy.53
  56.3 0.2 convert_reduce_fusion.1
  56.5 7.3 %all-to-all-done.2 = bf16[32,8,128]{2,1,0:T(8,128)(2,1)S(1)} async-done(((bf16[32,8,128]{2,1,0:T(8,128)(2,1)}), bf16[32,8,128]{2,1,0:T(8,128)(2,1)S(1)}, u32[]{:S(2)}, u32[]{:S(2)}) %all-to-all-start.2) | async-done | bytes 65568 | tf_op jit(solution)/shard_map/all_to_all | solution.py:66
  63.9 0.2 fusion.44
  64.1 2.0 %fusion.33 = bf16[1,8,8,128]{3,2,1,0:T(8,128)(2,1)S(1)} fusion(bf16[8,1024,256]{2,1,0:T(8,128)(2,1)} %bitcast.43, f32[8,128,8]{1,2,0:T(8,128)S(1)} %fusion.44, f32[8,8]{1,0:T(8,128)S(1)} %get-tuple-element.7, f32[8,128]{1,0:T(8,128)} %get-tuple-element.14, f32[8,8]{1,0:T(8,128)S(1)} %get-tuple-element.8, f32[8,8]{1,0:T(8,128)S(1)} %get-tuple-element.9, ...), kind=kOutput, calls=%fused_computation.24 | convolution fusion | flops 17022976 | bytes 2421760 | tf_op jit(solution)/shard_map/ngs,nsd->ngd/dot_general | solution.py:52
  66.2 0.7 broadcast_in_dim.113
  66.8 3.4 %all-to-all-start.3 = ((bf16[8,8,1024]{2,1,0:T(8,128)(2,1)}), bf16[8,8,1024]{2,1,0:T(8,128)(2,1)S(1)}, u32[]{:S(2)}, u32[]{:S(2)}) async-start(bf16[8,8,1024]{2,1,0:T(8,128)(2,1)} %broadcast_in_dim.113), calls=%async_computation.3 | async-start | bytes 262144 | tf_op jit(solution)/shard_map/all_to_all | solution.py:84
  70.2 7.8 %all-to-all-done.3 = bf16[8,8,1024]{2,1,0:T(8,128)(2,1)S(1)} async-done(((bf16[8,8,1024]{2,1,0:T(8,128)(2,1)}), bf16[8,8,1024]{2,1,0:T(8,128)(2,1)S(1)}, u32[]{:S(2)}, u32[]{:S(2)}) %all-to-all-start.3) | async-done | bytes 131104 | tf_op jit(solution)/shard_map/all_to_all | solution.py:84
  78.0 0.0 copy-done.1
  78.0 1.0 subtract_convert_fusion
  79.0 0.0 copy-start.3
  79.0 1.5 %fusion.38 = f32[128,1024]{1,0:T(8,128)S(1)} fusion(bf16[512,1024]{1,0:T(8,128)(2,1)} %param.21, bf16[64,512]{1,0:T(8,128)(2,1)S(1)} %get-tuple-element.5, bf16[64,512]{1,0:T(8,128)(2,1)S(1)} %get-tuple-element.6), kind=kOutput, calls=%fused_computation.30 | convolution fusion | flops 134479872 | bytes 1703936 | tf_op jit(solution)/shard_map/dot_general | solution.py:91
  80.5 0.0 copy-done
  80.6 0.5 fusion.15
  81.0 14.4 %all_to_all.25 = bf16[8,8,1024]{2,1,0:T(8,128)(2,1)S(1)} all-to-all(bf16[8,8,1024]{2,1,0:T(8,128)(2,1)S(1)} %fusion.15), channel_id=1, replica_groups=mesh['inst'=4,'batch'=8,'tensor'=8] {'tensor'}, dimensions={0} | all-to-all | bytes 262144 | tf_op jit(solution)/shard_map/all_to_all | solution.py:96
  95.5 0.0 copy-done.3
  95.5 0.6 add_convert_fusion
  (9 shorter events, 0.1 us)
Async XLA Ops:
  0.0 80.5 %copy-start = (bf16[1024,1024]{1,0:T(8,128)(2,1)S(1)}, bf16[1024,1024]{1,0:T(8,128)(2,1)}, u32[]{:S(2)}) copy-start(bf16[1024,1024]{1,0:T(8,128)(2,1)} %param.19) | copy-start | bytes 6291460
  2.5 27.8 %all-to-all-start = ((bf16[32,8,128]{2,1,0:T(8,128)(2,1)}), bf16[32,8,128]{2,1,0:T(8,128)(2,1)S(1)}, u32[]{:S(2)}, u32[]{:S(2)}) async-start(bf16[32,8,128]{2,1,0:T(8,128)(2,1)} %bitcast.17), calls=%async_computation | async-start | bytes 131072 | tf_op jit(solution)/shard_map/all_to_all | solution.py:35
  22.2 5.0 %copy-start.4 = (s32[8]{0:T(128)S(1)}, s32[8]{0:T(128)}, u32[]{:S(2)}) copy-start(s32[8]{0:T(128)} %param.16) | copy-start | bytes 100
  22.3 5.0 %copy-start.2 = (bf16[8,1024]{1,0:T(8,128)(2,1)S(1)}, bf16[8,1024]{1,0:T(8,128)(2,1)}, u32[]{:S(2)}) copy-start(bf16[8,1024]{1,0:T(8,128)(2,1)} %param.11) | copy-start | bytes 49156
  33.1 18.0 %all-to-all-start.1 = ((f32[32,2,8]{2,1,0:T(2,128)}), f32[32,2,8]{2,1,0:T(2,128)S(1)}, u32[]{:S(2)}, u32[]{:S(2)}) async-start(f32[32,2,8]{2,1,0:T(2,128)} %copy.46), calls=%async_computation.1 | async-start | bytes 65536 | tf_op jit(solution)/shard_map/all_to_all | solution.py:69
  44.7 33.4 %copy-start.1 = (bf16[1024,512]{1,0:T(8,128)(2,1)S(1)}, bf16[1024,512]{1,0:T(8,128)(2,1)}, u32[]{:S(2)}) copy-start(bf16[1024,512]{1,0:T(8,128)(2,1)} %param.20) | copy-start | bytes 3145732
  51.1 12.7 %all-to-all-start.2 = ((bf16[32,8,128]{2,1,0:T(8,128)(2,1)}), bf16[32,8,128]{2,1,0:T(8,128)(2,1)S(1)}, u32[]{:S(2)}, u32[]{:S(2)}) async-start(bf16[32,8,128]{2,1,0:T(8,128)(2,1)} %fusion.16), calls=%async_computation.2 | async-start | bytes 131072 | tf_op jit(solution)/shard_map/all_to_all | solution.py:66
  66.8 11.2 %all-to-all-start.3 = ((bf16[8,8,1024]{2,1,0:T(8,128)(2,1)}), bf16[8,8,1024]{2,1,0:T(8,128)(2,1)S(1)}, u32[]{:S(2)}, u32[]{:S(2)}) async-start(bf16[8,8,1024]{2,1,0:T(8,128)(2,1)} %broadcast_in_dim.113), calls=%async_computation.3 | async-start | bytes 262144 | tf_op jit(solution)/shard_map/all_to_all | solution.py:84
  79.0 16.5 %copy-start.3 = (bf16[8,1024]{1,0:T(8,128)(2,1)S(1)}, bf16[8,1024]{1,0:T(8,128)(2,1)}, u32[]{:S(2)}) copy-start(bf16[8,1024]{1,0:T(8,128)(2,1)} %param.18) | copy-start | bytes 49156

commit v2 on v1

v2 whole, which is shorter than its diff:
```python
import math

import jax
import jax.numpy as jnp
from jax import lax
from jax.experimental import pallas as pl
from jax.experimental.pallas import tpu as pltpu
from jax.sharding import PartitionSpec as P

HEAD_DIM = 128
GROUP = 8
ADAPTER_RANK = 64
FAR_POSITIONS = 4
SCALE = 1.0 / math.sqrt(HEAD_DIM)
NEVER = -1e30
VMEM = pl.BlockSpec(memory_space=pltpu.VMEM)
SMEM = pl.BlockSpec(memory_space=pltpu.SMEM)
NT = (((1,), (1,)), ((), ()))


def heads_of(q_ref, q_heads):
    q = q_ref[...].astype(jnp.float32)
    for head in range(GROUP):
        q_heads[:, head, :] = q[:, head * HEAD_DIM:(head + 1) * HEAD_DIM]


def outgoing_kernel(pages_ref, q_ref, out_ref, q_heads, rows):
    slots, pool, peers = q_ref.shape[0], 64, out_ref.shape[0]
    heads_of(q_ref, q_heads)
    rows[...] = jnp.zeros_like(rows)
    for slot in range(slots):
        for place in range(FAR_POSITIONS):
            entry = pages_ref[slot, place]
            rows[jnp.where(entry >= pool, entry - pool, peers)] = q_heads[slot]
    out_ref[...] = rows[:peers].astype(jnp.bfloat16)


def near_kernel(
    pages_ref, lengths_ref, q_ref, fresh_ref, pool_ref, out_ref, top_ref, total_ref, q_heads
):
    slots, places = pages_ref.shape
    pool, page_len, _ = pool_ref.shape
    heads_of(q_ref, q_heads)
    fresh = fresh_ref[...].astype(jnp.float32)
    lane = lax.broadcasted_iota(jnp.int32, (GROUP, page_len), 1)
    for slot in range(slots):
        q = q_heads[slot]
        q_half = q.astype(jnp.bfloat16)
        index, scores = [], []
        for place in range(places):
            entry = pages_ref[slot, place]
            limit = lengths_ref[slot] - place * page_len
            if place < FAR_POSITIONS:
                limit = jnp.where(entry < pool, limit, 0)
                entry = jnp.where(entry < pool, entry, 0)
            index.append(entry)
            score = lax.dot_general(
                q_half, pool_ref[entry, :, :HEAD_DIM], NT, preferred_element_type=jnp.float32
            )
            scores.append(jnp.where(lane < limit, score * SCALE, NEVER))
        own = jnp.sum(q * fresh[slot:slot + 1, :HEAD_DIM], axis=1, keepdims=True) * SCALE
        top = scores[0]
        for score in scores[1:]:
            top = jnp.maximum(top, score)
        top = jnp.maximum(jnp.max(top, axis=1, keepdims=True), own)
        own_weight = jnp.exp(own - top)
        summed = jnp.zeros((GROUP, page_len), jnp.float32)
        out = own_weight * fresh[slot:slot + 1, HEAD_DIM:]
        for place in range(places):
            probs = jnp.exp(scores[place] - top).astype(jnp.bfloat16)
            summed = summed + probs.astype(jnp.float32)
            out = out + jnp.dot(
                probs, pool_ref[index[place], :, HEAD_DIM:], preferred_element_type=jnp.float32
            )
        total = jnp.sum(summed, axis=1, keepdims=True) + own_weight
        out_ref[slot] = out
        top_ref[slot] = jnp.broadcast_to(top, (GROUP, HEAD_DIM))
        total_ref[slot] = jnp.broadcast_to(total, (GROUP, HEAD_DIM))


def far_kernel(listed_ref, q_ref, pool_ref, out_ref):
    peers = q_ref.shape[0]
    lane = lax.broadcasted_iota(jnp.int32, (GROUP, HEAD_DIM), 1)
    for peer in range(peers):
        page = jnp.maximum(listed_ref[0, peer], 0)
        score = SCALE * lax.dot_general(
            q_ref[peer], pool_ref[page, :, :HEAD_DIM], NT, preferred_element_type=jnp.float32
        )
        top = jnp.max(score, axis=1, keepdims=True).astype(jnp.bfloat16).astype(jnp.float32)
        probs = jnp.exp(score - top).astype(jnp.bfloat16)
        total = jnp.sum(probs.astype(jnp.float32), axis=1, keepdims=True)
        out = jnp.dot(probs, pool_ref[page, :, HEAD_DIM:], preferred_element_type=jnp.float32)
        high = total.astype(jnp.bfloat16).astype(jnp.float32)
        stats = jnp.where(lane == 0, top, jnp.where(lane == 1, high, total - high))
        out_ref[peer] = jnp.concatenate([out / total, stats], 0).astype(jnp.bfloat16)


def join_kernel(pages_ref, out_ref, top_ref, total_ref, back_ref, rows_ref, heads):
    slots, pool = pages_ref.shape[0], 64
    for slot in range(slots):
        tops, totals, outs = [top_ref[slot]], [total_ref[slot]], [out_ref[slot]]
        for place in range(FAR_POSITIONS):
            entry = pages_ref[slot, place]
            part = back_ref[jnp.maximum(entry - pool, 0)].astype(jnp.float32)
            stats = part[GROUP:]
            tops.append(jnp.where(entry >= pool, stats[:, 0:1], NEVER))
            totals.append(stats[:, 1:2] + stats[:, 2:3])
            outs.append(part[:GROUP])
        peak = tops[0]
        for top in tops[1:]:
            peak = jnp.maximum(peak, top)
        keep = jnp.exp(tops[0] - peak)
        denom = keep * totals[0]
        numer = keep * outs[0]
        for top, total, out in zip(tops[1:], totals[1:], outs[1:]):
            weight = jnp.exp(top - peak) * total
            denom = denom + weight
            numer = numer + weight * out
        heads[slot] = numer / denom
    for head in range(GROUP):
        block = heads[:, head, :].astype(jnp.bfloat16)
        for copy in range(rows_ref.shape[0]):
            rows_ref[copy, :, head * HEAD_DIM:(head + 1) * HEAD_DIM] = block


def body(
    queries,
    current_key_value,
    key_value_pages,
    transfer_pages,
    request_pages,
    lengths,
    request_adapter,
    residual_input,
    wo,
    down_weight,
    up_weight,
):
    slots, _ = request_pages.shape
    peers = transfer_pages.shape[1]
    heads = (slots, GROUP, HEAD_DIM)
    around = ("inst", "batch")
    params = pltpu.CompilerParams(vmem_limit_bytes=16 * 1024 * 1024)
    out_q = pl.pallas_call(
        outgoing_kernel,
        out_shape=jax.ShapeDtypeStruct((peers, GROUP, HEAD_DIM), jnp.bfloat16),
        in_specs=[SMEM, VMEM],
        out_specs=VMEM,
        scratch_shapes=[
            pltpu.VMEM(heads, jnp.float32),
            pltpu.VMEM((peers + 1, GROUP, HEAD_DIM), jnp.float32),
        ],
        compiler_params=params,
        name="outgoing",
    )(request_pages, queries)
    in_q = lax.all_to_all(out_q, around, 0, 0, tiled=True)
    near_out, near_top, near_total = pl.pallas_call(
        near_kernel,
        out_shape=[jax.ShapeDtypeStruct(heads, jnp.float32)] * 3,
        in_specs=[SMEM, SMEM, VMEM, VMEM, VMEM],
        out_specs=[VMEM] * 3,
        scratch_shapes=[pltpu.VMEM(heads, jnp.float32)],
        compiler_params=params,
        cost_estimate=pl.CostEstimate(flops=34_000_000, bytes_accessed=4_300_000, transcendentals=70_000),
        name="near",
    )(request_pages, lengths, queries, current_key_value, key_value_pages)
    far = pl.pallas_call(
        far_kernel,
        out_shape=jax.ShapeDtypeStruct((peers, 2 * GROUP, HEAD_DIM), jnp.bfloat16),
        in_specs=[SMEM, VMEM, VMEM],
        out_specs=VMEM,
        compiler_params=params,
        cost_estimate=pl.CostEstimate(flops=17_000_000, bytes_accessed=2_200_000, transcendentals=35_000),
        name="far",
    )(transfer_pages, in_q, key_value_pages)
    back = lax.all_to_all(far, around, 0, 0, tiled=True)
    group = lax.axis_size("batch")
    copies = pl.pallas_call(
        join_kernel,
        out_shape=jax.ShapeDtypeStruct((group, slots, GROUP * HEAD_DIM), jnp.bfloat16),
        in_specs=[SMEM, VMEM, VMEM, VMEM, VMEM],
        out_specs=VMEM,
        scratch_shapes=[pltpu.VMEM(heads, jnp.float32)],
        compiler_params=params,
        name="join",
    )(request_pages, near_out, near_top, near_total, back)
    rows = lax.all_to_all(copies, "batch", 0, 0, tiled=True).reshape(-1, GROUP * HEAD_DIM)
    base = jnp.dot(rows, wo, preferred_element_type=jnp.float32)
    shrink = jnp.dot(rows, down_weight, preferred_element_type=jnp.float32)
    adapter_of = jnp.arange(down_weight.shape[1], dtype=jnp.int32) // ADAPTER_RANK
    shrink = jnp.where(request_adapter[:, None] == adapter_of[None], shrink, 0.0)
    high = shrink.astype(jnp.bfloat16)
    low = (shrink - high.astype(jnp.float32)).astype(jnp.bfloat16)
    both = jnp.dot(
        jnp.concatenate([high, low], 0), up_weight, preferred_element_type=jnp.float32
    )
    count = rows.shape[0]
    part = (base + both[:count] + both[count:]).astype(jnp.bfloat16)
    parts = lax.all_to_all(
        part.reshape(lax.axis_size("tensor"), -1, part.shape[1]), "tensor", 0, 0, tiled=True
    )
    summed = jnp.sum(parts.astype(jnp.float32), axis=0)
    return (residual_input.astype(jnp.float32) + summed).astype(jnp.bfloat16)


def solution(mesh):
    return jax.shard_map(
        body,
        mesh=mesh,
        in_specs=(
            P(("inst", "batch"), "tensor"),
            P(("inst", "batch"), "tensor"),
            P(("inst", "batch"), None, "tensor"),
            P(("inst", "batch"), None),
            P(("inst", "batch"), None),
            P(("inst", "batch")),
            P("inst"),
            P(("inst", "tensor"), "batch"),
            P("tensor", "batch"),
            P("tensor", None),
            P(None, "batch"),
        ),
        out_specs=P(("inst", "tensor"), "batch"),
        check_vma=False,
    )
```

time: 96.9 us -> 77.7 us (0.80)
  starting transfers between devices: 28.5 us -> 7.26 us
  blocking collectives: 14.4 us -> 34.3 us
  Pallas kernels: 0 us -> 15 us
  matrix products: 13.4 us -> 2.32 us
  waiting for transfers between devices: 21.6 us -> 11 us
  other arithmetic: 6.37 us -> 0.64 us
  local copies, waits for them, and re-layouts: 11.6 us -> 6.61 us
    all_to_all x3 -> x1, starting transfers between devices: 25.1 us -> 3.86 us  [body(): back = lax.all_to_all(far, around, 0, 0, tiled=True)]
    all_to_all x0 -> x1, blocking collectives: none -> 20.7 us  [body(): in_q = lax.all_to_all(out_q, around, 0, 0, tiled=True)]
    pallas_call x0 -> x4, Pallas kernels: none -> 15 us  [the longest x1 8.8 us: body(): pl.pallas_call(far_kernel, out_shape=jax.ShapeDtypeStruct((peers, 2 * GRO...]
    all_to_all x3 -> x1, waiting for transfers between devices: 13.8 us -> 2.93 us  [body(): back = lax.all_to_all(far, around, 0, 0, tiled=True)]
    dot_general x7 -> x0, matrix products: 10.5 us -> none  [the longest x1 2.92 us: body(): jnp.einsum('ngd,nsd->ngs', q, chosen[..., :HEAD_DIM], preferred_element_t...]
    gather x2 -> x0, local copies, waits for them, and re-layouts: 9.14 us -> none  [the longest x1 4.95 us: body(): chosen = key_value_pages[jnp.where(mine, request_pages, 0)]]
    unnamed x12 -> x26, local copies, waits for them, and re-layouts: 0.67 us -> 6.61 us
    max x2 -> x0, other arithmetic: 1.36 us -> none  [the longest x1 0.7 us: body(): peak = jnp.maximum(jnp.max(reach, axis=1), top)]
  transfers between devices with their start and end apart: 4 -> 2, of which waited for: 3 -> 2; matrix products, arithmetic and copies ran while one was open for 20% -> 0% of each run, Pallas kernels for 0% -> 5%
where the time goes in v2:
time: 77.7 us; the launch traced here: 77.2 us
  blocking collectives  34.3 us (44%)
  Pallas kernels  15 us (19%)
  waiting for transfers between devices  11 us (14%)
  starting transfers between devices  7.26 us (9%)
  local copies, waits for them, and re-layouts  6.61 us (9%)
  matrix products  2.32 us (3%)
    all_to_all x1, blocking collectives, body(): in_q = lax.all_to_all(out_q, around, 0, 0, tiled=True)  20.7 us
    all_to_all x1, blocking collectives, body(): lax.all_to_all(part.reshape(lax.axis_size('tensor'), -1, part.shape[1]),...  13.6 us
    pallas_call x1, Pallas kernels, body(): pl.pallas_call(far_kernel, out_shape=jax.ShapeDtypeStruct((peers, 2 * GRO...  8.8 us
    all_to_all x1, waiting for transfers between devices, body(): lax.all_to_all(copies, 'batch', 0, 0, tiled=True)  8.03 us
    unnamed x26, local copies, waits for them, and re-layouts  6.61 us
    pallas_call x1, Pallas kernels, body(): pl.pallas_call(near_kernel, out_shape=[jax.ShapeDtypeStruct(heads, jnp.fl...  3.97 us
    all_to_all x1, starting transfers between devices, body(): back = lax.all_to_all(far, around, 0, 0, tiled=True)  3.86 us
    all_to_all x1, starting transfers between devices, body(): lax.all_to_all(copies, 'batch', 0, 0, tiled=True)  3.41 us
  transfers between devices with their start and end apart: 2, of which 2 were waited for; matrix products, arithmetic and copies ran while one was open for 0% of the time, Pallas kernels for 5%

profile of v2, /device:TPU:1, one launch (start us, length us, event | category | flops | bytes accessed | tf_op | source)
XLA Modules:
  0.0 77.2 jit_solution(17761376864566852878)
XLA Ops:
  0.0 0.0 copy-start
  0.0 0.0 copy-start.3
  0.0 0.9 %copy-done.3 = bf16[8,1024]{1,0:T(8,128)(2,1)S(1)} copy-done((bf16[8,1024]{1,0:T(8,128)(2,1)S(1)}, bf16[8,1024]{1,0:T(8,128)(2,1)}, u32[]{:S(2)}) %copy-start.3) | copy-done | bytes 16408
  0.9 0.0 copy-start.5
  0.9 0.7 copy-done.5
  1.6 0.7 outgoing.1
  2.2 20.7 %all_to_all.20.q_ref = bf16[32,8,128]{2,1,0:T(8,128)(2,1)S(1)} all-to-all(bf16[32,8,128]{2,1,0:T(8,128)(2,1)S(1)} %outgoing.1), channel_id=1, replica_groups=mesh['inst'=4,'batch'=8,'tensor'=8] {'inst','batch'}, dimensions={0} | all-to-all | bytes 131072 | tf_op jit(solution)/shard_map/all_to_all | solution.py:156
  22.9 0.0 copy-start.1
  22.9 2.2 %copy-done.1 = bf16[64,128,256]{2,1,0:T(8,128)(2,1)S(1)} copy-done((bf16[64,128,256]{2,1,0:T(8,128)(2,1)S(1)}, bf16[64,128,256]{2,1,0:T(8,128)(2,1)}, u32[]{:S(2)}) %copy-start.1) | copy-done | bytes 4194328
  25.1 0.0 copy-start.8
  25.1 0.7 copy-done.8
  25.8 0.0 copy-start.4
  25.8 0.0 copy-start.6
  25.8 0.0 copy-start.7
  25.8 0.0 copy-start.9
  25.8 8.8 %far.1 = bf16[32,16,128]{2,1,0:T(8,128)(2,1)} custom-call(s32[1,32]{1,0:T(1,128)S(1)} %copy-done.8, bf16[32,8,128]{2,1,0:T(8,128)(2,1)S(1)} %all_to_all.20.q_ref, bf16[64,128,256]{2,1,0:T(8,128)(2,1)S(1)} %copy-done.1), custom_call_target="tpu_custom_call" | custom-call | flops 17000000 | bytes 2200000 | tf_op jit(solution)/shard_map/far/pallas_call | solution.py:167
  34.6 3.9 %all-to-all-start.1 = ((bf16[32,16,128]{2,1,0:T(8,128)(2,1)}), bf16[32,16,128]{2,1,0:T(8,128)(2,1)S(1)}, u32[]{:S(2)}, u32[]{:S(2)}) async-start(bf16[32,16,128]{2,1,0:T(8,128)(2,1)} %far.1), calls=%async_computation.1 | async-start | bytes 262144 | tf_op jit(solution)/shard_map/all_to_all | solution.py:176
  38.4 0.0 copy-done.4
  38.5 0.0 copy-done.6
  38.5 0.0 copy-done.7
  38.5 0.0 copy-done.9
  38.5 0.0 copy-start.2
  38.5 2.2 %copy-done.2 = bf16[64,128,256]{2,1,0:T(8,128)(2,1)S(1)} copy-done((bf16[64,128,256]{2,1,0:T(8,128)(2,1)S(1)}, bf16[64,128,256]{2,1,0:T(8,128)(2,1)}, u32[]{:S(2)}) %copy-start.2) | copy-done | bytes 4194328
  40.7 0.0 copy-start.10
  40.7 0.0 copy-start.12
  40.7 4.0 %near.1 = (f32[8,8,128]{2,1,0:T(8,128)S(1)}, f32[8,8,128]{2,1,0:T(8,128)S(1)}, f32[8,8,128]{2,1,0:T(8,128)S(1)}) custom-call(s32[8,8]{1,0:T(8,128)S(1)} %copy-done.6, s32[8]{0:T(128)S(1)} %copy-done.9, bf16[8,1024]{1,0:T(8,128)(2,1)S(1)} %copy-done.4, bf16[8,256]{1,0:T(8,128)(2,1)S(1)} %copy-done.7, bf16[64,128,256]{2,1,0:T(8,128)(2,1)S(1)} %copy-done.2), custom_call_target="tpu_custom_call" | custom-call | flops 34000000 | bytes 4300000 | tf_op jit(solution)/shard_map/near/pallas_call | solution.py:157
  44.7 2.9 %all-to-all-done.1.back_ref = bf16[32,16,128]{2,1,0:T(8,128)(2,1)S(1)} async-done(((bf16[32,16,128]{2,1,0:T(8,128)(2,1)}), bf16[32,16,128]{2,1,0:T(8,128)(2,1)S(1)}, u32[]{:S(2)}, u32[]{:S(2)}) %all-to-all-start.1) | async-done | bytes 131104 | tf_op jit(solution)/shard_map/all_to_all | solution.py:176
  47.6 1.5 %join.1 = bf16[8,8,1024]{2,1,0:T(8,128)(2,1)} custom-call(s32[8,8]{1,0:T(8,128)S(1)} %copy-done.6, f32[8,8,128]{2,1,0:T(8,128)S(1)} %get-tuple-element.8.out_ref, f32[8,8,128]{2,1,0:T(8,128)S(1)} %get-tuple-element.9.top_ref, f32[8,8,128]{2,1,0:T(8,128)S(1)} %get-tuple-element.10.total_ref, bf16[32,16,128]{2,1,0:T(8,128)(2,1)S(1)} %all-to-all-done.1.back_ref), custom_call_target="tpu_custom_call" | custom-call | tf_op jit(solution)/shard_map/join/pallas_call | solution.py:178
  49.1 3.4 %all-to-all-start.2 = ((bf16[8,8,1024]{2,1,0:T(8,128)(2,1)}), bf16[8,8,1024]{2,1,0:T(8,128)(2,1)S(1)}, u32[]{:S(2)}, u32[]{:S(2)}) async-start(bf16[8,8,1024]{2,1,0:T(8,128)(2,1)} %join.1), calls=%async_computation.2 | async-start | bytes 262144 | tf_op jit(solution)/shard_map/all_to_all | solution.py:187
  52.5 8.0 %all-to-all-done.2 = bf16[8,8,1024]{2,1,0:T(8,128)(2,1)S(1)} async-done(((bf16[8,8,1024]{2,1,0:T(8,128)(2,1)}), bf16[8,8,1024]{2,1,0:T(8,128)(2,1)S(1)}, u32[]{:S(2)}, u32[]{:S(2)}) %all-to-all-start.2) | async-done | bytes 131104 | tf_op jit(solution)/shard_map/all_to_all | solution.py:187
  60.6 0.0 copy-done.10
  60.6 0.0 copy-done.12
  60.6 0.3 subtract_convert_fusion
  60.9 0.0 copy-start.11
  60.9 1.5 %fusion.3 = f32[128,1024]{1,0:T(8,128)S(1)} fusion(bf16[512,1024]{1,0:T(8,128)(2,1)} %param.21, bf16[64,512]{1,0:T(8,128)(2,1)S(1)} %get-tuple-element.11, bf16[64,512]{1,0:T(8,128)(2,1)S(1)} %get-tuple-element.12), kind=kOutput, calls=%fused_computation.6 | convolution fusion | flops 134479872 | bytes 1703936 | tf_op jit(solution)/shard_map/dot_general | solution.py:194
  62.4 0.0 copy-done
  62.4 0.5 fusion.2
  62.9 13.6 %all_to_all.21 = bf16[8,8,1024]{2,1,0:T(8,128)(2,1)S(1)} all-to-all(bf16[8,8,1024]{2,1,0:T(8,128)(2,1)S(1)} %fusion.2), channel_id=1, replica_groups=mesh['inst'=4,'batch'=8,'tensor'=8] {'tensor'}, dimensions={0} | all-to-all | bytes 262144 | tf_op jit(solution)/shard_map/all_to_all | solution.py:199
  76.6 0.0 copy-done.11
  76.6 0.6 add_convert_fusion
  (2 shorter events, 0.0 us)
Async XLA Ops:
  0.0 62.4 %copy-start = (bf16[1024,1024]{1,0:T(8,128)(2,1)S(1)}, bf16[1024,1024]{1,0:T(8,128)(2,1)}, u32[]{:S(2)}) copy-start(bf16[1024,1024]{1,0:T(8,128)(2,1)} %param.19) | copy-start | bytes 6291460
  0.0 0.9 %copy-start.3 = (bf16[8,1024]{1,0:T(8,128)(2,1)S(1)}, bf16[8,1024]{1,0:T(8,128)(2,1)}, u32[]{:S(2)}) copy-start(bf16[8,1024]{1,0:T(8,128)(2,1)} %q_ref.3) | copy-start | bytes 49156
  0.9 0.7 copy-start.5
  22.9 2.2 %copy-start.1 = (bf16[64,128,256]{2,1,0:T(8,128)(2,1)S(1)}, bf16[64,128,256]{2,1,0:T(8,128)(2,1)}, u32[]{:S(2)}) copy-start(bf16[64,128,256]{2,1,0:T(8,128)(2,1)} %pool_ref.3) | copy-start | bytes 12582916
  25.1 0.7 copy-start.8
  25.8 12.7 %copy-start.4 = (bf16[8,1024]{1,0:T(8,128)(2,1)S(1)}, bf16[8,1024]{1,0:T(8,128)(2,1)}, u32[]{:S(2)}) copy-start(bf16[8,1024]{1,0:T(8,128)(2,1)} %q_ref.3) | copy-start | bytes 49156
  25.8 12.7 %copy-start.6 = (s32[8,8]{1,0:T(8,128)S(1)}, s32[8,8]{1,0:T(8,128)}, u32[]{:S(2)}) copy-start(s32[8,8]{1,0:T(8,128)} %pages_ref.5) | copy-start | bytes 772
  25.8 12.7 %copy-start.7 = (bf16[8,256]{1,0:T(8,128)(2,1)S(1)}, bf16[8,256]{1,0:T(8,128)(2,1)}, u32[]{:S(2)}) copy-start(bf16[8,256]{1,0:T(8,128)(2,1)} %fresh_ref.1) | copy-start | bytes 12292
  25.8 12.7 %copy-start.9 = (s32[8]{0:T(128)S(1)}, s32[8]{0:T(128)}, u32[]{:S(2)}) copy-start(s32[8]{0:T(128)} %lengths_ref.1) | copy-start | bytes 100
  34.6 13.0 %all-to-all-start.1 = ((bf16[32,16,128]{2,1,0:T(8,128)(2,1)}), bf16[32,16,128]{2,1,0:T(8,128)(2,1)S(1)}, u32[]{:S(2)}, u32[]{:S(2)}) async-start(bf16[32,16,128]{2,1,0:T(8,128)(2,1)} %far.1), calls=%async_computation.1 | async-start | bytes 262144 | tf_op jit(solution)/shard_map/all_to_all | solution.py:176
  38.5 2.2 %copy-start.2 = (bf16[64,128,256]{2,1,0:T(8,128)(2,1)S(1)}, bf16[64,128,256]{2,1,0:T(8,128)(2,1)}, u32[]{:S(2)}) copy-start(bf16[64,128,256]{2,1,0:T(8,128)(2,1)} %pool_ref.3) | copy-start | bytes 12582916
  40.7 19.9 %copy-start.10 = (bf16[1024,512]{1,0:T(8,128)(2,1)S(1)}, bf16[1024,512]{1,0:T(8,128)(2,1)}, u32[]{:S(2)}) copy-start(bf16[1024,512]{1,0:T(8,128)(2,1)} %param.20) | copy-start | bytes 3145732
  40.7 19.9 %copy-start.12 = (s32[64]{0:T(128)S(1)}, s32[64]{0:T(128)}, u32[]{:S(2)}) copy-start(s32[64]{0:T(128)} %param.17) | copy-start | bytes 772
  49.1 11.4 %all-to-all-start.2 = ((bf16[8,8,1024]{2,1,0:T(8,128)(2,1)}), bf16[8,8,1024]{2,1,0:T(8,128)(2,1)S(1)}, u32[]{:S(2)}, u32[]{:S(2)}) async-start(bf16[8,8,1024]{2,1,0:T(8,128)(2,1)} %join.1), calls=%async_computation.2 | async-start | bytes 262144 | tf_op jit(solution)/shard_map/all_to_all | solution.py:187
  60.9 15.7 %copy-start.11 = (bf16[8,1024]{1,0:T(8,128)(2,1)S(1)}, bf16[8,1024]{1,0:T(8,128)(2,1)}, u32[]{:S(2)}) copy-start(bf16[8,1024]{1,0:T(8,128)(2,1)} %param.18) | copy-start | bytes 49156

commit v3 on v2

v3 whole, which is shorter than its diff:
```python
import math

import jax
import jax.numpy as jnp
from jax import lax
from jax.experimental import pallas as pl
from jax.experimental.pallas import tpu as pltpu
from jax.sharding import PartitionSpec as P

HEAD_DIM = 128
GROUP = 8
ADAPTER_RANK = 64
FAR_POSITIONS = 4
FAR_BLOCK = 32
NEAR_BLOCK = 4
POOL = 64
SCALE = 1.0 / math.sqrt(HEAD_DIM)
NEVER = -1e30
VMEM = pl.BlockSpec(memory_space=pltpu.VMEM)
SMEM = pl.BlockSpec(memory_space=pltpu.SMEM)
HBM = pl.BlockSpec(memory_space=pltpu.HBM)
NT = (((1,), (1,)), ((), ()))


def in_hbm(array):
    return pltpu.with_memory_space_constraint(array, pltpu.HBM)


def heads_of(q_ref, q_heads):
    q = q_ref[...].astype(jnp.float32)
    for head in range(GROUP):
        q_heads[:, head, :] = q[:, head * HEAD_DIM:(head + 1) * HEAD_DIM]


def outgoing_kernel(
    pages_hbm, q_hbm, listed_hbm, out_ref, listed_ref, pages_ref, q_ref, q_heads, rows, sems
):
    first = pltpu.make_async_copy(q_hbm, q_ref, sems.at[0])
    second = pltpu.make_async_copy(pages_hbm, pages_ref, sems.at[1])
    third = pltpu.make_async_copy(listed_hbm, listed_ref, sems.at[2])
    first.start()
    second.start()
    third.start()
    rows[...] = jnp.zeros_like(rows)
    first.wait()
    heads_of(q_ref, q_heads)
    second.wait()
    slots, peers = q_ref.shape[0], out_ref.shape[0]
    for slot in range(slots):
        for place in range(FAR_POSITIONS):
            entry = pages_ref[slot, place]
            rows[jnp.where(entry >= POOL, entry - POOL, peers)] = q_heads[slot]
    out_ref[...] = rows[:peers].astype(jnp.bfloat16)
    third.wait()


def near_kernel(
    pages_ref, lengths_ref, adapter_ref, q_ref, fresh_ref, pool_ref,
    out_ref, top_ref, total_ref, which_ref, q_heads,
):
    slots, places = pages_ref.shape
    page_len = pool_ref.shape[1]
    heads_of(q_ref, q_heads)
    fresh = fresh_ref[...].astype(jnp.float32)
    lane = lax.broadcasted_iota(jnp.int32, (GROUP, page_len), 1)
    for first in range(0, slots, NEAR_BLOCK):
        block = range(first, first + NEAR_BLOCK)
        index = {}
        scores = {}
        for slot in block:
            limits = []
            for place in range(places):
                entry = pages_ref[slot, place]
                limit = lengths_ref[slot] - place * page_len
                if place < FAR_POSITIONS:
                    limit = jnp.where(entry < POOL, limit, 0)
                    entry = jnp.where(entry < POOL, entry, 0)
                index[slot, place] = entry
                limits.append(limit)
            keys = [pool_ref[index[slot, place], :, :HEAD_DIM] for place in range(places)]
            score = SCALE * lax.dot_general(
                q_heads[slot].astype(jnp.bfloat16),
                jnp.concatenate(keys, 0),
                NT,
                preferred_element_type=jnp.float32,
            )
            scores[slot] = [
                jnp.where(lane < limit, score[:, at * page_len:(at + 1) * page_len], NEVER)
                for at, limit in enumerate(limits)
            ]
        owns = [
            SCALE
            * jnp.sum(q_heads[slot] * fresh[slot:slot + 1, :HEAD_DIM], axis=1, keepdims=True)
            for slot in block
        ]
        tops = []
        for slot, own in zip(block, owns):
            top = scores[slot][0]
            for score in scores[slot][1:]:
                top = jnp.maximum(top, score)
            tops.append(jnp.maximum(jnp.max(top, axis=1, keepdims=True), own))
        weights = [jnp.exp(own - top) for own, top in zip(owns, tops)]
        for slot, top, weight in zip(block, tops, weights):
            probs = [jnp.exp(score - top).astype(jnp.bfloat16) for score in scores[slot]]
            summed = probs[0].astype(jnp.float32)
            for prob in probs[1:]:
                summed = summed + prob.astype(jnp.float32)
            values = [pool_ref[index[slot, place], :, HEAD_DIM:] for place in range(places)]
            out = jnp.dot(
                jnp.concatenate(probs, 1),
                jnp.concatenate(values, 0),
                preferred_element_type=jnp.float32,
            )
            total = jnp.sum(summed, axis=1, keepdims=True) + weight
            out_ref[slot] = out + weight * fresh[slot:slot + 1, HEAD_DIM:]
            top_ref[slot] = jnp.broadcast_to(top, (GROUP, HEAD_DIM))
            total_ref[slot] = jnp.broadcast_to(total, (GROUP, HEAD_DIM))
    for row in range(which_ref.shape[0]):
        which_ref[row:row + 1, :] = jnp.full((1, HEAD_DIM), adapter_ref[row], jnp.int32)


def far_kernel(listed_ref, q_ref, pool_ref, out_ref):
    peers = q_ref.shape[0]
    page_len = pool_ref.shape[1]
    lane = lax.broadcasted_iota(jnp.int32, (GROUP, HEAD_DIM), 1)
    none = jnp.zeros((GROUP, page_len), jnp.bfloat16)
    for first in range(0, peers, FAR_BLOCK):
        block = range(first, first + FAR_BLOCK)
        pages = [jnp.maximum(listed_ref[0, peer], 0) for peer in block]
        scores = []
        for at in range(0, FAR_BLOCK, 2):
            peer = first + at
            keys = jnp.concatenate(
                [pool_ref[pages[at], :, :HEAD_DIM], pool_ref[pages[at + 1], :, :HEAD_DIM]], 0
            )
            both = jnp.concatenate([q_ref[peer], q_ref[peer + 1]], 0)
            score = SCALE * lax.dot_general(both, keys, NT, preferred_element_type=jnp.float32)
            scores += [score[:GROUP, :page_len], score[GROUP:, page_len:]]
        tops = [
            jnp.max(score, axis=1, keepdims=True).astype(jnp.bfloat16).astype(jnp.float32)
            for score in scores
        ]
        probs = [jnp.exp(score - top).astype(jnp.bfloat16) for score, top in zip(scores, tops)]
        totals = [jnp.sum(prob.astype(jnp.float32), axis=1, keepdims=True) for prob in probs]
        outs = []
        for at in range(0, FAR_BLOCK, 2):
            values = jnp.concatenate(
                [pool_ref[pages[at], :, HEAD_DIM:], pool_ref[pages[at + 1], :, HEAD_DIM:]], 0
            )
            both = jnp.concatenate(
                [
                    jnp.concatenate([probs[at], none], 1),
                    jnp.concatenate([none, probs[at + 1]], 1),
                ],
                0,
            )
            out = jnp.dot(both, values, preferred_element_type=jnp.float32)
            outs += [out[:GROUP], out[GROUP:]]
        for peer, out, top, total in zip(block, outs, tops, totals):
            high = total.astype(jnp.bfloat16).astype(jnp.float32)
            stats = jnp.where(lane == 0, top, jnp.where(lane == 1, high, total - high))
            out_ref[peer] = jnp.concatenate([out / total, stats], 0).astype(jnp.bfloat16)


def join_kernel(pages_ref, out_ref, top_ref, total_ref, back_ref, rows_ref, heads):
    slots = range(pages_ref.shape[0])
    places = range(FAR_POSITIONS)
    entries = [[pages_ref[slot, place] for place in places] for slot in slots]
    parts = [
        [back_ref[jnp.maximum(entry - POOL, 0)].astype(jnp.float32) for entry in row]
        for row in entries
    ]
    tops = [
        [jnp.where(entry >= POOL, part[GROUP:, 0:1], NEVER) for entry, part in zip(*pair)]
        for pair in zip(entries, parts)
    ]
    totals = [[part[GROUP:, 1:2] + part[GROUP:, 2:3] for part in row] for row in parts]
    near_tops = [top_ref[slot] for slot in slots]
    peaks = near_tops
    for place in places:
        peaks = [jnp.maximum(peak, row[place]) for peak, row in zip(peaks, tops)]
    keeps = [jnp.exp(top - peak) for top, peak in zip(near_tops, peaks)]
    denoms = [keep * total_ref[slot] for slot, keep in zip(slots, keeps)]
    numers = [keep * out_ref[slot] for slot, keep in zip(slots, keeps)]
    for place in places:
        for slot in slots:
            weight = jnp.exp(tops[slot][place] - peaks[slot]) * totals[slot][place]
            denoms[slot] = denoms[slot] + weight
            numers[slot] = numers[slot] + weight * parts[slot][place][:GROUP]
    for slot in slots:
        heads[slot] = numers[slot] / denoms[slot]
    for head in range(GROUP):
        block = heads[:, head, :].astype(jnp.bfloat16)
        for copy in range(rows_ref.shape[0]):
            rows_ref[copy, :, head * HEAD_DIM:(head + 1) * HEAD_DIM] = block


def project_kernel(rows_ref, which_ref, wo_ref, down_ref, up_ref, part_ref):
    rows = rows_ref[...]
    count = rows.shape[0]
    shrink = jnp.dot(rows, down_ref[...], preferred_element_type=jnp.float32)
    base = jnp.dot(rows, wo_ref[...], preferred_element_type=jnp.float32)
    adapter_of = lax.broadcasted_iota(jnp.int32, shrink.shape, 1) // ADAPTER_RANK
    which = jnp.concatenate([which_ref[...]] * (shrink.shape[1] // which_ref.shape[1]), 1)
    shrink = jnp.where(which == adapter_of, shrink, 0.0)
    high = shrink.astype(jnp.bfloat16)
    low = (shrink - high.astype(jnp.float32)).astype(jnp.bfloat16)
    both = jnp.dot(
        jnp.concatenate([high, low], 0), up_ref[...], preferred_element_type=jnp.float32
    )
    part_ref[...] = (base + both[:count] + both[count:]).astype(jnp.bfloat16)


def body(
    queries,
    current_key_value,
    key_value_pages,
    transfer_pages,
    request_pages,
    lengths,
    request_adapter,
    residual_input,
    wo,
    down_weight,
    up_weight,
):
    slots, _ = request_pages.shape
    peers = transfer_pages.shape[1]
    heads = (slots, GROUP, HEAD_DIM)
    around = ("inst", "batch")
    params = pltpu.CompilerParams(vmem_limit_bytes=16 * 1024 * 1024)
    out_q, listed = pl.pallas_call(
        outgoing_kernel,
        out_shape=[
            jax.ShapeDtypeStruct((peers, GROUP, HEAD_DIM), jnp.bfloat16),
            jax.ShapeDtypeStruct(transfer_pages.shape, jnp.int32),
        ],
        in_specs=[HBM, HBM, HBM],
        out_specs=[VMEM, VMEM],
        scratch_shapes=[
            pltpu.SMEM(request_pages.shape, jnp.int32),
            pltpu.VMEM(queries.shape, jnp.bfloat16),
            pltpu.VMEM(heads, jnp.float32),
            pltpu.VMEM((peers + 1, GROUP, HEAD_DIM), jnp.float32),
            pltpu.SemaphoreType.DMA((3,)),
        ],
        compiler_params=params,
        cost_estimate=pl.CostEstimate(
            flops=100_000_000_000, bytes_accessed=400_000_000, transcendentals=0
        ),
        name="outgoing",
    )(in_hbm(request_pages), in_hbm(queries), in_hbm(transfer_pages))
    in_q = lax.all_to_all(out_q, around, 0, 0, tiled=True)
    near_out, near_top, near_total, which = pl.pallas_call(
        near_kernel,
        out_shape=[jax.ShapeDtypeStruct(heads, jnp.float32)] * 3
        + [jax.ShapeDtypeStruct((request_adapter.shape[0], HEAD_DIM), jnp.int32)],
        in_specs=[SMEM, SMEM, SMEM, VMEM, VMEM, VMEM],
        out_specs=[VMEM] * 4,
        scratch_shapes=[pltpu.VMEM(heads, jnp.float32)],
        compiler_params=params,
        cost_estimate=pl.CostEstimate(
            flops=34_000_000, bytes_accessed=14_000_000, transcendentals=70_000
        ),
        name="near",
    )(request_pages, lengths, request_adapter, queries, current_key_value, key_value_pages)
    far = pl.pallas_call(
        far_kernel,
        out_shape=jax.ShapeDtypeStruct((peers, 2 * GROUP, HEAD_DIM), jnp.bfloat16),
        in_specs=[SMEM, VMEM, VMEM],
        out_specs=VMEM,
        compiler_params=params,
        cost_estimate=pl.CostEstimate(
            flops=17_000_000, bytes_accessed=4_200_000, transcendentals=35_000
        ),
        name="far",
    )(listed, in_q, key_value_pages)
    back = lax.all_to_all(far, around, 0, 0, tiled=True)
    group = lax.axis_size("batch")
    copies = pl.pallas_call(
        join_kernel,
        out_shape=jax.ShapeDtypeStruct((group, slots, GROUP * HEAD_DIM), jnp.bfloat16),
        in_specs=[SMEM, VMEM, VMEM, VMEM, VMEM],
        out_specs=VMEM,
        scratch_shapes=[pltpu.VMEM(heads, jnp.float32)],
        compiler_params=params,
        cost_estimate=pl.CostEstimate(
            flops=100_000_000_000, bytes_accessed=400_000_000, transcendentals=0
        ),
        name="join",
    )(request_pages, near_out, near_top, near_total, back)
    rows = lax.all_to_all(copies, "batch", 0, 0, tiled=True).reshape(-1, GROUP * HEAD_DIM)
    part = pl.pallas_call(
        project_kernel,
        out_shape=jax.ShapeDtypeStruct((rows.shape[0], wo.shape[1]), jnp.bfloat16),
        in_specs=[VMEM] * 5,
        out_specs=VMEM,
        compiler_params=params,
        name="project",
    )(rows, which, wo, down_weight, up_weight)
    parts = lax.all_to_all(
        part.reshape(lax.axis_size("tensor"), -1, part.shape[1]), "tensor", 0, 0, tiled=True
    )
    summed = jnp.sum(parts.astype(jnp.float32), axis=0)
    return (residual_input.astype(jnp.float32) + summed).astype(jnp.bfloat16)


def solution(mesh):
    return jax.shard_map(
        body,
        mesh=mesh,
        in_specs=(
            P(("inst", "batch"), "tensor"),
            P(("inst", "batch"), "tensor"),
            P(("inst", "batch"), None, "tensor"),
            P(("inst", "batch"), None),
            P(("inst", "batch"), None),
            P(("inst", "batch")),
            P("inst"),
            P(("inst", "tensor"), "batch"),
            P("tensor", "batch"),
            P("tensor", None),
            P(None, "batch"),
        ),
        out_specs=P(("inst", "tensor"), "batch"),
        check_vma=False,
    )
```

time: 77.7 us -> 63.7 us (0.82)
  blocking collectives: 34.3 us -> 45.1 us
  Pallas kernels: 15 us -> 6.28 us
  waiting for transfers between devices: 11 us -> 5.17 us
  local copies, waits for them, and re-layouts: 6.61 us -> 2.24 us
  starting transfers between devices: 7.26 us -> 3.84 us
  matrix products: 2.32 us -> 0 us
    all_to_all x0 -> x1, blocking collectives: none -> 10.5 us  [body(): lax.all_to_all(copies, 'batch', 0, 0, tiled=True)]
    all_to_all x1 -> x0, waiting for transfers between devices: 8.03 us -> none  [body(): lax.all_to_all(copies, 'batch', 0, 0, tiled=True)]
    pallas_call x1, Pallas kernels: 8.8 us -> 1.8 us  [body(): pl.pallas_call(far_kernel, out_shape=jax.ShapeDtypeStruct((peers, 2 * GRO...]
    unnamed x26 -> x22, local copies, waits for them, and re-layouts: 6.61 us -> 2.24 us
    all_to_all x1 -> x0, starting transfers between devices: 3.41 us -> none  [body(): lax.all_to_all(copies, 'batch', 0, 0, tiled=True)]
    dot_general x3 -> x0, matrix products: 2.32 us -> none  [the longest x1 1.54 us: body(): jnp.dot(jnp.concatenate([high, low], 0), up_weight, preferred_element_typ...]
    pallas_call x1, Pallas kernels: 3.97 us -> 1.73 us  [body(): pl.pallas_call(near_kernel, out_shape=[jax.ShapeDtypeStruct(heads, jnp.fl...]
    all_to_all x1, waiting for transfers between devices: 2.93 us -> 5.17 us  [body(): back = lax.all_to_all(far, around, 0, 0, tiled=True)]
  transfers between devices with their start and end apart: 2 -> 1, of which waited for: 2 -> 1; matrix products, arithmetic and copies ran while one was open for 0% -> 0% of each run, Pallas kernels for 5% -> 3%
where the time goes in v3:
time: 63.7 us; the launch traced here: 63.4 us
  blocking collectives  45.1 us (71%)
  Pallas kernels  6.28 us (10%)
  waiting for transfers between devices  5.17 us (8%)
  starting transfers between devices  3.84 us (6%)
  local copies, waits for them, and re-layouts  2.24 us (4%)
  other arithmetic  0.64 us (1%)
    all_to_all x1, blocking collectives, body(): in_q = lax.all_to_all(out_q, around, 0, 0, tiled=True)  20.8 us
    all_to_all x1, blocking collectives, body(): lax.all_to_all(part.reshape(lax.axis_size('tensor'), -1, part.shape[1]),...  13.8 us
    all_to_all x1, blocking collectives, body(): lax.all_to_all(copies, 'batch', 0, 0, tiled=True)  10.5 us
    all_to_all x1, waiting for transfers between devices, body(): back = lax.all_to_all(far, around, 0, 0, tiled=True)  5.17 us
    all_to_all x1, starting transfers between devices, body(): back = lax.all_to_all(far, around, 0, 0, tiled=True)  3.84 us
    unnamed x22, local copies, waits for them, and re-layouts  2.24 us
    pallas_call x1, Pallas kernels, body(): pl.pallas_call(far_kernel, out_shape=jax.ShapeDtypeStruct((peers, 2 * GRO...  1.8 us
    pallas_call x1, Pallas kernels, body(): pl.pallas_call(near_kernel, out_shape=[jax.ShapeDtypeStruct(heads, jnp.fl...  1.73 us
  transfers between devices with their start and end apart: 1, of which 1 were waited for; matrix products, arithmetic and copies ran while one was open for 0% of the time, Pallas kernels for 3%

profile of v3, /device:TPU:1, one launch (start us, length us, event | category | flops | bytes accessed | tf_op | source)
XLA Modules:
  0.0 63.4 jit_solution(8261745533060321999)
XLA Ops:
  0.0 0.0 copy-start
  0.0 1.0 %outgoing.1 = (bf16[32,8,128]{2,1,0:T(8,128)(2,1)S(1)}, s32[1,32]{1,0:T(1,128)S(1)}) custom-call(s32[8,8]{1,0:T(8,128)} %pages_ref.3, bf16[8,1024]{1,0:T(8,128)(2,1)} %q_hbm.1, s32[1,32]{1,0:T(1,128)} %listed_hbm.1), custom_call_target="tpu_custom_call" | custom-call | flops 99999997952 | bytes 400000000 | tf_op jit(solution)/shard_map/outgoing/pallas_call | solution.py:232
  1.0 0.0 copy-start.5
  1.0 0.0 copy-start.6
  1.0 0.0 copy-start.7
  1.0 0.0 copy-start.8
  1.0 0.0 copy-start.9
  1.1 20.8 %all_to_all.20.q_ref = bf16[32,8,128]{2,1,0:T(8,128)(2,1)S(1)} all-to-all(bf16[32,8,128]{2,1,0:T(8,128)(2,1)S(1)} %get-tuple-element.15), channel_id=1, replica_groups=mesh['inst'=4,'batch'=8,'tensor'=8] {'inst','batch'}, dimensions={0} | all-to-all | bytes 131072 | tf_op jit(solution)/shard_map/all_to_all | solution.py:253
  21.9 0.0 copy-done
  21.9 1.8 %far.1 = bf16[32,16,128]{2,1,0:T(8,128)(2,1)} custom-call(s32[1,32]{1,0:T(1,128)S(1)} %get-tuple-element.14.listed_ref, bf16[32,8,128]{2,1,0:T(8,128)(2,1)S(1)} %all_to_all.20.q_ref, bf16[64,128,256]{2,1,0:T(8,128)(2,1)S(1)} %copy-done), custom_call_target="tpu_custom_call" | custom-call | flops 17000000 | bytes 4200000 | tf_op jit(solution)/shard_map/far/pallas_call | solution.py:267
  23.7 3.8 %all-to-all-start.1 = ((bf16[32,16,128]{2,1,0:T(8,128)(2,1)}), bf16[32,16,128]{2,1,0:T(8,128)(2,1)S(1)}, u32[]{:S(2)}, u32[]{:S(2)}) async-start(bf16[32,16,128]{2,1,0:T(8,128)(2,1)} %far.1), calls=%async_computation.1 | async-start | bytes 262144 | tf_op jit(solution)/shard_map/all_to_all | solution.py:278
  27.5 0.0 copy-done.5
  27.5 0.0 copy-done.6
  27.6 0.0 copy-done.7
  27.6 0.0 copy-done.8
  27.6 0.0 copy-done.9
  27.6 0.0 copy-start.1
  27.6 2.2 %copy-done.1 = bf16[64,128,256]{2,1,0:T(8,128)(2,1)S(1)} copy-done((bf16[64,128,256]{2,1,0:T(8,128)(2,1)S(1)}, bf16[64,128,256]{2,1,0:T(8,128)(2,1)}, u32[]{:S(2)}) %copy-start.1) | copy-done | bytes 4194328
  29.8 1.7 %near.1 = (f32[8,8,128]{2,1,0:T(8,128)S(1)}, f32[8,8,128]{2,1,0:T(8,128)S(1)}, f32[8,8,128]{2,1,0:T(8,128)S(1)}, s32[64,128]{1,0:T(8,128)S(1)}) custom-call(s32[8,8]{1,0:T(8,128)S(1)} %copy-done.7, s32[8]{0:T(128)S(1)} %copy-done.8, s32[64]{0:T(128)S(1)} %copy-done.9, bf16[8,1024]{1,0:T(8,128)(2,1)S(1)} %copy-done.5, bf16[8,256]{1,0:T(8,128)(2,1)S(1)} %copy-done.6, ...), custom_call_target="tpu_custom_call" | custom-call | flops 34000000 | bytes 14000000 | tf_op jit(solution)/shard_map/near/pallas_call | solution.py:254
  31.5 5.2 %all-to-all-done.1.back_ref = bf16[32,16,128]{2,1,0:T(8,128)(2,1)S(1)} async-done(((bf16[32,16,128]{2,1,0:T(8,128)(2,1)}), bf16[32,16,128]{2,1,0:T(8,128)(2,1)S(1)}, u32[]{:S(2)}, u32[]{:S(2)}) %all-to-all-start.1) | async-done | bytes 131104 | tf_op jit(solution)/shard_map/all_to_all | solution.py:278
  36.7 0.0 copy-start.2
  36.7 0.0 copy-start.3
  36.7 0.0 copy-start.4
  36.7 0.9 %join.1 = bf16[8,8,1024]{2,1,0:T(8,128)(2,1)S(1)} custom-call(s32[8,8]{1,0:T(8,128)S(1)} %copy-done.7, f32[8,8,128]{2,1,0:T(8,128)S(1)} %get-tuple-element.11.out_ref, f32[8,8,128]{2,1,0:T(8,128)S(1)} %get-tuple-element.12.top_ref, f32[8,8,128]{2,1,0:T(8,128)S(1)} %get-tuple-element.13.total_ref, bf16[32,16,128]{2,1,0:T(8,128)(2,1)S(1)} %all-to-all-done.1.back_ref), custom_call_target="tpu_custom_call" | custom-call | flops 99999997952 | bytes 400000000 | tf_op jit(solution)/shard_map/join/pallas_call | solution.py:280
  37.6 0.0 copy-start.10
  37.6 10.5 %all_to_all.21 = bf16[8,8,1024]{2,1,0:T(8,128)(2,1)S(1)} all-to-all(bf16[8,8,1024]{2,1,0:T(8,128)(2,1)S(1)} %join.1), channel_id=1, replica_groups=mesh['inst'=4,'batch'=8,'tensor'=8] {'batch'}, dimensions={0} | all-to-all | bytes 262144 | tf_op jit(solution)/shard_map/all_to_all | solution.py:292
  48.1 0.0 copy-done.2
  48.1 0.0 copy-done.3
  48.1 0.0 copy-done.4
  48.1 0.9 %project.1 = bf16[64,1024]{1,0:T(8,128)(2,1)S(1)} custom-call(bf16[64,1024]{1,0:T(8,128)(2,1)S(1)} %bitcast.2, s32[64,128]{1,0:T(8,128)S(1)} %get-tuple-element.16.which_ref, bf16[1024,1024]{1,0:T(8,128)(2,1)S(1)} %copy-done.2, bf16[1024,512]{1,0:T(8,128)(2,1)S(1)} %copy-done.3, bf16[512,1024]{1,0:T(8,128)(2,1)S(1)} %copy-done.4), custom_call_target="tpu_custom_call" | custom-call | tf_op jit(solution)/shard_map/project/pallas_call | solution.py:293
  49.0 13.8 %all_to_all.22 = bf16[8,8,1024]{2,1,0:T(8,128)(2,1)S(1)} all-to-all(bf16[8,8,1024]{2,1,0:T(8,128)(2,1)S(1)} %bitcast.3), channel_id=1, replica_groups=mesh['inst'=4,'batch'=8,'tensor'=8] {'tensor'}, dimensions={0} | all-to-all | bytes 262144 | tf_op jit(solution)/shard_map/all_to_all | solution.py:301
  62.8 0.0 copy-done.10
  62.8 0.6 add_convert_fusion
  (1 shorter events, 0.0 us)
Async XLA Ops:
  0.0 21.9 %copy-start = (bf16[64,128,256]{2,1,0:T(8,128)(2,1)S(1)}, bf16[64,128,256]{2,1,0:T(8,128)(2,1)}, u32[]{:S(2)}) copy-start(bf16[64,128,256]{2,1,0:T(8,128)(2,1)} %pool_ref.3) | copy-start | bytes 12582916
  1.0 26.5 %copy-start.5 = (bf16[8,1024]{1,0:T(8,128)(2,1)S(1)}, bf16[8,1024]{1,0:T(8,128)(2,1)}, u32[]{:S(2)}) copy-start(bf16[8,1024]{1,0:T(8,128)(2,1)} %q_hbm.1) | copy-start | bytes 49156
  1.0 26.5 %copy-start.6 = (bf16[8,256]{1,0:T(8,128)(2,1)S(1)}, bf16[8,256]{1,0:T(8,128)(2,1)}, u32[]{:S(2)}) copy-start(bf16[8,256]{1,0:T(8,128)(2,1)} %fresh_ref.1) | copy-start | bytes 12292
  1.0 26.5 %copy-start.7 = (s32[8,8]{1,0:T(8,128)S(1)}, s32[8,8]{1,0:T(8,128)}, u32[]{:S(2)}) copy-start(s32[8,8]{1,0:T(8,128)} %pages_ref.3) | copy-start | bytes 772
  1.0 26.5 %copy-start.8 = (s32[8]{0:T(128)S(1)}, s32[8]{0:T(128)}, u32[]{:S(2)}) copy-start(s32[8]{0:T(128)} %lengths_ref.1) | copy-start | bytes 100
  1.0 26.5 %copy-start.9 = (s32[64]{0:T(128)S(1)}, s32[64]{0:T(128)}, u32[]{:S(2)}) copy-start(s32[64]{0:T(128)} %adapter_ref.1) | copy-start | bytes 772
  23.7 13.0 %all-to-all-start.1 = ((bf16[32,16,128]{2,1,0:T(8,128)(2,1)}), bf16[32,16,128]{2,1,0:T(8,128)(2,1)S(1)}, u32[]{:S(2)}, u32[]{:S(2)}) async-start(bf16[32,16,128]{2,1,0:T(8,128)(2,1)} %far.1), calls=%async_computation.1 | async-start | bytes 262144 | tf_op jit(solution)/shard_map/all_to_all | solution.py:278
  27.6 2.2 %copy-start.1 = (bf16[64,128,256]{2,1,0:T(8,128)(2,1)S(1)}, bf16[64,128,256]{2,1,0:T(8,128)(2,1)}, u32[]{:S(2)}) copy-start(bf16[64,128,256]{2,1,0:T(8,128)(2,1)} %pool_ref.3) | copy-start | bytes 12582916
  36.7 11.4 %copy-start.2 = (bf16[1024,1024]{1,0:T(8,128)(2,1)S(1)}, bf16[1024,1024]{1,0:T(8,128)(2,1)}, u32[]{:S(2)}) copy-start(bf16[1024,1024]{1,0:T(8,128)(2,1)} %wo_ref.1) | copy-start | bytes 6291460
  36.7 11.4 %copy-start.3 = (bf16[1024,512]{1,0:T(8,128)(2,1)S(1)}, bf16[1024,512]{1,0:T(8,128)(2,1)}, u32[]{:S(2)}) copy-start(bf16[1024,512]{1,0:T(8,128)(2,1)} %down_ref.1) | copy-start | bytes 3145732
  36.7 11.4 %copy-start.4 = (bf16[512,1024]{1,0:T(8,128)(2,1)S(1)}, bf16[512,1024]{1,0:T(8,128)(2,1)}, u32[]{:S(2)}) copy-start(bf16[512,1024]{1,0:T(8,128)(2,1)} %up_ref.1) | copy-start | bytes 3145732
  37.6 25.3 %copy-start.10 = (bf16[8,1024]{1,0:T(8,128)(2,1)S(1)}, bf16[8,1024]{1,0:T(8,128)(2,1)}, u32[]{:S(2)}) copy-start(bf16[8,1024]{1,0:T(8,128)(2,1)} %param.18) | copy-start | bytes 49156

commit v4 on v3

v4 whole, which is shorter than its diff:
```python
import math

import jax
import jax.numpy as jnp
from jax import lax
from jax.experimental import pallas as pl
from jax.experimental.pallas import tpu as pltpu
from jax.sharding import PartitionSpec as P

HEAD_DIM = 128
GROUP = 8
ADAPTER_RANK = 64
FAR_POSITIONS = 4
FAR_BLOCK = 32
NEAR_BLOCK = 4
POOL = 64
SCALE = 1.0 / math.sqrt(HEAD_DIM)
NEVER = -1e30
VMEM = pl.BlockSpec(memory_space=pltpu.VMEM)
HBM = pl.BlockSpec(memory_space=pltpu.HBM)
NT = (((1,), (1,)), ((), ()))


def in_hbm(array):
    return pltpu.with_memory_space_constraint(array, pltpu.HBM)


def down_rows(line):
    square = (line.shape[1], line.shape[1])
    diagonal = lax.broadcasted_iota(jnp.int32, square, 0) == lax.broadcasted_iota(
        jnp.int32, square, 1
    )
    column = jnp.sum(jnp.where(diagonal, line.astype(jnp.float32), 0.0), axis=1, keepdims=True)
    return column.astype(jnp.int32)


def heads_of(q_ref, q_heads):
    q = q_ref[...].astype(jnp.float32)
    for head in range(GROUP):
        q_heads[:, head, :] = q[:, head * HEAD_DIM:(head + 1) * HEAD_DIM]


def outgoing_kernel(pages_hbm, q_hbm, out_ref, pages_ref, q_ref, q_heads, rows, sems):
    first = pltpu.make_async_copy(q_hbm, q_ref, sems.at[0])
    second = pltpu.make_async_copy(pages_hbm, pages_ref, sems.at[1])
    first.start()
    second.start()
    rows[...] = jnp.zeros_like(rows)
    first.wait()
    second.wait()
    heads_of(q_ref, q_heads)
    slots, peers = q_ref.shape[0], out_ref.shape[0]
    pages = pages_ref[...]
    targets = jnp.where(pages >= POOL, pages - POOL, peers)
    for slot in range(slots):
        for place in range(FAR_POSITIONS):
            rows[targets[slot, place]] = q_heads[slot]
    out_ref[...] = rows[:peers].astype(jnp.bfloat16)


def far_kernel(listed_ref, q_ref, pool_ref, out_ref):
    peers = q_ref.shape[0]
    page_len = pool_ref.shape[1]
    lane = lax.broadcasted_iota(jnp.int32, (GROUP, HEAD_DIM), 1)
    none = jnp.zeros((GROUP, page_len), jnp.bfloat16)
    listed = jnp.maximum(listed_ref[...], 0)
    for first in range(0, peers, FAR_BLOCK):
        block = range(first, first + FAR_BLOCK)
        pages = [listed[0, peer] for peer in block]
        scores = []
        for at in range(0, FAR_BLOCK, 2):
            peer = first + at
            keys = jnp.concatenate(
                [pool_ref[pages[at], :, :HEAD_DIM], pool_ref[pages[at + 1], :, :HEAD_DIM]], 0
            )
            both = jnp.concatenate([q_ref[peer], q_ref[peer + 1]], 0)
            score = SCALE * lax.dot_general(both, keys, NT, preferred_element_type=jnp.float32)
            scores += [score[:GROUP, :page_len], score[GROUP:, page_len:]]
        tops = [
            jnp.max(score, axis=1, keepdims=True).astype(jnp.bfloat16).astype(jnp.float32)
            for score in scores
        ]
        probs = [jnp.exp(score - top).astype(jnp.bfloat16) for score, top in zip(scores, tops)]
        totals = [jnp.sum(prob.astype(jnp.float32), axis=1, keepdims=True) for prob in probs]
        outs = []
        for at in range(0, FAR_BLOCK, 2):
            values = jnp.concatenate(
                [pool_ref[pages[at], :, HEAD_DIM:], pool_ref[pages[at + 1], :, HEAD_DIM:]], 0
            )
            both = jnp.concatenate(
                [
                    jnp.concatenate([probs[at], none], 1),
                    jnp.concatenate([none, probs[at + 1]], 1),
                ],
                0,
            )
            out = jnp.dot(both, values, preferred_element_type=jnp.float32)
            outs += [out[:GROUP], out[GROUP:]]
        for peer, out, top, total in zip(block, outs, tops, totals):
            high = total.astype(jnp.bfloat16).astype(jnp.float32)
            stats = jnp.where(lane == 0, top, jnp.where(lane == 1, high, total - high))
            out_ref[peer] = jnp.concatenate([out / total, stats], 0).astype(jnp.bfloat16)


def near_parts(pages_ref, lengths_ref, q_ref, fresh_ref, pool_ref, q_heads):
    slots, places = pages_ref.shape
    page_len = pool_ref.shape[1]
    pages = pages_ref[...]
    before = page_len * lax.broadcasted_iota(jnp.int32, pages.shape, 1)
    limits = jnp.where(pages < POOL, down_rows(lengths_ref[...]) - before, 0)
    pages = jnp.where(pages < POOL, pages, 0)
    heads_of(q_ref, q_heads)
    fresh = fresh_ref[...].astype(jnp.float32)
    lane = lax.broadcasted_iota(jnp.int32, (GROUP, page_len), 1)
    near_tops, near_totals, near_outs = [], [], []
    for first in range(0, slots, NEAR_BLOCK):
        block = range(first, first + NEAR_BLOCK)
        index = {}
        scores = {}
        for slot in block:
            for place in range(places):
                index[slot, place] = pages[slot, place]
            keys = [pool_ref[index[slot, place], :, :HEAD_DIM] for place in range(places)]
            score = SCALE * lax.dot_general(
                q_heads[slot].astype(jnp.bfloat16),
                jnp.concatenate(keys, 0),
                NT,
                preferred_element_type=jnp.float32,
            )
            scores[slot] = [
                jnp.where(
                    lane < limits[slot:slot + 1, at:at + 1],
                    score[:, at * page_len:(at + 1) * page_len],
                    NEVER,
                )
                for at in range(places)
            ]
        owns = [
            SCALE
            * jnp.sum(q_heads[slot] * fresh[slot:slot + 1, :HEAD_DIM], axis=1, keepdims=True)
            for slot in block
        ]
        tops = []
        for slot, own in zip(block, owns):
            top = scores[slot][0]
            for score in scores[slot][1:]:
                top = jnp.maximum(top, score)
            tops.append(jnp.maximum(jnp.max(top, axis=1, keepdims=True), own))
        weights = [jnp.exp(own - top) for own, top in zip(owns, tops)]
        for slot, top, weight in zip(block, tops, weights):
            probs = [jnp.exp(score - top).astype(jnp.bfloat16) for score in scores[slot]]
            summed = probs[0].astype(jnp.float32)
            for prob in probs[1:]:
                summed = summed + prob.astype(jnp.float32)
            values = [pool_ref[index[slot, place], :, HEAD_DIM:] for place in range(places)]
            out = jnp.dot(
                jnp.concatenate(probs, 1),
                jnp.concatenate(values, 0),
                preferred_element_type=jnp.float32,
            )
            total = jnp.sum(summed, axis=1, keepdims=True) + weight
            near_tops.append(top)
            near_totals.append(total)
            near_outs.append(out + weight * fresh[slot:slot + 1, HEAD_DIM:])
    return near_tops, near_totals, near_outs


def join_kernel(
    pages_ref, lengths_ref, q_ref, fresh_ref, pool_ref, back_ref, rows_ref, q_heads, heads
):
    near_tops, near_totals, near_outs = near_parts(
        pages_ref, lengths_ref, q_ref, fresh_ref, pool_ref, q_heads
    )
    slots = range(pages_ref.shape[0])
    places = range(FAR_POSITIONS)
    pages = pages_ref[...]
    senders = jnp.maximum(pages - POOL, 0)
    parts = [
        [back_ref[senders[slot, place]].astype(jnp.float32) for place in places]
        for slot in slots
    ]
    tops = [
        [
            jnp.where(
                pages[slot:slot + 1, place:place + 1] >= POOL,
                parts[slot][place][GROUP:, 0:1],
                NEVER,
            )
            for place in places
        ]
        for slot in slots
    ]
    totals = [[part[GROUP:, 1:2] + part[GROUP:, 2:3] for part in row] for row in parts]
    peaks = near_tops
    for place in places:
        peaks = [jnp.maximum(peak, row[place]) for peak, row in zip(peaks, tops)]
    keeps = [jnp.exp(top - peak) for top, peak in zip(near_tops, peaks)]
    denoms = [keep * total for total, keep in zip(near_totals, keeps)]
    numers = [keep * out for out, keep in zip(near_outs, keeps)]
    for place in places:
        for slot in slots:
            weight = jnp.exp(tops[slot][place] - peaks[slot]) * totals[slot][place]
            denoms[slot] = denoms[slot] + weight
            numers[slot] = numers[slot] + weight * parts[slot][place][:GROUP]
    for slot in slots:
        heads[slot] = numers[slot] / denoms[slot]
    for head in range(GROUP):
        block = heads[:, head, :].astype(jnp.bfloat16)
        for copy in range(rows_ref.shape[0]):
            rows_ref[copy, :, head * HEAD_DIM:(head + 1) * HEAD_DIM] = block


def project_kernel(rows_ref, which_ref, wo_ref, down_ref, up_ref, part_ref):
    rows = rows_ref[...]
    count = rows.shape[0]
    shrink = jnp.dot(rows, down_ref[...], preferred_element_type=jnp.float32)
    base = jnp.dot(rows, wo_ref[...], preferred_element_type=jnp.float32)
    adapter_of = lax.broadcasted_iota(jnp.int32, shrink.shape, 1) // ADAPTER_RANK
    which = down_rows(which_ref[...])
    shrink = jnp.where(which == adapter_of, shrink, 0.0)
    high = shrink.astype(jnp.bfloat16)
    low = (shrink - high.astype(jnp.float32)).astype(jnp.bfloat16)
    both = jnp.dot(
        jnp.concatenate([high, low], 0), up_ref[...], preferred_element_type=jnp.float32
    )
    part_ref[...] = (base + both[:count] + both[count:]).astype(jnp.bfloat16)


def body(
    queries,
    current_key_value,
    key_value_pages,
    transfer_pages,
    request_pages,
    lengths,
    request_adapter,
    residual_input,
    wo,
    down_weight,
    up_weight,
):
    slots, _ = request_pages.shape
    peers = transfer_pages.shape[1]
    heads = (slots, GROUP, HEAD_DIM)
    around = ("inst", "batch")
    params = pltpu.CompilerParams(vmem_limit_bytes=16 * 1024 * 1024)
    out_q = pl.pallas_call(
        outgoing_kernel,
        out_shape=jax.ShapeDtypeStruct((peers, GROUP, HEAD_DIM), jnp.bfloat16),
        in_specs=[HBM, HBM],
        out_specs=VMEM,
        scratch_shapes=[
            pltpu.VMEM(request_pages.shape, jnp.int32),
            pltpu.VMEM(queries.shape, jnp.bfloat16),
            pltpu.VMEM(heads, jnp.float32),
            pltpu.VMEM((peers + 1, GROUP, HEAD_DIM), jnp.float32),
            pltpu.SemaphoreType.DMA((2,)),
        ],
        compiler_params=params,
        cost_estimate=pl.CostEstimate(
            flops=100_000_000_000, bytes_accessed=400_000_000, transcendentals=0
        ),
        name="outgoing",
    )(in_hbm(request_pages), in_hbm(queries))
    in_q = lax.all_to_all(out_q, around, 0, 0, tiled=True)
    far = pl.pallas_call(
        far_kernel,
        out_shape=jax.ShapeDtypeStruct((peers, 2 * GROUP, HEAD_DIM), jnp.bfloat16),
        in_specs=[VMEM, VMEM, VMEM],
        out_specs=VMEM,
        compiler_params=params,
        cost_estimate=pl.CostEstimate(
            flops=100_000_000_000, bytes_accessed=400_000_000, transcendentals=0
        ),
        name="far",
    )(transfer_pages, in_q, key_value_pages)
    back = lax.all_to_all(far, around, 0, 0, tiled=True)
    group = lax.axis_size("batch")
    copies = pl.pallas_call(
        join_kernel,
        out_shape=jax.ShapeDtypeStruct((group, slots, GROUP * HEAD_DIM), jnp.bfloat16),
        in_specs=[VMEM] * 6,
        out_specs=VMEM,
        scratch_shapes=[pltpu.VMEM(heads, jnp.float32), pltpu.VMEM(heads, jnp.float32)],
        compiler_params=params,
        cost_estimate=pl.CostEstimate(
            flops=100_000_000_000, bytes_accessed=400_000_000, transcendentals=0
        ),
        name="join",
    )(
        request_pages,
        lengths[None],
        queries,
        current_key_value,
        key_value_pages,
        back,
    )
    rows = lax.all_to_all(copies, "batch", 0, 0, tiled=True).reshape(-1, GROUP * HEAD_DIM)
    part = pl.pallas_call(
        project_kernel,
        out_shape=jax.ShapeDtypeStruct((rows.shape[0], wo.shape[1]), jnp.bfloat16),
        in_specs=[VMEM] * 5,
        out_specs=VMEM,
        compiler_params=params,
        name="project",
    )(rows, request_adapter[None], wo, down_weight, up_weight)
    parts = lax.all_to_all(
        part.reshape(lax.axis_size("tensor"), -1, part.shape[1]), "tensor", 0, 0, tiled=True
    )
    summed = jnp.sum(parts.astype(jnp.float32), axis=0)
    return (residual_input.astype(jnp.float32) + summed).astype(jnp.bfloat16)


def solution(mesh):
    return jax.shard_map(
        body,
        mesh=mesh,
        in_specs=(
            P(("inst", "batch"), "tensor"),
            P(("inst", "batch"), "tensor"),
            P(("inst", "batch"), None, "tensor"),
            P(("inst", "batch"), None),
            P(("inst", "batch"), None),
            P(("inst", "batch")),
            P("inst"),
            P(("inst", "tensor"), "batch"),
            P("tensor", "batch"),
            P("tensor", None),
            P(None, "batch"),
        ),
        out_specs=P(("inst", "tensor"), "batch"),
        check_vma=False,
    )
```

time: 63.7 us -> 62.5 us (0.981)
  blocking collectives: 45.1 us -> 57.3 us
  waiting for transfers between devices: 5.17 us -> 0 us
  starting transfers between devices: 3.84 us -> 0 us
  local copies, waits for them, and re-layouts: 2.24 us -> 0.06 us
  Pallas kernels: 6.28 us -> 4.19 us
    all_to_all x0 -> x1, blocking collectives: none -> 12.3 us  [body(): back = lax.all_to_all(far, around, 0, 0, tiled=True)]
    all_to_all x1 -> x0, waiting for transfers between devices: 5.17 us -> none  [body(): back = lax.all_to_all(far, around, 0, 0, tiled=True)]
    all_to_all x1 -> x0, starting transfers between devices: 3.84 us -> none  [body(): back = lax.all_to_all(far, around, 0, 0, tiled=True)]
    unnamed x22, local copies, waits for them, and re-layouts: 2.24 us -> 0.06 us
    pallas_call x2 -> x1, Pallas kernels: 2.71 us -> 1.02 us  [body(): pl.pallas_call(outgoing_kernel, out_shape=jax.ShapeDtypeStruct((peers, GR...]
    pallas_call x1, Pallas kernels: 1.8 us -> 0.73 us  [body(): pl.pallas_call(far_kernel, out_shape=jax.ShapeDtypeStruct((peers, 2 * GRO...]
    pallas_call x1, Pallas kernels: 0.87 us -> 1.54 us  [body(): pl.pallas_call(join_kernel, out_shape=jax.ShapeDtypeStruct((group, slots,...]
  transfers between devices with their start and end apart: 1 -> 0, of which waited for: 1 -> 0; matrix products, arithmetic and copies ran while one was open for 0% -> 0% of each run, Pallas kernels for 3% -> 0%
where the time goes in v4:
time: 62.5 us; the launch traced here: 62.3 us
  blocking collectives  57.3 us (92%)
  Pallas kernels  4.19 us (7%)
  other arithmetic  0.64 us (1%)
    all_to_all x1, blocking collectives, body(): in_q = lax.all_to_all(out_q, around, 0, 0, tiled=True)  20.8 us
    all_to_all x1, blocking collectives, body(): lax.all_to_all(part.reshape(lax.axis_size('tensor'), -1, part.shape[1]),...  13.7 us
    all_to_all x1, blocking collectives, body(): back = lax.all_to_all(far, around, 0, 0, tiled=True)  12.3 us
    all_to_all x1, blocking collectives, body(): lax.all_to_all(copies, 'batch', 0, 0, tiled=True)  10.4 us
    pallas_call x1, Pallas kernels, body(): pl.pallas_call(join_kernel, out_shape=jax.ShapeDtypeStruct((group, slots,...  1.54 us

profile of v4, /device:TPU:1, one launch (start us, length us, event | category | flops | bytes accessed | tf_op | source)
XLA Modules:
  0.0 62.3 jit_solution(5489007803806474605)
XLA Ops:
  0.0 0.0 copy-start.4
  0.0 0.0 copy-start.8
  0.0 1.0 %outgoing.1 = bf16[32,8,128]{2,1,0:T(8,128)(2,1)S(1)} custom-call(s32[8,8]{1,0:T(8,128)} %pages_ref.1, bf16[8,1024]{1,0:T(8,128)(2,1)} %q_ref.1), custom_call_target="tpu_custom_call" | custom-call | flops 99999997952 | bytes 400000000 | tf_op jit(solution)/shard_map/outgoing/pallas_call | solution.py:247
  1.0 20.8 %all_to_all.20.q_ref = bf16[32,8,128]{2,1,0:T(8,128)(2,1)S(1)} all-to-all(bf16[32,8,128]{2,1,0:T(8,128)(2,1)S(1)} %outgoing.1), channel_id=1, replica_groups=mesh['inst'=4,'batch'=8,'tensor'=8] {'inst','batch'}, dimensions={0} | all-to-all | bytes 131072 | tf_op jit(solution)/shard_map/all_to_all | solution.py:265
  21.9 0.0 copy-done.4
  21.9 0.0 copy-done.8
  21.9 0.0 copy-start.5
  21.9 0.0 copy-start.6
  21.9 0.0 copy-start.7
  21.9 0.0 copy-start.9
  21.9 0.7 %far.1 = bf16[32,16,128]{2,1,0:T(8,128)(2,1)S(1)} custom-call(s32[1,32]{1,0:T(1,128)S(1)} %copy-done.8, bf16[32,8,128]{2,1,0:T(8,128)(2,1)S(1)} %all_to_all.20.q_ref, bf16[64,128,256]{2,1,0:T(8,128)(2,1)S(1)} %copy-done.4), custom_call_target="tpu_custom_call" | custom-call | flops 99999997952 | bytes 400000000 | tf_op jit(solution)/shard_map/far/pallas_call | solution.py:266
  22.6 12.3 %all_to_all.21.back_ref = bf16[32,16,128]{2,1,0:T(8,128)(2,1)S(1)} all-to-all(bf16[32,16,128]{2,1,0:T(8,128)(2,1)S(1)} %far.1), channel_id=1, replica_groups=mesh['inst'=4,'batch'=8,'tensor'=8] {'inst','batch'}, dimensions={0} | all-to-all | bytes 262144 | tf_op jit(solution)/shard_map/all_to_all | solution.py:277
  34.9 0.0 copy-done.5
  34.9 0.0 copy-done.6
  34.9 0.0 copy-done.7
  34.9 0.0 copy-done.9
  35.0 0.0 copy-start
  35.0 0.0 copy-start.1
  35.0 0.0 copy-start.2
  35.0 0.0 copy-start.3
  35.0 1.5 %join.1 = bf16[8,8,1024]{2,1,0:T(8,128)(2,1)S(1)} custom-call(s32[8,8]{1,0:T(8,128)S(1)} %copy-done.6, s32[1,8]{1,0:T(1,128)S(1)} %bitcast.7, bf16[8,1024]{1,0:T(8,128)(2,1)S(1)} %copy-done.5, bf16[8,256]{1,0:T(8,128)(2,1)S(1)} %copy-done.7, bf16[64,128,256]{2,1,0:T(8,128)(2,1)S(1)} %copy-done.4, bf16[32,16,128]{2,1,0:T(8,128)(2,1)S(1)} %all_to_all.21.back_ref), custom_call_target="tpu_custom_call" | custom-call | flops 99999997952 | bytes 400000000 | tf_op jit(solution)/shard_map/join/pallas_call | solution.py:279
  36.5 0.0 copy-start.10
  36.6 10.4 %all_to_all.22 = bf16[8,8,1024]{2,1,0:T(8,128)(2,1)S(1)} all-to-all(bf16[8,8,1024]{2,1,0:T(8,128)(2,1)S(1)} %join.1), channel_id=1, replica_groups=mesh['inst'=4,'batch'=8,'tensor'=8] {'batch'}, dimensions={0} | all-to-all | bytes 262144 | tf_op jit(solution)/shard_map/all_to_all | solution.py:298
  47.0 0.0 copy-done
  47.0 0.0 copy-done.1
  47.0 0.0 copy-done.2
  47.0 0.0 copy-done.3
  47.0 0.9 %project.1 = bf16[64,1024]{1,0:T(8,128)(2,1)S(1)} custom-call(bf16[64,1024]{1,0:T(8,128)(2,1)S(1)} %bitcast.4, s32[1,64]{1,0:T(1,128)S(1)} %bitcast.6, bf16[1024,1024]{1,0:T(8,128)(2,1)S(1)} %copy-done, bf16[1024,512]{1,0:T(8,128)(2,1)S(1)} %copy-done.1, bf16[512,1024]{1,0:T(8,128)(2,1)S(1)} %copy-done.2), custom_call_target="tpu_custom_call" | custom-call | tf_op jit(solution)/shard_map/project/pallas_call | solution.py:299
  47.9 13.7 %all_to_all.23 = bf16[8,8,1024]{2,1,0:T(8,128)(2,1)S(1)} all-to-all(bf16[8,8,1024]{2,1,0:T(8,128)(2,1)S(1)} %bitcast.5), channel_id=1, replica_groups=mesh['inst'=4,'batch'=8,'tensor'=8] {'tensor'}, dimensions={0} | all-to-all | bytes 262144 | tf_op jit(solution)/shard_map/all_to_all | solution.py:307
  61.6 0.0 copy-done.10
  61.7 0.6 add_convert_fusion
  (1 shorter events, 0.0 us)
Async XLA Ops:
  0.0 21.9 %copy-start.4 = (bf16[64,128,256]{2,1,0:T(8,128)(2,1)S(1)}, bf16[64,128,256]{2,1,0:T(8,128)(2,1)}, u32[]{:S(2)}) copy-start(bf16[64,128,256]{2,1,0:T(8,128)(2,1)} %pool_ref.3) | copy-start | bytes 12582916
  0.0 21.9 %copy-start.8 = (s32[1,32]{1,0:T(1,128)S(1)}, s32[1,32]{1,0:T(1,128)}, u32[]{:S(2)}) copy-start(s32[1,32]{1,0:T(1,128)} %listed_ref.1) | copy-start | bytes 388
  21.9 13.1 %copy-start.5 = (bf16[8,1024]{1,0:T(8,128)(2,1)S(1)}, bf16[8,1024]{1,0:T(8,128)(2,1)}, u32[]{:S(2)}) copy-start(bf16[8,1024]{1,0:T(8,128)(2,1)} %q_ref.1) | copy-start | bytes 49156
  21.9 13.1 %copy-start.6 = (s32[8,8]{1,0:T(8,128)S(1)}, s32[8,8]{1,0:T(8,128)}, u32[]{:S(2)}) copy-start(s32[8,8]{1,0:T(8,128)} %pages_ref.1) | copy-start | bytes 772
  21.9 13.1 %copy-start.7 = (bf16[8,256]{1,0:T(8,128)(2,1)S(1)}, bf16[8,256]{1,0:T(8,128)(2,1)}, u32[]{:S(2)}) copy-start(bf16[8,256]{1,0:T(8,128)(2,1)} %fresh_ref.1) | copy-start | bytes 12292
  21.9 13.1 %copy-start.9 = (s32[8]{0:T(128)S(1)}, s32[8]{0:T(128)}, u32[]{:S(2)}) copy-start(s32[8]{0:T(128)} %param.16) | copy-start | bytes 100
  35.0 12.0 %copy-start = (bf16[1024,1024]{1,0:T(8,128)(2,1)S(1)}, bf16[1024,1024]{1,0:T(8,128)(2,1)}, u32[]{:S(2)}) copy-start(bf16[1024,1024]{1,0:T(8,128)(2,1)} %wo_ref.1) | copy-start | bytes 6291460
  35.0 12.0 %copy-start.1 = (bf16[1024,512]{1,0:T(8,128)(2,1)S(1)}, bf16[1024,512]{1,0:T(8,128)(2,1)}, u32[]{:S(2)}) copy-start(bf16[1024,512]{1,0:T(8,128)(2,1)} %down_ref.1) | copy-start | bytes 3145732
  35.0 12.0 %copy-start.2 = (bf16[512,1024]{1,0:T(8,128)(2,1)S(1)}, bf16[512,1024]{1,0:T(8,128)(2,1)}, u32[]{:S(2)}) copy-start(bf16[512,1024]{1,0:T(8,128)(2,1)} %up_ref.1) | copy-start | bytes 3145732
  35.0 12.0 %copy-start.3 = (s32[64]{0:T(128)S(1)}, s32[64]{0:T(128)}, u32[]{:S(2)}) copy-start(s32[64]{0:T(128)} %param.17) | copy-start | bytes 772
  36.5 25.1 %copy-start.10 = (bf16[8,1024]{1,0:T(8,128)(2,1)S(1)}, bf16[8,1024]{1,0:T(8,128)(2,1)}, u32[]{:S(2)}) copy-start(bf16[8,1024]{1,0:T(8,128)(2,1)} %param.18) | copy-start | bytes 49156

commit v5 on v4

--- a/solution.py
+++ b/solution.py
@@ -12,7 +12,7 @@
 ADAPTER_RANK = 64
 FAR_POSITIONS = 4
 FAR_BLOCK = 32
-NEAR_BLOCK = 4
+NEAR_BLOCK = 8
 POOL = 64
 SCALE = 1.0 / math.sqrt(HEAD_DIM)
 NEVER = -1e30

time: 62.5 us -> 62.2 us (level)
  no operation moved by 1% of the time
where the time goes in v5:
time: 62.2 us; the launch traced here: 62 us
  blocking collectives  57.3 us (92%)
  Pallas kernels  3.91 us (6%)
  other arithmetic  0.64 us (1%)
    all_to_all x1, blocking collectives, body(): in_q = lax.all_to_all(out_q, around, 0, 0, tiled=True)  20.8 us
    all_to_all x1, blocking collectives, body(): lax.all_to_all(part.reshape(lax.axis_size('tensor'), -1, part.shape[1]),...  13.7 us
    all_to_all x1, blocking collectives, body(): back = lax.all_to_all(far, around, 0, 0, tiled=True)  12.3 us
    all_to_all x1, blocking collectives, body(): lax.all_to_all(copies, 'batch', 0, 0, tiled=True)  10.4 us
    pallas_call x1, Pallas kernels, body(): pl.pallas_call(join_kernel, out_shape=jax.ShapeDtypeStruct((group, slots,...  1.26 us

profile of v5, /device:TPU:1, one launch (start us, length us, event | category | flops | bytes accessed | tf_op | source)
XLA Modules:
  0.0 62.0 jit_solution(13243110009472456749)
XLA Ops:
  0.0 0.0 copy-start.4
  0.0 0.0 copy-start.8
  0.0 1.0 %outgoing.1 = bf16[32,8,128]{2,1,0:T(8,128)(2,1)S(1)} custom-call(s32[8,8]{1,0:T(8,128)} %pages_ref.1, bf16[8,1024]{1,0:T(8,128)(2,1)} %q_ref.1), custom_call_target="tpu_custom_call" | custom-call | flops 99999997952 | bytes 400000000 | tf_op jit(solution)/shard_map/outgoing/pallas_call | solution.py:247
  1.0 20.8 %all_to_all.20.q_ref = bf16[32,8,128]{2,1,0:T(8,128)(2,1)S(1)} all-to-all(bf16[32,8,128]{2,1,0:T(8,128)(2,1)S(1)} %outgoing.1), channel_id=1, replica_groups=mesh['inst'=4,'batch'=8,'tensor'=8] {'inst','batch'}, dimensions={0} | all-to-all | bytes 131072 | tf_op jit(solution)/shard_map/all_to_all | solution.py:265
  21.9 0.0 copy-done.4
  21.9 0.0 copy-done.8
  21.9 0.0 copy-start.5
  21.9 0.0 copy-start.6
  21.9 0.0 copy-start.7
  21.9 0.0 copy-start.9
  21.9 0.7 %far.1 = bf16[32,16,128]{2,1,0:T(8,128)(2,1)S(1)} custom-call(s32[1,32]{1,0:T(1,128)S(1)} %copy-done.8, bf16[32,8,128]{2,1,0:T(8,128)(2,1)S(1)} %all_to_all.20.q_ref, bf16[64,128,256]{2,1,0:T(8,128)(2,1)S(1)} %copy-done.4), custom_call_target="tpu_custom_call" | custom-call | flops 99999997952 | bytes 400000000 | tf_op jit(solution)/shard_map/far/pallas_call | solution.py:266
  22.6 12.3 %all_to_all.21.back_ref = bf16[32,16,128]{2,1,0:T(8,128)(2,1)S(1)} all-to-all(bf16[32,16,128]{2,1,0:T(8,128)(2,1)S(1)} %far.1), channel_id=1, replica_groups=mesh['inst'=4,'batch'=8,'tensor'=8] {'inst','batch'}, dimensions={0} | all-to-all | bytes 262144 | tf_op jit(solution)/shard_map/all_to_all | solution.py:277
  34.9 0.0 copy-done.5
  34.9 0.0 copy-done.6
  34.9 0.0 copy-done.7
  34.9 0.0 copy-done.9
  34.9 0.0 copy-start
  35.0 0.0 copy-start.1
  35.0 0.0 copy-start.2
  35.0 0.0 copy-start.3
  35.0 1.3 %join.1 = bf16[8,8,1024]{2,1,0:T(8,128)(2,1)S(1)} custom-call(s32[8,8]{1,0:T(8,128)S(1)} %copy-done.6, s32[1,8]{1,0:T(1,128)S(1)} %bitcast.7, bf16[8,1024]{1,0:T(8,128)(2,1)S(1)} %copy-done.5, bf16[8,256]{1,0:T(8,128)(2,1)S(1)} %copy-done.7, bf16[64,128,256]{2,1,0:T(8,128)(2,1)S(1)} %copy-done.4, bf16[32,16,128]{2,1,0:T(8,128)(2,1)S(1)} %all_to_all.21.back_ref), custom_call_target="tpu_custom_call" | custom-call | flops 99999997952 | bytes 400000000 | tf_op jit(solution)/shard_map/join/pallas_call | solution.py:279
  36.3 0.0 copy-start.10
  36.3 10.4 %all_to_all.22 = bf16[8,8,1024]{2,1,0:T(8,128)(2,1)S(1)} all-to-all(bf16[8,8,1024]{2,1,0:T(8,128)(2,1)S(1)} %join.1), channel_id=1, replica_groups=mesh['inst'=4,'batch'=8,'tensor'=8] {'batch'}, dimensions={0} | all-to-all | bytes 262144 | tf_op jit(solution)/shard_map/all_to_all | solution.py:298
  46.7 0.0 copy-done
  46.7 0.0 copy-done.1
  46.7 0.0 copy-done.2
  46.7 0.0 copy-done.3
  46.7 0.9 %project.1 = bf16[64,1024]{1,0:T(8,128)(2,1)S(1)} custom-call(bf16[64,1024]{1,0:T(8,128)(2,1)S(1)} %bitcast.4, s32[1,64]{1,0:T(1,128)S(1)} %bitcast.6, bf16[1024,1024]{1,0:T(8,128)(2,1)S(1)} %copy-done, bf16[1024,512]{1,0:T(8,128)(2,1)S(1)} %copy-done.1, bf16[512,1024]{1,0:T(8,128)(2,1)S(1)} %copy-done.2), custom_call_target="tpu_custom_call" | custom-call | tf_op jit(solution)/shard_map/project/pallas_call | solution.py:299
  47.6 13.7 %all_to_all.23 = bf16[8,8,1024]{2,1,0:T(8,128)(2,1)S(1)} all-to-all(bf16[8,8,1024]{2,1,0:T(8,128)(2,1)S(1)} %bitcast.5), channel_id=1, replica_groups=mesh['inst'=4,'batch'=8,'tensor'=8] {'tensor'}, dimensions={0} | all-to-all | bytes 262144 | tf_op jit(solution)/shard_map/all_to_all | solution.py:307
  61.4 0.0 copy-done.10
  61.4 0.6 add_convert_fusion
  (1 shorter events, 0.0 us)
Async XLA Ops:
  0.0 21.9 %copy-start.4 = (bf16[64,128,256]{2,1,0:T(8,128)(2,1)S(1)}, bf16[64,128,256]{2,1,0:T(8,128)(2,1)}, u32[]{:S(2)}) copy-start(bf16[64,128,256]{2,1,0:T(8,128)(2,1)} %pool_ref.3) | copy-start | bytes 12582916
  0.0 21.9 %copy-start.8 = (s32[1,32]{1,0:T(1,128)S(1)}, s32[1,32]{1,0:T(1,128)}, u32[]{:S(2)}) copy-start(s32[1,32]{1,0:T(1,128)} %listed_ref.1) | copy-start | bytes 388
  21.9 13.1 %copy-start.5 = (bf16[8,1024]{1,0:T(8,128)(2,1)S(1)}, bf16[8,1024]{1,0:T(8,128)(2,1)}, u32[]{:S(2)}) copy-start(bf16[8,1024]{1,0:T(8,128)(2,1)} %q_ref.1) | copy-start | bytes 49156
  21.9 13.1 %copy-start.6 = (s32[8,8]{1,0:T(8,128)S(1)}, s32[8,8]{1,0:T(8,128)}, u32[]{:S(2)}) copy-start(s32[8,8]{1,0:T(8,128)} %pages_ref.1) | copy-start | bytes 772
  21.9 13.1 %copy-start.7 = (bf16[8,256]{1,0:T(8,128)(2,1)S(1)}, bf16[8,256]{1,0:T(8,128)(2,1)}, u32[]{:S(2)}) copy-start(bf16[8,256]{1,0:T(8,128)(2,1)} %fresh_ref.1) | copy-start | bytes 12292
  21.9 13.1 %copy-start.9 = (s32[8]{0:T(128)S(1)}, s32[8]{0:T(128)}, u32[]{:S(2)}) copy-start(s32[8]{0:T(128)} %param.16) | copy-start | bytes 100
  34.9 11.7 %copy-start = (bf16[1024,1024]{1,0:T(8,128)(2,1)S(1)}, bf16[1024,1024]{1,0:T(8,128)(2,1)}, u32[]{:S(2)}) copy-start(bf16[1024,1024]{1,0:T(8,128)(2,1)} %wo_ref.1) | copy-start | bytes 6291460
  35.0 11.7 %copy-start.1 = (bf16[1024,512]{1,0:T(8,128)(2,1)S(1)}, bf16[1024,512]{1,0:T(8,128)(2,1)}, u32[]{:S(2)}) copy-start(bf16[1024,512]{1,0:T(8,128)(2,1)} %down_ref.1) | copy-start | bytes 3145732
  35.0 11.7 %copy-start.2 = (bf16[512,1024]{1,0:T(8,128)(2,1)S(1)}, bf16[512,1024]{1,0:T(8,128)(2,1)}, u32[]{:S(2)}) copy-start(bf16[512,1024]{1,0:T(8,128)(2,1)} %up_ref.1) | copy-start | bytes 3145732
  35.0 11.7 %copy-start.3 = (s32[64]{0:T(128)S(1)}, s32[64]{0:T(128)}, u32[]{:S(2)}) copy-start(s32[64]{0:T(128)} %param.17) | copy-start | bytes 772
  36.3 25.1 %copy-start.10 = (bf16[8,1024]{1,0:T(8,128)(2,1)S(1)}, bf16[8,1024]{1,0:T(8,128)(2,1)}, u32[]{:S(2)}) copy-start(bf16[8,1024]{1,0:T(8,128)(2,1)} %param.18) | copy-start | bytes 49156

commit v6 on v5

--- a/solution.py
+++ b/solution.py
@@ -17,12 +17,8 @@
 SCALE = 1.0 / math.sqrt(HEAD_DIM)
 NEVER = -1e30
 VMEM = pl.BlockSpec(memory_space=pltpu.VMEM)
-HBM = pl.BlockSpec(memory_space=pltpu.HBM)
 NT = (((1,), (1,)), ((), ()))
-
-
-def in_hbm(array):
-    return pltpu.with_memory_space_constraint(array, pltpu.HBM)
+AHEAD = pl.CostEstimate(flops=100_000_000_000, bytes_accessed=400_000_000, transcendentals=0)
 
 
 def down_rows(line):
@@ -40,14 +36,12 @@
         q_heads[:, head, :] = q[:, head * HEAD_DIM:(head + 1) * HEAD_DIM]
 
 
-def outgoing_kernel(pages_hbm, q_hbm, out_ref, pages_ref, q_ref, q_heads, rows, sems):
-    first = pltpu.make_async_copy(q_hbm, q_ref, sems.at[0])
-    second = pltpu.make_async_copy(pages_hbm, pages_ref, sems.at[1])
-    first.start()
-    second.start()
-    rows[...] = jnp.zeros_like(rows)
-    first.wait()
-    second.wait()
+def opening_kernel(out_ref):
+    out_ref[...] = jnp.zeros_like(out_ref)
+
+
+def outgoing_kernel(opening_ref, pages_ref, q_ref, out_ref, q_heads, rows):
+    rows[...] = opening_ref[...]
     heads_of(q_ref, q_heads)
     slots, peers = q_ref.shape[0], out_ref.shape[0]
     pages = pages_ref[...]
@@ -244,24 +238,27 @@
     heads = (slots, GROUP, HEAD_DIM)
     around = ("inst", "batch")
     params = pltpu.CompilerParams(vmem_limit_bytes=16 * 1024 * 1024)
+    opening = pl.pallas_call(
+        opening_kernel,
+        out_shape=jax.ShapeDtypeStruct((peers + 1, GROUP, HEAD_DIM), jnp.float32),
+        out_specs=VMEM,
+        compiler_params=params,
+        cost_estimate=AHEAD,
+        name="opening",
+    )()
     out_q = pl.pallas_call(
         outgoing_kernel,
         out_shape=jax.ShapeDtypeStruct((peers, GROUP, HEAD_DIM), jnp.bfloat16),
-        in_specs=[HBM, HBM],
+        in_specs=[VMEM] * 3,
         out_specs=VMEM,
         scratch_shapes=[
-            pltpu.VMEM(request_pages.shape, jnp.int32),
-            pltpu.VMEM(queries.shape, jnp.bfloat16),
             pltpu.VMEM(heads, jnp.float32),
             pltpu.VMEM((peers + 1, GROUP, HEAD_DIM), jnp.float32),
-            pltpu.SemaphoreType.DMA((2,)),
         ],
         compiler_params=params,
-        cost_estimate=pl.CostEstimate(
-            flops=100_000_000_000, bytes_accessed=400_000_000, transcendentals=0
-        ),
+        cost_estimate=AHEAD,
         name="outgoing",
-    )(in_hbm(request_pages), in_hbm(queries))
+    )(opening, request_pages, queries)
     in_q = lax.all_to_all(out_q, around, 0, 0, tiled=True)
     far = pl.pallas_call(
         far_kernel,
@@ -269,9 +266,7 @@
         in_specs=[VMEM, VMEM, VMEM],
         out_specs=VMEM,
         compiler_params=params,
-        cost_estimate=pl.CostEstimate(
-            flops=100_000_000_000, bytes_accessed=400_000_000, transcendentals=0
-        ),
+        cost_estimate=AHEAD,
         name="far",
     )(transfer_pages, in_q, key_value_pages)
     back = lax.all_to_all(far, around, 0, 0, tiled=True)
@@ -283,9 +278,7 @@
         out_specs=VMEM,
         scratch_shapes=[pltpu.VMEM(heads, jnp.float32), pltpu.VMEM(heads, jnp.float32)],
         compiler_params=params,
-        cost_estimate=pl.CostEstimate(
-            flops=100_000_000_000, bytes_accessed=400_000_000, transcendentals=0
-        ),
+        cost_estimate=AHEAD,
         name="join",
     )(
         request_pages,

time: 62.2 us -> 62.3 us (level)
  Pallas kernels: 3.91 us -> 3.04 us
  local copies, waits for them, and re-layouts: 0.06 us -> 0.76 us
    pallas_call x1, Pallas kernels: 1.02 us -> 0.14 us  [body(): pl.pallas_call(outgoing_kernel, out_shape=jax.ShapeDtypeStruct((peers, GR...]
    unnamed x22, local copies, waits for them, and re-layouts: 0.06 us -> 0.76 us
where the time goes in v6:
time: 62.3 us; the launch traced here: 61.9 us
  blocking collectives  57.4 us (92%)
  Pallas kernels  3.04 us (5%)
  local copies, waits for them, and re-layouts  0.76 us (1%)
  other arithmetic  0.64 us (1%)
    all_to_all x1, blocking collectives, body(): in_q = lax.all_to_all(out_q, around, 0, 0, tiled=True)  21 us
    all_to_all x1, blocking collectives, body(): lax.all_to_all(part.reshape(lax.axis_size('tensor'), -1, part.shape[1]),...  13.7 us
    all_to_all x1, blocking collectives, body(): back = lax.all_to_all(far, around, 0, 0, tiled=True)  12.3 us
    all_to_all x1, blocking collectives, body(): lax.all_to_all(copies, 'batch', 0, 0, tiled=True)  10.4 us
    pallas_call x1, Pallas kernels, body(): pl.pallas_call(join_kernel, out_shape=jax.ShapeDtypeStruct((group, slots,...  1.26 us

profile of v6, /device:TPU:1, one launch (start us, length us, event | category | flops | bytes accessed | tf_op | source)
XLA Modules:
  0.0 61.9 jit_solution(2911449820015850405)
XLA Ops:
  0.0 0.0 copy-start.6
  0.0 0.0 copy-start.5
  0.0 0.7 %copy-done.6 = s32[8,8]{1,0:T(8,128)S(1)} copy-done((s32[8,8]{1,0:T(8,128)S(1)}, s32[8,8]{1,0:T(8,128)}, u32[]{:S(2)}) %copy-start.6) | copy-done | bytes 280
  0.7 0.0 copy-done.5
  0.7 0.0 copy-start.4
  0.7 0.0 copy-start.8
  0.7 0.1 outgoing.1
  0.9 21.0 %all_to_all.20.q_ref = bf16[32,8,128]{2,1,0:T(8,128)(2,1)S(1)} all-to-all(bf16[32,8,128]{2,1,0:T(8,128)(2,1)S(1)} %outgoing.1), channel_id=1, replica_groups=mesh['inst'=4,'batch'=8,'tensor'=8] {'inst','batch'}, dimensions={0} | all-to-all | bytes 131072 | tf_op jit(solution)/shard_map/all_to_all | solution.py:262
  21.8 0.0 copy-done.4
  21.8 0.0 copy-done.8
  21.8 0.0 copy-start.7
  21.8 0.0 copy-start.9
  21.9 0.7 %far.1 = bf16[32,16,128]{2,1,0:T(8,128)(2,1)S(1)} custom-call(s32[1,32]{1,0:T(1,128)S(1)} %copy-done.8, bf16[32,8,128]{2,1,0:T(8,128)(2,1)S(1)} %all_to_all.20.q_ref, bf16[64,128,256]{2,1,0:T(8,128)(2,1)S(1)} %copy-done.4), custom_call_target="tpu_custom_call" | custom-call | flops 99999997952 | bytes 400000000 | tf_op jit(solution)/shard_map/far/pallas_call | solution.py:263
  22.6 12.3 %all_to_all.21.back_ref = bf16[32,16,128]{2,1,0:T(8,128)(2,1)S(1)} all-to-all(bf16[32,16,128]{2,1,0:T(8,128)(2,1)S(1)} %far.1), channel_id=1, replica_groups=mesh['inst'=4,'batch'=8,'tensor'=8] {'inst','batch'}, dimensions={0} | all-to-all | bytes 262144 | tf_op jit(solution)/shard_map/all_to_all | solution.py:272
  34.9 0.0 copy-done.7
  34.9 0.0 copy-done.9
  34.9 0.0 copy-start
  34.9 0.0 copy-start.1
  34.9 0.0 copy-start.2
  34.9 0.0 copy-start.3
  34.9 1.3 %join.1 = bf16[8,8,1024]{2,1,0:T(8,128)(2,1)S(1)} custom-call(s32[8,8]{1,0:T(8,128)S(1)} %copy-done.6, s32[1,8]{1,0:T(1,128)S(1)} %bitcast.7, bf16[8,1024]{1,0:T(8,128)(2,1)S(1)} %copy-done.5, bf16[8,256]{1,0:T(8,128)(2,1)S(1)} %copy-done.7, bf16[64,128,256]{2,1,0:T(8,128)(2,1)S(1)} %copy-done.4, bf16[32,16,128]{2,1,0:T(8,128)(2,1)S(1)} %all_to_all.21.back_ref), custom_call_target="tpu_custom_call" | custom-call | flops 99999997952 | bytes 400000000 | tf_op jit(solution)/shard_map/join/pallas_call | solution.py:274
  36.2 0.0 copy-start.10
  36.2 10.4 %all_to_all.22 = bf16[8,8,1024]{2,1,0:T(8,128)(2,1)S(1)} all-to-all(bf16[8,8,1024]{2,1,0:T(8,128)(2,1)S(1)} %join.1), channel_id=1, replica_groups=mesh['inst'=4,'batch'=8,'tensor'=8] {'batch'}, dimensions={0} | all-to-all | bytes 262144 | tf_op jit(solution)/shard_map/all_to_all | solution.py:291
  46.6 0.0 copy-done
  46.6 0.0 copy-done.1
  46.6 0.0 copy-done.2
  46.6 0.0 copy-done.3
  46.6 0.9 %project.1 = bf16[64,1024]{1,0:T(8,128)(2,1)S(1)} custom-call(bf16[64,1024]{1,0:T(8,128)(2,1)S(1)} %bitcast.4, s32[1,64]{1,0:T(1,128)S(1)} %bitcast.6, bf16[1024,1024]{1,0:T(8,128)(2,1)S(1)} %copy-done, bf16[1024,512]{1,0:T(8,128)(2,1)S(1)} %copy-done.1, bf16[512,1024]{1,0:T(8,128)(2,1)S(1)} %copy-done.2), custom_call_target="tpu_custom_call" | custom-call | tf_op jit(solution)/shard_map/project/pallas_call | solution.py:292
  47.5 13.7 %all_to_all.23 = bf16[8,8,1024]{2,1,0:T(8,128)(2,1)S(1)} all-to-all(bf16[8,8,1024]{2,1,0:T(8,128)(2,1)S(1)} %bitcast.5), channel_id=1, replica_groups=mesh['inst'=4,'batch'=8,'tensor'=8] {'tensor'}, dimensions={0} | all-to-all | bytes 262144 | tf_op jit(solution)/shard_map/all_to_all | solution.py:300
  61.3 0.0 copy-done.10
  61.3 0.6 add_convert_fusion
  (2 shorter events, 0.0 us)
Async XLA Ops:
  0.0 0.7 %copy-start.6 = (s32[8,8]{1,0:T(8,128)S(1)}, s32[8,8]{1,0:T(8,128)}, u32[]{:S(2)}) copy-start(s32[8,8]{1,0:T(8,128)} %pages_ref.3) | copy-start | bytes 772
  0.0 0.7 %copy-start.5 = (bf16[8,1024]{1,0:T(8,128)(2,1)S(1)}, bf16[8,1024]{1,0:T(8,128)(2,1)}, u32[]{:S(2)}) copy-start(bf16[8,1024]{1,0:T(8,128)(2,1)} %q_ref.3) | copy-start | bytes 49156
  0.7 21.1 %copy-start.4 = (bf16[64,128,256]{2,1,0:T(8,128)(2,1)S(1)}, bf16[64,128,256]{2,1,0:T(8,128)(2,1)}, u32[]{:S(2)}) copy-start(bf16[64,128,256]{2,1,0:T(8,128)(2,1)} %pool_ref.3) | copy-start | bytes 12582916
  0.7 21.1 %copy-start.8 = (s32[1,32]{1,0:T(1,128)S(1)}, s32[1,32]{1,0:T(1,128)}, u32[]{:S(2)}) copy-start(s32[1,32]{1,0:T(1,128)} %listed_ref.1) | copy-start | bytes 388
  21.8 13.0 %copy-start.7 = (bf16[8,256]{1,0:T(8,128)(2,1)S(1)}, bf16[8,256]{1,0:T(8,128)(2,1)}, u32[]{:S(2)}) copy-start(bf16[8,256]{1,0:T(8,128)(2,1)} %fresh_ref.1) | copy-start | bytes 12292
  21.8 13.0 %copy-start.9 = (s32[8]{0:T(128)S(1)}, s32[8]{0:T(128)}, u32[]{:S(2)}) copy-start(s32[8]{0:T(128)} %param.16) | copy-start | bytes 100
  34.9 11.7 %copy-start = (bf16[1024,1024]{1,0:T(8,128)(2,1)S(1)}, bf16[1024,1024]{1,0:T(8,128)(2,1)}, u32[]{:S(2)}) copy-start(bf16[1024,1024]{1,0:T(8,128)(2,1)} %wo_ref.1) | copy-start | bytes 6291460
  34.9 11.7 %copy-start.1 = (bf16[1024,512]{1,0:T(8,128)(2,1)S(1)}, bf16[1024,512]{1,0:T(8,128)(2,1)}, u32[]{:S(2)}) copy-start(bf16[1024,512]{1,0:T(8,128)(2,1)} %down_ref.1) | copy-start | bytes 3145732
  34.9 11.7 %copy-start.2 = (bf16[512,1024]{1,0:T(8,128)(2,1)S(1)}, bf16[512,1024]{1,0:T(8,128)(2,1)}, u32[]{:S(2)}) copy-start(bf16[512,1024]{1,0:T(8,128)(2,1)} %up_ref.1) | copy-start | bytes 3145732
  34.9 11.7 %copy-start.3 = (s32[64]{0:T(128)S(1)}, s32[64]{0:T(128)}, u32[]{:S(2)}) copy-start(s32[64]{0:T(128)} %param.17) | copy-start | bytes 772
  36.2 25.1 %copy-start.10 = (bf16[8,1024]{1,0:T(8,128)(2,1)S(1)}, bf16[8,1024]{1,0:T(8,128)(2,1)}, u32[]{:S(2)}) copy-start(bf16[8,1024]{1,0:T(8,128)(2,1)} %param.18) | copy-start | bytes 49156

commit v7 on v6

--- a/solution.py
+++ b/solution.py
@@ -11,8 +11,6 @@
 GROUP = 8
 ADAPTER_RANK = 64
 FAR_POSITIONS = 4
-FAR_BLOCK = 32
-NEAR_BLOCK = 8
 POOL = 64
 SCALE = 1.0 / math.sqrt(HEAD_DIM)
 NEVER = -1e30
@@ -52,121 +50,118 @@
     out_ref[...] = rows[:peers].astype(jnp.bfloat16)
 
 
-def far_kernel(listed_ref, q_ref, pool_ref, out_ref):
-    peers = q_ref.shape[0]
+def attend_kernel(
+    listed_ref, in_q_ref, pool_ref, pages_ref, lengths_ref, q_ref, fresh_ref,
+    far_ref, near_ref, top_ref, total_ref, q_heads,
+):
+    peers = range(in_q_ref.shape[0])
+    slots = range(pages_ref.shape[0])
+    places = range(pages_ref.shape[1])
     page_len = pool_ref.shape[1]
-    lane = lax.broadcasted_iota(jnp.int32, (GROUP, HEAD_DIM), 1)
+    lane = lax.broadcasted_iota(jnp.int32, (GROUP, page_len), 1)
     none = jnp.zeros((GROUP, page_len), jnp.bfloat16)
     listed = jnp.maximum(listed_ref[...], 0)
-    for first in range(0, peers, FAR_BLOCK):
-        block = range(first, first + FAR_BLOCK)
-        pages = [listed[0, peer] for peer in block]
-        scores = []
-        for at in range(0, FAR_BLOCK, 2):
-            peer = first + at
-            keys = jnp.concatenate(
-                [pool_ref[pages[at], :, :HEAD_DIM], pool_ref[pages[at + 1], :, :HEAD_DIM]], 0
-            )
-            both = jnp.concatenate([q_ref[peer], q_ref[peer + 1]], 0)
-            score = SCALE * lax.dot_general(both, keys, NT, preferred_element_type=jnp.float32)
-            scores += [score[:GROUP, :page_len], score[GROUP:, page_len:]]
-        tops = [
-            jnp.max(score, axis=1, keepdims=True).astype(jnp.bfloat16).astype(jnp.float32)
-            for score in scores
-        ]
-        probs = [jnp.exp(score - top).astype(jnp.bfloat16) for score, top in zip(scores, tops)]
-        totals = [jnp.sum(prob.astype(jnp.float32), axis=1, keepdims=True) for prob in probs]
-        outs = []
-        for at in range(0, FAR_BLOCK, 2):
-            values = jnp.concatenate(
-                [pool_ref[pages[at], :, HEAD_DIM:], pool_ref[pages[at + 1], :, HEAD_DIM:]], 0
-            )
-            both = jnp.concatenate(
-                [
-                    jnp.concatenate([probs[at], none], 1),
-                    jnp.concatenate([none, probs[at + 1]], 1),
-                ],
-                0,
-            )
-            out = jnp.dot(both, values, preferred_element_type=jnp.float32)
-            outs += [out[:GROUP], out[GROUP:]]
-        for peer, out, top, total in zip(block, outs, tops, totals):
-            high = total.astype(jnp.bfloat16).astype(jnp.float32)
-            stats = jnp.where(lane == 0, top, jnp.where(lane == 1, high, total - high))
-            out_ref[peer] = jnp.concatenate([out / total, stats], 0).astype(jnp.bfloat16)
-
-
-def near_parts(pages_ref, lengths_ref, q_ref, fresh_ref, pool_ref, q_heads):
-    slots, places = pages_ref.shape
-    page_len = pool_ref.shape[1]
+    listed = [listed[0, peer] for peer in peers]
     pages = pages_ref[...]
     before = page_len * lax.broadcasted_iota(jnp.int32, pages.shape, 1)
     limits = jnp.where(pages < POOL, down_rows(lengths_ref[...]) - before, 0)
     pages = jnp.where(pages < POOL, pages, 0)
+    index = [[pages[slot, place] for place in places] for slot in slots]
     heads_of(q_ref, q_heads)
     fresh = fresh_ref[...].astype(jnp.float32)
-    lane = lax.broadcasted_iota(jnp.int32, (GROUP, page_len), 1)
-    near_tops, near_totals, near_outs = [], [], []
-    for first in range(0, slots, NEAR_BLOCK):
-        block = range(first, first + NEAR_BLOCK)
-        index = {}
-        scores = {}
-        for slot in block:
-            for place in range(places):
-                index[slot, place] = pages[slot, place]
-            keys = [pool_ref[index[slot, place], :, :HEAD_DIM] for place in range(places)]
-            score = SCALE * lax.dot_general(
-                q_heads[slot].astype(jnp.bfloat16),
-                jnp.concatenate(keys, 0),
-                NT,
-                preferred_element_type=jnp.float32,
-            )
-            scores[slot] = [
+
+    far_scores, near_scores = [], []
+    for peer in peers[::2]:
+        keys = [pool_ref[listed[at], :, :HEAD_DIM] for at in (peer, peer + 1)]
+        both = jnp.concatenate([in_q_ref[peer], in_q_ref[peer + 1]], 0)
+        score = SCALE * lax.dot_general(
+            both, jnp.concatenate(keys, 0), NT, preferred_element_type=jnp.float32
+        )
+        far_scores += [score[:GROUP, :page_len], score[GROUP:, page_len:]]
+    for slot in slots:
+        keys = [pool_ref[index[slot][place], :, :HEAD_DIM] for place in places]
+        score = SCALE * lax.dot_general(
+            q_heads[slot].astype(jnp.bfloat16),
+            jnp.concatenate(keys, 0),
+            NT,
+            preferred_element_type=jnp.float32,
+        )
+        near_scores.append(
+            [
                 jnp.where(
                     lane < limits[slot:slot + 1, at:at + 1],
                     score[:, at * page_len:(at + 1) * page_len],
                     NEVER,
                 )
-                for at in range(places)
+                for at in places
             ]
-        owns = [
-            SCALE
-            * jnp.sum(q_heads[slot] * fresh[slot:slot + 1, :HEAD_DIM], axis=1, keepdims=True)
-            for slot in block
-        ]
-        tops = []
-        for slot, own in zip(block, owns):
-            top = scores[slot][0]
-            for score in scores[slot][1:]:
-                top = jnp.maximum(top, score)
-            tops.append(jnp.maximum(jnp.max(top, axis=1, keepdims=True), own))
-        weights = [jnp.exp(own - top) for own, top in zip(owns, tops)]
-        for slot, top, weight in zip(block, tops, weights):
-            probs = [jnp.exp(score - top).astype(jnp.bfloat16) for score in scores[slot]]
-            summed = probs[0].astype(jnp.float32)
-            for prob in probs[1:]:
-                summed = summed + prob.astype(jnp.float32)
-            values = [pool_ref[index[slot, place], :, HEAD_DIM:] for place in range(places)]
-            out = jnp.dot(
-                jnp.concatenate(probs, 1),
-                jnp.concatenate(values, 0),
-                preferred_element_type=jnp.float32,
-            )
-            total = jnp.sum(summed, axis=1, keepdims=True) + weight
-            near_tops.append(top)
-            near_totals.append(total)
-            near_outs.append(out + weight * fresh[slot:slot + 1, HEAD_DIM:])
-    return near_tops, near_totals, near_outs
-
-
-def join_kernel(
-    pages_ref, lengths_ref, q_ref, fresh_ref, pool_ref, back_ref, rows_ref, q_heads, heads
-):
-    near_tops, near_totals, near_outs = near_parts(
-        pages_ref, lengths_ref, q_ref, fresh_ref, pool_ref, q_heads
-    )
+        )
+
+    far_tops = [
+        jnp.max(score, axis=1, keepdims=True).astype(jnp.bfloat16).astype(jnp.float32)
+        for score in far_scores
+    ]
+    owns = [
+        SCALE * jnp.sum(q_heads[slot] * fresh[slot:slot + 1, :HEAD_DIM], axis=1, keepdims=True)
+        for slot in slots
+    ]
+    near_tops = []
+    for slot in slots:
+        top = near_scores[slot][0]
+        for score in near_scores[slot][1:]:
+            top = jnp.maximum(top, score)
+        near_tops.append(jnp.maximum(jnp.max(top, axis=1, keepdims=True), owns[slot]))
+    far_probs = [
+        jnp.exp(score - top).astype(jnp.bfloat16) for score, top in zip(far_scores, far_tops)
+    ]
+    far_totals = [
+        jnp.sum(prob.astype(jnp.float32), axis=1, keepdims=True) for prob in far_probs
+    ]
+    near_probs = [
+        [jnp.exp(score - top).astype(jnp.bfloat16) for score in row]
+        for row, top in zip(near_scores, near_tops)
+    ]
+    weights = [jnp.exp(own - top) for own, top in zip(owns, near_tops)]
+
+    far_outs = []
+    for peer in peers[::2]:
+        values = [pool_ref[listed[at], :, HEAD_DIM:] for at in (peer, peer + 1)]
+        both = jnp.concatenate(
+            [
+                jnp.concatenate([far_probs[peer], none], 1),
+                jnp.concatenate([none, far_probs[peer + 1]], 1),
+            ],
+            0,
+        )
+        out = jnp.dot(both, jnp.concatenate(values, 0), preferred_element_type=jnp.float32)
+        far_outs += [out[:GROUP], out[GROUP:]]
+    for slot in slots:
+        values = [pool_ref[index[slot][place], :, HEAD_DIM:] for place in places]
+        out = jnp.dot(
+            jnp.concatenate(near_probs[slot], 1),
+            jnp.concatenate(values, 0),
+            preferred_element_type=jnp.float32,
+        )
+        summed = near_probs[slot][0].astype(jnp.float32)
+        for prob in near_probs[slot][1:]:
+            summed = summed + prob.astype(jnp.float32)
+        total = jnp.sum(summed, axis=1, keepdims=True) + weights[slot]
+        near_ref[slot] = out + weights[slot] * fresh[slot:slot + 1, HEAD_DIM:]
+        top_ref[slot] = jnp.broadcast_to(near_tops[slot], out.shape)
+        total_ref[slot] = jnp.broadcast_to(total, out.shape)
+    for peer in peers:
+        total = far_totals[peer]
+        high = total.astype(jnp.bfloat16).astype(jnp.float32)
+        stats = jnp.where(lane == 0, far_tops[peer], jnp.where(lane == 1, high, total - high))
+        far_ref[peer] = jnp.concatenate([far_outs[peer] / total, stats], 0).astype(jnp.bfloat16)
+
+
+def join_kernel(pages_ref, near_ref, top_ref, total_ref, back_ref, rows_ref, heads):
     slots = range(pages_ref.shape[0])
     places = range(FAR_POSITIONS)
+    near_tops = [top_ref[slot] for slot in slots]
+    near_totals = [total_ref[slot] for slot in slots]
+    near_outs = [near_ref[slot] for slot in slots]
     pages = pages_ref[...]
     senders = jnp.maximum(pages - POOL, 0)
     parts = [
@@ -260,34 +255,37 @@
         name="outgoing",
     )(opening, request_pages, queries)
     in_q = lax.all_to_all(out_q, around, 0, 0, tiled=True)
-    far = pl.pallas_call(
-        far_kernel,
-        out_shape=jax.ShapeDtypeStruct((peers, 2 * GROUP, HEAD_DIM), jnp.bfloat16),
-        in_specs=[VMEM, VMEM, VMEM],
-        out_specs=VMEM,
+    far, near_out, near_top, near_total = pl.pallas_call(
+        attend_kernel,
+        out_shape=[jax.ShapeDtypeStruct((peers, 2 * GROUP, HEAD_DIM), jnp.bfloat16)]
+        + [jax.ShapeDtypeStruct(heads, jnp.float32)] * 3,
+        in_specs=[VMEM] * 7,
+        out_specs=[VMEM] * 4,
+        scratch_shapes=[pltpu.VMEM(heads, jnp.float32)],
         compiler_params=params,
         cost_estimate=AHEAD,
-        name="far",
-    )(transfer_pages, in_q, key_value_pages)
+        name="attend",
+    )(
+        transfer_pages,
+        in_q,
+        key_value_pages,
+        request_pages,
+        lengths[None],
+        queries,
+        current_key_value,
+    )
     back = lax.all_to_all(far, around, 0, 0, tiled=True)
     group = lax.axis_size("batch")
     copies = pl.pallas_call(
         join_kernel,
         out_shape=jax.ShapeDtypeStruct((group, slots, GROUP * HEAD_DIM), jnp.bfloat16),
-        in_specs=[VMEM] * 6,
+        in_specs=[VMEM] * 5,
         out_specs=VMEM,
-        scratch_shapes=[pltpu.VMEM(heads, jnp.float32), pltpu.VMEM(heads, jnp.float32)],
+        scratch_shapes=[pltpu.VMEM(heads, jnp.float32)],
         compiler_params=params,
         cost_estimate=AHEAD,
         name="join",
-    )(
-        request_pages,
-        lengths[None],
-        queries,
-        current_key_value,
-        key_value_pages,
-        back,
-    )
+    )(request_pages, near_out, near_top, near_total, back)
     rows = lax.all_to_all(copies, "batch", 0, 0, tiled=True).reshape(-1, GROUP * HEAD_DIM)
     part = pl.pallas_call(
         project_kernel,

time: 62.3 us -> 62.4 us (level)
    pallas_call x1, Pallas kernels: 1.26 us -> 0.38 us  [body(): pl.pallas_call(join_kernel, out_shape=jax.ShapeDtypeStruct((group, slots,...]
    pallas_call x1, Pallas kernels: 0.73 us -> 1.46 us  [body(): pl.pallas_call(attend_kernel, out_shape=[jax.ShapeDtypeStruct((peers, 2 *...]
where the time goes in v7:
time: 62.4 us; the launch traced here: 62 us
  blocking collectives  57.7 us (92%)
  Pallas kernels  2.89 us (5%)
  local copies, waits for them, and re-layouts  0.75 us (1%)
  other arithmetic  0.63 us (1%)
    all_to_all x1, blocking collectives, body(): in_q = lax.all_to_all(out_q, around, 0, 0, tiled=True)  21 us
    all_to_all x1, blocking collectives, body(): lax.all_to_all(part.reshape(lax.axis_size('tensor'), -1, part.shape[1]),...  13.7 us
    all_to_all x1, blocking collectives, body(): back = lax.all_to_all(far, around, 0, 0, tiled=True)  12.3 us
    all_to_all x1, blocking collectives, body(): lax.all_to_all(copies, 'batch', 0, 0, tiled=True)  10.7 us
    pallas_call x1, Pallas kernels, body(): pl.pallas_call(attend_kernel, out_shape=[jax.ShapeDtypeStruct((peers, 2 *...  1.46 us

profile of v7, /device:TPU:1, one launch (start us, length us, event | category | flops | bytes accessed | tf_op | source)
XLA Modules:
  0.0 62.0 jit_solution(17571559345654551832)
XLA Ops:
  0.0 0.0 copy-start.7
  0.0 0.0 copy-start.5
  0.0 0.7 %copy-done.7 = s32[8,8]{1,0:T(8,128)S(1)} copy-done((s32[8,8]{1,0:T(8,128)S(1)}, s32[8,8]{1,0:T(8,128)}, u32[]{:S(2)}) %copy-start.7) | copy-done | bytes 280
  0.7 0.0 copy-done.5
  0.7 0.0 copy-start.4
  0.7 0.0 copy-start.6
  0.7 0.0 copy-start.8
  0.7 0.0 copy-start.9
  0.7 0.1 outgoing.1
  0.9 21.0 %all_to_all.20.in_q_ref = bf16[32,8,128]{2,1,0:T(8,128)(2,1)S(1)} all-to-all(bf16[32,8,128]{2,1,0:T(8,128)(2,1)S(1)} %outgoing.1), channel_id=1, replica_groups=mesh['inst'=4,'batch'=8,'tensor'=8] {'inst','batch'}, dimensions={0} | all-to-all | bytes 131072 | tf_op jit(solution)/shard_map/all_to_all | solution.py:257
  21.9 0.0 copy-done.4
  21.9 0.0 copy-done.6
  21.9 0.0 copy-done.8
  21.9 0.0 copy-done.9
  21.9 1.5 %attend.1 = (bf16[32,16,128]{2,1,0:T(8,128)(2,1)S(1)}, f32[8,8,128]{2,1,0:T(8,128)S(1)}, f32[8,8,128]{2,1,0:T(8,128)S(1)}, f32[8,8,128]{2,1,0:T(8,128)S(1)}) custom-call(s32[1,32]{1,0:T(1,128)S(1)} %copy-done.8, bf16[32,8,128]{2,1,0:T(8,128)(2,1)S(1)} %all_to_all.20.in_q_ref, bf16[64,128,256]{2,1,0:T(8,128)(2,1)S(1)} %copy-done.4, s32[8,8]{1,0:T(8,128)S(1)} %copy-done.7, ...), custom_call_target="tpu_custom_call" | custom-call | flops 99999997952 | bytes 400000000 | tf_op jit(solution)/shard_map/attend/pallas_call | solution.py:258
  23.3 12.3 %all_to_all.21.back_ref = bf16[32,16,128]{2,1,0:T(8,128)(2,1)S(1)} all-to-all(bf16[32,16,128]{2,1,0:T(8,128)(2,1)S(1)} %get-tuple-element.12), channel_id=1, replica_groups=mesh['inst'=4,'batch'=8,'tensor'=8] {'inst','batch'}, dimensions={0} | all-to-all | bytes 262144 | tf_op jit(solution)/shard_map/all_to_all | solution.py:277
  35.6 0.0 copy-start
  35.6 0.0 copy-start.1
  35.6 0.0 copy-start.2
  35.7 0.0 copy-start.3
  35.7 0.4 join.1
  36.0 0.0 copy-start.10
  36.1 10.7 %all_to_all.22 = bf16[8,8,1024]{2,1,0:T(8,128)(2,1)S(1)} all-to-all(bf16[8,8,1024]{2,1,0:T(8,128)(2,1)S(1)} %join.1), channel_id=1, replica_groups=mesh['inst'=4,'batch'=8,'tensor'=8] {'batch'}, dimensions={0} | all-to-all | bytes 262144 | tf_op jit(solution)/shard_map/all_to_all | solution.py:289
  46.7 0.0 copy-done
  46.7 0.0 copy-done.1
  46.7 0.0 copy-done.2
  46.7 0.0 copy-done.3
  46.8 0.9 %project.1 = bf16[64,1024]{1,0:T(8,128)(2,1)S(1)} custom-call(bf16[64,1024]{1,0:T(8,128)(2,1)S(1)} %bitcast.4, s32[1,64]{1,0:T(1,128)S(1)} %bitcast.6, bf16[1024,1024]{1,0:T(8,128)(2,1)S(1)} %copy-done, bf16[1024,512]{1,0:T(8,128)(2,1)S(1)} %copy-done.1, bf16[512,1024]{1,0:T(8,128)(2,1)S(1)} %copy-done.2), custom_call_target="tpu_custom_call" | custom-call | tf_op jit(solution)/shard_map/project/pallas_call | solution.py:290
  47.7 13.7 %all_to_all.23 = bf16[8,8,1024]{2,1,0:T(8,128)(2,1)S(1)} all-to-all(bf16[8,8,1024]{2,1,0:T(8,128)(2,1)S(1)} %bitcast.5), channel_id=1, replica_groups=mesh['inst'=4,'batch'=8,'tensor'=8] {'tensor'}, dimensions={0} | all-to-all | bytes 262144 | tf_op jit(solution)/shard_map/all_to_all | solution.py:298
  61.4 0.0 copy-done.10
  61.4 0.6 add_convert_fusion
  (2 shorter events, 0.0 us)
Async XLA Ops:
  0.0 0.7 %copy-start.7 = (s32[8,8]{1,0:T(8,128)S(1)}, s32[8,8]{1,0:T(8,128)}, u32[]{:S(2)}) copy-start(s32[8,8]{1,0:T(8,128)} %pages_ref.5) | copy-start | bytes 772
  0.0 0.7 %copy-start.5 = (bf16[8,1024]{1,0:T(8,128)(2,1)S(1)}, bf16[8,1024]{1,0:T(8,128)(2,1)}, u32[]{:S(2)}) copy-start(bf16[8,1024]{1,0:T(8,128)(2,1)} %q_ref.3) | copy-start | bytes 49156
  0.7 21.1 %copy-start.4 = (bf16[64,128,256]{2,1,0:T(8,128)(2,1)S(1)}, bf16[64,128,256]{2,1,0:T(8,128)(2,1)}, u32[]{:S(2)}) copy-start(bf16[64,128,256]{2,1,0:T(8,128)(2,1)} %pool_ref.1) | copy-start | bytes 12582916
  0.7 21.1 %copy-start.6 = (bf16[8,256]{1,0:T(8,128)(2,1)S(1)}, bf16[8,256]{1,0:T(8,128)(2,1)}, u32[]{:S(2)}) copy-start(bf16[8,256]{1,0:T(8,128)(2,1)} %fresh_ref.1) | copy-start | bytes 12292
  0.7 21.1 %copy-start.8 = (s32[1,32]{1,0:T(1,128)S(1)}, s32[1,32]{1,0:T(1,128)}, u32[]{:S(2)}) copy-start(s32[1,32]{1,0:T(1,128)} %listed_ref.1) | copy-start | bytes 388
  0.7 21.1 %copy-start.9 = (s32[8]{0:T(128)S(1)}, s32[8]{0:T(128)}, u32[]{:S(2)}) copy-start(s32[8]{0:T(128)} %param.16) | copy-start | bytes 100
  35.6 11.1 %copy-start = (bf16[1024,1024]{1,0:T(8,128)(2,1)S(1)}, bf16[1024,1024]{1,0:T(8,128)(2,1)}, u32[]{:S(2)}) copy-start(bf16[1024,1024]{1,0:T(8,128)(2,1)} %wo_ref.1) | copy-start | bytes 6291460
  35.6 11.1 %copy-start.1 = (bf16[1024,512]{1,0:T(8,128)(2,1)S(1)}, bf16[1024,512]{1,0:T(8,128)(2,1)}, u32[]{:S(2)}) copy-start(bf16[1024,512]{1,0:T(8,128)(2,1)} %down_ref.1) | copy-start | bytes 3145732
  35.6 11.1 %copy-start.2 = (bf16[512,1024]{1,0:T(8,128)(2,1)S(1)}, bf16[512,1024]{1,0:T(8,128)(2,1)}, u32[]{:S(2)}) copy-start(bf16[512,1024]{1,0:T(8,128)(2,1)} %up_ref.1) | copy-start | bytes 3145732
  35.7 11.1 %copy-start.3 = (s32[64]{0:T(128)S(1)}, s32[64]{0:T(128)}, u32[]{:S(2)}) copy-start(s32[64]{0:T(128)} %param.17) | copy-start | bytes 772
  36.0 25.4 %copy-start.10 = (bf16[8,1024]{1,0:T(8,128)(2,1)S(1)}, bf16[8,1024]{1,0:T(8,128)(2,1)}, u32[]{:S(2)}) copy-start(bf16[8,1024]{1,0:T(8,128)(2,1)} %param.18) | copy-start | bytes 49156

commit v8 on v7

--- a/solution.py
+++ b/solution.py
@@ -16,6 +16,7 @@
 NEVER = -1e30
 VMEM = pl.BlockSpec(memory_space=pltpu.VMEM)
 NT = (((1,), (1,)), ((), ()))
+NOTHING = pl.CostEstimate(flops=0, bytes_accessed=0, transcendentals=0)
 AHEAD = pl.CostEstimate(flops=100_000_000_000, bytes_accessed=400_000_000, transcendentals=0)
 
 
@@ -283,7 +284,7 @@
         out_specs=VMEM,
         scratch_shapes=[pltpu.VMEM(heads, jnp.float32)],
         compiler_params=params,
-        cost_estimate=AHEAD,
+        cost_estimate=NOTHING,
         name="join",
     )(request_pages, near_out, near_top, near_total, back)
     rows = lax.all_to_all(copies, "batch", 0, 0, tiled=True).reshape(-1, GROUP * HEAD_DIM)

time: 62.4 us -> 62.3 us (level)
  no operation moved by 1% of the time
where the time goes in v8:
time: 62.3 us; the launch traced here: 62 us
  blocking collectives  57.5 us (92%)
  Pallas kernels  2.92 us (5%)
  local copies, waits for them, and re-layouts  0.76 us (1%)
  other arithmetic  0.63 us (1%)
    all_to_all x1, blocking collectives, body(): in_q = lax.all_to_all(out_q, around, 0, 0, tiled=True)  21 us
    all_to_all x1, blocking collectives, body(): lax.all_to_all(part.reshape(lax.axis_size('tensor'), -1, part.shape[1]),...  13.7 us
    all_to_all x1, blocking collectives, body(): back = lax.all_to_all(far, around, 0, 0, tiled=True)  12.4 us
    all_to_all x1, blocking collectives, body(): lax.all_to_all(copies, 'batch', 0, 0, tiled=True)  10.4 us
    pallas_call x1, Pallas kernels, body(): pl.pallas_call(attend_kernel, out_shape=[jax.ShapeDtypeStruct((peers, 2 *...  1.5 us

profile of v8, /device:TPU:1, one launch (start us, length us, event | category | flops | bytes accessed | tf_op | source)
XLA Modules:
  0.0 62.0 jit_solution(4419599352316206260)
XLA Ops:
  0.0 0.0 copy-start.3
  0.0 0.0 copy-start.6
  0.0 0.7 %copy-done.3 = s32[8,8]{1,0:T(8,128)S(1)} copy-done((s32[8,8]{1,0:T(8,128)S(1)}, s32[8,8]{1,0:T(8,128)}, u32[]{:S(2)}) %copy-start.3) | copy-done | bytes 280
  0.7 0.0 copy-done.6
  0.7 0.0 copy-start.5
  0.7 0.0 copy-start.7
  0.7 0.0 copy-start.8
  0.7 0.0 copy-start.9
  0.7 0.1 outgoing.1
  0.9 21.0 %all_to_all.20.in_q_ref = bf16[32,8,128]{2,1,0:T(8,128)(2,1)S(1)} all-to-all(bf16[32,8,128]{2,1,0:T(8,128)(2,1)S(1)} %outgoing.1), channel_id=1, replica_groups=mesh['inst'=4,'batch'=8,'tensor'=8] {'inst','batch'}, dimensions={0} | all-to-all | bytes 131072 | tf_op jit(solution)/shard_map/all_to_all | solution.py:258
  21.9 0.0 copy-done.5
  21.9 0.0 copy-done.7
  21.9 0.0 copy-done.8
  21.9 0.0 copy-done.9
  21.9 0.0 copy-start
  21.9 0.0 copy-start.1
  21.9 0.0 copy-start.2
  21.9 0.0 copy-start.4
  21.9 1.5 %attend.1 = (bf16[32,16,128]{2,1,0:T(8,128)(2,1)S(1)}, f32[8,8,128]{2,1,0:T(8,128)S(1)}, f32[8,8,128]{2,1,0:T(8,128)S(1)}, f32[8,8,128]{2,1,0:T(8,128)S(1)}) custom-call(s32[1,32]{1,0:T(1,128)S(1)} %copy-done.8, bf16[32,8,128]{2,1,0:T(8,128)(2,1)S(1)} %all_to_all.20.in_q_ref, bf16[64,128,256]{2,1,0:T(8,128)(2,1)S(1)} %copy-done.5, s32[8,8]{1,0:T(8,128)S(1)} %copy-done.3, ...), custom_call_target="tpu_custom_call" | custom-call | flops 99999997952 | bytes 400000000 | tf_op jit(solution)/shard_map/attend/pallas_call | solution.py:259
  23.4 0.0 copy-start.10
  23.4 12.4 %all_to_all.21.back_ref = bf16[32,16,128]{2,1,0:T(8,128)(2,1)S(1)} all-to-all(bf16[32,16,128]{2,1,0:T(8,128)(2,1)S(1)} %get-tuple-element.12), channel_id=1, replica_groups=mesh['inst'=4,'batch'=8,'tensor'=8] {'inst','batch'}, dimensions={0} | all-to-all | bytes 262144 | tf_op jit(solution)/shard_map/all_to_all | solution.py:278
  35.9 0.4 join.1
  36.3 10.4 %all_to_all.22 = bf16[8,8,1024]{2,1,0:T(8,128)(2,1)S(1)} all-to-all(bf16[8,8,1024]{2,1,0:T(8,128)(2,1)S(1)} %join.1), channel_id=1, replica_groups=mesh['inst'=4,'batch'=8,'tensor'=8] {'batch'}, dimensions={0} | all-to-all | bytes 262144 | tf_op jit(solution)/shard_map/all_to_all | solution.py:290
  46.7 0.0 copy-done
  46.7 0.0 copy-done.1
  46.7 0.0 copy-done.2
  46.7 0.0 copy-done.4
  46.7 0.9 %project.1 = bf16[64,1024]{1,0:T(8,128)(2,1)S(1)} custom-call(bf16[64,1024]{1,0:T(8,128)(2,1)S(1)} %bitcast.4, s32[1,64]{1,0:T(1,128)S(1)} %bitcast.6, bf16[1024,1024]{1,0:T(8,128)(2,1)S(1)} %copy-done, bf16[1024,512]{1,0:T(8,128)(2,1)S(1)} %copy-done.1, bf16[512,1024]{1,0:T(8,128)(2,1)S(1)} %copy-done.2), custom_call_target="tpu_custom_call" | custom-call | tf_op jit(solution)/shard_map/project/pallas_call | solution.py:291
  47.6 13.7 %all_to_all.23 = bf16[8,8,1024]{2,1,0:T(8,128)(2,1)S(1)} all-to-all(bf16[8,8,1024]{2,1,0:T(8,128)(2,1)S(1)} %bitcast.5), channel_id=1, replica_groups=mesh['inst'=4,'batch'=8,'tensor'=8] {'tensor'}, dimensions={0} | all-to-all | bytes 262144 | tf_op jit(solution)/shard_map/all_to_all | solution.py:299
  61.3 0.0 copy-done.10
  61.3 0.6 add_convert_fusion
  (2 shorter events, 0.0 us)
Async XLA Ops:
  0.0 0.7 %copy-start.3 = (s32[8,8]{1,0:T(8,128)S(1)}, s32[8,8]{1,0:T(8,128)}, u32[]{:S(2)}) copy-start(s32[8,8]{1,0:T(8,128)} %pages_ref.5) | copy-start | bytes 772
  0.0 0.7 %copy-start.6 = (bf16[8,1024]{1,0:T(8,128)(2,1)S(1)}, bf16[8,1024]{1,0:T(8,128)(2,1)}, u32[]{:S(2)}) copy-start(bf16[8,1024]{1,0:T(8,128)(2,1)} %q_ref.3) | copy-start | bytes 49156
  0.7 21.1 %copy-start.5 = (bf16[64,128,256]{2,1,0:T(8,128)(2,1)S(1)}, bf16[64,128,256]{2,1,0:T(8,128)(2,1)}, u32[]{:S(2)}) copy-start(bf16[64,128,256]{2,1,0:T(8,128)(2,1)} %pool_ref.1) | copy-start | bytes 12582916
  0.7 21.1 %copy-start.7 = (bf16[8,256]{1,0:T(8,128)(2,1)S(1)}, bf16[8,256]{1,0:T(8,128)(2,1)}, u32[]{:S(2)}) copy-start(bf16[8,256]{1,0:T(8,128)(2,1)} %fresh_ref.1) | copy-start | bytes 12292
  0.7 21.1 %copy-start.8 = (s32[1,32]{1,0:T(1,128)S(1)}, s32[1,32]{1,0:T(1,128)}, u32[]{:S(2)}) copy-start(s32[1,32]{1,0:T(1,128)} %listed_ref.1) | copy-start | bytes 388
  0.7 21.1 %copy-start.9 = (s32[8]{0:T(128)S(1)}, s32[8]{0:T(128)}, u32[]{:S(2)}) copy-start(s32[8]{0:T(128)} %param.16) | copy-start | bytes 100
  21.9 24.8 %copy-start = (bf16[1024,1024]{1,0:T(8,128)(2,1)S(1)}, bf16[1024,1024]{1,0:T(8,128)(2,1)}, u32[]{:S(2)}) copy-start(bf16[1024,1024]{1,0:T(8,128)(2,1)} %wo_ref.1) | copy-start | bytes 6291460
  21.9 24.8 %copy-start.1 = (bf16[1024,512]{1,0:T(8,128)(2,1)S(1)}, bf16[1024,512]{1,0:T(8,128)(2,1)}, u32[]{:S(2)}) copy-start(bf16[1024,512]{1,0:T(8,128)(2,1)} %down_ref.1) | copy-start | bytes 3145732
  21.9 24.8 %copy-start.2 = (bf16[512,1024]{1,0:T(8,128)(2,1)S(1)}, bf16[512,1024]{1,0:T(8,128)(2,1)}, u32[]{:S(2)}) copy-start(bf16[512,1024]{1,0:T(8,128)(2,1)} %up_ref.1) | copy-start | bytes 3145732
  21.9 24.8 %copy-start.4 = (s32[64]{0:T(128)S(1)}, s32[64]{0:T(128)}, u32[]{:S(2)}) copy-start(s32[64]{0:T(128)} %param.17) | copy-start | bytes 772
  23.4 37.9 %copy-start.10 = (bf16[8,1024]{1,0:T(8,128)(2,1)S(1)}, bf16[8,1024]{1,0:T(8,128)(2,1)}, u32[]{:S(2)}) copy-start(bf16[8,1024]{1,0:T(8,128)(2,1)} %param.18) | copy-start | bytes 49156

commit v9 on v8

--- a/solution.py
+++ b/solution.py
@@ -264,7 +264,7 @@
         out_specs=[VMEM] * 4,
         scratch_shapes=[pltpu.VMEM(heads, jnp.float32)],
         compiler_params=params,
-        cost_estimate=AHEAD,
+        cost_estimate=NOTHING,
         name="attend",
     )(
         transfer_pages,

time: 62.3 us -> 62.1 us (level)
  no operation moved by 1% of the time
where the time goes in v9:
time: 62.1 us; the launch traced here: 61.8 us
  blocking collectives  57.4 us (92%)
  Pallas kernels  2.89 us (5%)
  local copies, waits for them, and re-layouts  0.76 us (1%)
  other arithmetic  0.63 us (1%)
    all_to_all x1, blocking collectives, body(): in_q = lax.all_to_all(out_q, around, 0, 0, tiled=True)  21 us
    all_to_all x1, blocking collectives, body(): lax.all_to_all(part.reshape(lax.axis_size('tensor'), -1, part.shape[1]),...  13.7 us
    all_to_all x1, blocking collectives, body(): back = lax.all_to_all(far, around, 0, 0, tiled=True)  12.3 us
    all_to_all x1, blocking collectives, body(): lax.all_to_all(copies, 'batch', 0, 0, tiled=True)  10.4 us
    pallas_call x1, Pallas kernels, body(): pl.pallas_call(attend_kernel, out_shape=[jax.ShapeDtypeStruct((peers, 2 *...  1.46 us

profile of v9, /device:TPU:1, one launch (start us, length us, event | category | flops | bytes accessed | tf_op | source)
XLA Modules:
  0.0 61.8 jit_solution(7631715030040847088)
XLA Ops:
  0.0 0.0 copy-start.5
  0.0 0.0 copy-start.4
  0.0 0.7 %copy-done.5 = s32[8,8]{1,0:T(8,128)S(1)} copy-done((s32[8,8]{1,0:T(8,128)S(1)}, s32[8,8]{1,0:T(8,128)}, u32[]{:S(2)}) %copy-start.5) | copy-done | bytes 280
  0.7 0.0 copy-done.4
  0.7 0.0 copy-start
  0.7 0.0 copy-start.6
  0.7 0.0 copy-start.7
  0.7 0.0 copy-start.8
  0.7 0.1 outgoing.1
  0.9 0.0 copy-start.1
  0.9 0.0 copy-start.2
  0.9 0.0 copy-start.3
  0.9 0.0 copy-start.9
  0.9 21.0 %all_to_all.20.in_q_ref = bf16[32,8,128]{2,1,0:T(8,128)(2,1)S(1)} all-to-all(bf16[32,8,128]{2,1,0:T(8,128)(2,1)S(1)} %outgoing.1), channel_id=1, replica_groups=mesh['inst'=4,'batch'=8,'tensor'=8] {'inst','batch'}, dimensions={0} | all-to-all | bytes 131072 | tf_op jit(solution)/shard_map/all_to_all | solution.py:258
  21.9 0.0 copy-done
  21.9 0.0 copy-done.6
  21.9 0.0 copy-done.7
  21.9 0.0 copy-done.8
  21.9 0.0 copy-start.10
  21.9 1.5 %attend.1 = (bf16[32,16,128]{2,1,0:T(8,128)(2,1)S(1)}, f32[8,8,128]{2,1,0:T(8,128)S(1)}, f32[8,8,128]{2,1,0:T(8,128)S(1)}, f32[8,8,128]{2,1,0:T(8,128)S(1)}) custom-call(s32[1,32]{1,0:T(1,128)S(1)} %copy-done.7, bf16[32,8,128]{2,1,0:T(8,128)(2,1)S(1)} %all_to_all.20.in_q_ref, bf16[64,128,256]{2,1,0:T(8,128)(2,1)S(1)} %copy-done, s32[8,8]{1,0:T(8,128)S(1)} %copy-done.5, ...), custom_call_target="tpu_custom_call" | custom-call | tf_op jit(solution)/shard_map/attend/pallas_call | solution.py:259
  23.4 12.3 %all_to_all.21.back_ref = bf16[32,16,128]{2,1,0:T(8,128)(2,1)S(1)} all-to-all(bf16[32,16,128]{2,1,0:T(8,128)(2,1)S(1)} %get-tuple-element.12), channel_id=1, replica_groups=mesh['inst'=4,'batch'=8,'tensor'=8] {'inst','batch'}, dimensions={0} | all-to-all | bytes 262144 | tf_op jit(solution)/shard_map/all_to_all | solution.py:278
  35.7 0.4 join.1
  36.1 10.4 %all_to_all.22 = bf16[8,8,1024]{2,1,0:T(8,128)(2,1)S(1)} all-to-all(bf16[8,8,1024]{2,1,0:T(8,128)(2,1)S(1)} %join.1), channel_id=1, replica_groups=mesh['inst'=4,'batch'=8,'tensor'=8] {'batch'}, dimensions={0} | all-to-all | bytes 262144 | tf_op jit(solution)/shard_map/all_to_all | solution.py:290
  46.5 0.0 copy-done.1
  46.5 0.0 copy-done.2
  46.5 0.0 copy-done.3
  46.5 0.0 copy-done.9
  46.5 0.9 %project.1 = bf16[64,1024]{1,0:T(8,128)(2,1)S(1)} custom-call(bf16[64,1024]{1,0:T(8,128)(2,1)S(1)} %bitcast.4, s32[1,64]{1,0:T(1,128)S(1)} %bitcast.7, bf16[1024,1024]{1,0:T(8,128)(2,1)S(1)} %copy-done.1, bf16[1024,512]{1,0:T(8,128)(2,1)S(1)} %copy-done.2, bf16[512,1024]{1,0:T(8,128)(2,1)S(1)} %copy-done.3), custom_call_target="tpu_custom_call" | custom-call | tf_op jit(solution)/shard_map/project/pallas_call | solution.py:291
  47.4 13.7 %all_to_all.23 = bf16[8,8,1024]{2,1,0:T(8,128)(2,1)S(1)} all-to-all(bf16[8,8,1024]{2,1,0:T(8,128)(2,1)S(1)} %bitcast.5), channel_id=1, replica_groups=mesh['inst'=4,'batch'=8,'tensor'=8] {'tensor'}, dimensions={0} | all-to-all | bytes 262144 | tf_op jit(solution)/shard_map/all_to_all | solution.py:299
  61.2 0.0 copy-done.10
  61.2 0.6 add_convert_fusion
  (2 shorter events, 0.0 us)
Async XLA Ops:
  0.0 0.7 %copy-start.5 = (s32[8,8]{1,0:T(8,128)S(1)}, s32[8,8]{1,0:T(8,128)}, u32[]{:S(2)}) copy-start(s32[8,8]{1,0:T(8,128)} %pages_ref.5) | copy-start | bytes 772
  0.0 0.7 %copy-start.4 = (bf16[8,1024]{1,0:T(8,128)(2,1)S(1)}, bf16[8,1024]{1,0:T(8,128)(2,1)}, u32[]{:S(2)}) copy-start(bf16[8,1024]{1,0:T(8,128)(2,1)} %q_ref.3) | copy-start | bytes 49156
  0.7 21.2 %copy-start = (bf16[64,128,256]{2,1,0:T(8,128)(2,1)S(1)}, bf16[64,128,256]{2,1,0:T(8,128)(2,1)}, u32[]{:S(2)}) copy-start(bf16[64,128,256]{2,1,0:T(8,128)(2,1)} %pool_ref.1) | copy-start | bytes 12582916
  0.7 21.2 %copy-start.6 = (bf16[8,256]{1,0:T(8,128)(2,1)S(1)}, bf16[8,256]{1,0:T(8,128)(2,1)}, u32[]{:S(2)}) copy-start(bf16[8,256]{1,0:T(8,128)(2,1)} %fresh_ref.1) | copy-start | bytes 12292
  0.7 21.2 %copy-start.7 = (s32[1,32]{1,0:T(1,128)S(1)}, s32[1,32]{1,0:T(1,128)}, u32[]{:S(2)}) copy-start(s32[1,32]{1,0:T(1,128)} %listed_ref.1) | copy-start | bytes 388
  0.7 21.2 %copy-start.8 = (s32[8]{0:T(128)S(1)}, s32[8]{0:T(128)}, u32[]{:S(2)}) copy-start(s32[8]{0:T(128)} %param.16) | copy-start | bytes 100
  0.9 45.6 %copy-start.1 = (bf16[1024,1024]{1,0:T(8,128)(2,1)S(1)}, bf16[1024,1024]{1,0:T(8,128)(2,1)}, u32[]{:S(2)}) copy-start(bf16[1024,1024]{1,0:T(8,128)(2,1)} %wo_ref.1) | copy-start | bytes 6291460
  0.9 45.6 %copy-start.2 = (bf16[1024,512]{1,0:T(8,128)(2,1)S(1)}, bf16[1024,512]{1,0:T(8,128)(2,1)}, u32[]{:S(2)}) copy-start(bf16[1024,512]{1,0:T(8,128)(2,1)} %down_ref.1) | copy-start | bytes 3145732
  0.9 45.6 %copy-start.3 = (bf16[512,1024]{1,0:T(8,128)(2,1)S(1)}, bf16[512,1024]{1,0:T(8,128)(2,1)}, u32[]{:S(2)}) copy-start(bf16[512,1024]{1,0:T(8,128)(2,1)} %up_ref.1) | copy-start | bytes 3145732
  0.9 45.6 %copy-start.9 = (s32[64]{0:T(128)S(1)}, s32[64]{0:T(128)}, u32[]{:S(2)}) copy-start(s32[64]{0:T(128)} %param.17) | copy-start | bytes 772
  21.9 39.3 %copy-start.10 = (bf16[8,1024]{1,0:T(8,128)(2,1)S(1)}, bf16[8,1024]{1,0:T(8,128)(2,1)}, u32[]{:S(2)}) copy-start(bf16[8,1024]{1,0:T(8,128)(2,1)} %param.18) | copy-start | bytes 49156

commit v10 on v6

--- a/solution.py
+++ b/solution.py
@@ -18,6 +18,7 @@
 NEVER = -1e30
 VMEM = pl.BlockSpec(memory_space=pltpu.VMEM)
 NT = (((1,), (1,)), ((), ()))
+NOTHING = pl.CostEstimate(flops=0, bytes_accessed=0, transcendentals=0)
 AHEAD = pl.CostEstimate(flops=100_000_000_000, bytes_accessed=400_000_000, transcendentals=0)
 
 
@@ -266,7 +267,7 @@
         in_specs=[VMEM, VMEM, VMEM],
         out_specs=VMEM,
         compiler_params=params,
-        cost_estimate=AHEAD,
+        cost_estimate=NOTHING,
         name="far",
     )(transfer_pages, in_q, key_value_pages)
     back = lax.all_to_all(far, around, 0, 0, tiled=True)
@@ -278,7 +279,7 @@
         out_specs=VMEM,
         scratch_shapes=[pltpu.VMEM(heads, jnp.float32), pltpu.VMEM(heads, jnp.float32)],
         compiler_params=params,
-        cost_estimate=AHEAD,
+        cost_estimate=NOTHING,
         name="join",
     )(
         request_pages,

time: 62.3 us -> 62.4 us (level)
  no operation moved by 1% of the time
where the time goes in v10:
time: 62.4 us; the launch traced here: 62.1 us
  blocking collectives  57.5 us (92%)
  Pallas kernels  3.03 us (5%)
  local copies, waits for them, and re-layouts  0.76 us (1%)
  other arithmetic  0.63 us (1%)
    all_to_all x1, blocking collectives, body(): in_q = lax.all_to_all(out_q, around, 0, 0, tiled=True)  21 us
    all_to_all x1, blocking collectives, body(): lax.all_to_all(part.reshape(lax.axis_size('tensor'), -1, part.shape[1]),...  13.7 us
    all_to_all x1, blocking collectives, body(): back = lax.all_to_all(far, around, 0, 0, tiled=True)  12.4 us
    all_to_all x1, blocking collectives, body(): lax.all_to_all(copies, 'batch', 0, 0, tiled=True)  10.4 us
    pallas_call x1, Pallas kernels, body(): pl.pallas_call(join_kernel, out_shape=jax.ShapeDtypeStruct((group, slots,...  1.26 us

profile of v10, /device:TPU:1, one launch (start us, length us, event | category | flops | bytes accessed | tf_op | source)
XLA Modules:
  0.0 62.1 jit_solution(12079746254123584005)
XLA Ops:
  0.0 0.0 copy-start.5
  0.0 0.0 copy-start.4
  0.0 0.7 %copy-done.5 = s32[8,8]{1,0:T(8,128)S(1)} copy-done((s32[8,8]{1,0:T(8,128)S(1)}, s32[8,8]{1,0:T(8,128)}, u32[]{:S(2)}) %copy-start.5) | copy-done | bytes 280
  0.7 0.0 copy-done.4
  0.7 0.0 copy-start
  0.7 0.0 copy-start.7
  0.7 0.1 outgoing.1
  0.9 0.0 copy-start.6
  0.9 0.0 copy-start.8
  0.9 21.0 %all_to_all.20.q_ref = bf16[32,8,128]{2,1,0:T(8,128)(2,1)S(1)} all-to-all(bf16[32,8,128]{2,1,0:T(8,128)(2,1)S(1)} %outgoing.1), channel_id=1, replica_groups=mesh['inst'=4,'batch'=8,'tensor'=8] {'inst','batch'}, dimensions={0} | all-to-all | bytes 131072 | tf_op jit(solution)/shard_map/all_to_all | solution.py:263
  21.9 0.0 copy-done
  21.9 0.0 copy-done.7
  21.9 0.0 copy-start.1
  21.9 0.0 copy-start.2
  21.9 0.0 copy-start.3
  21.9 0.0 copy-start.9
  21.9 0.7 %far.1 = bf16[32,16,128]{2,1,0:T(8,128)(2,1)S(1)} custom-call(s32[1,32]{1,0:T(1,128)S(1)} %copy-done.7, bf16[32,8,128]{2,1,0:T(8,128)(2,1)S(1)} %all_to_all.20.q_ref, bf16[64,128,256]{2,1,0:T(8,128)(2,1)S(1)} %copy-done), custom_call_target="tpu_custom_call" | custom-call | tf_op jit(solution)/shard_map/far/pallas_call | solution.py:264
  22.6 12.4 %all_to_all.21.back_ref = bf16[32,16,128]{2,1,0:T(8,128)(2,1)S(1)} all-to-all(bf16[32,16,128]{2,1,0:T(8,128)(2,1)S(1)} %far.1), channel_id=1, replica_groups=mesh['inst'=4,'batch'=8,'tensor'=8] {'inst','batch'}, dimensions={0} | all-to-all | bytes 262144 | tf_op jit(solution)/shard_map/all_to_all | solution.py:273
  35.1 0.0 copy-done.6
  35.1 0.0 copy-done.8
  35.1 0.0 copy-start.10
  35.1 1.3 %join.1 = bf16[8,8,1024]{2,1,0:T(8,128)(2,1)S(1)} custom-call(s32[8,8]{1,0:T(8,128)S(1)} %copy-done.5, s32[1,8]{1,0:T(1,128)S(1)} %bitcast.6, bf16[8,1024]{1,0:T(8,128)(2,1)S(1)} %copy-done.4, bf16[8,256]{1,0:T(8,128)(2,1)S(1)} %copy-done.6, bf16[64,128,256]{2,1,0:T(8,128)(2,1)S(1)} %copy-done, bf16[32,16,128]{2,1,0:T(8,128)(2,1)S(1)} %all_to_all.21.back_ref), custom_call_target="tpu_custom_call" | custom-call | tf_op jit(solution)/shard_map/join/pallas_call | solution.py:275
  36.3 10.4 %all_to_all.22 = bf16[8,8,1024]{2,1,0:T(8,128)(2,1)S(1)} all-to-all(bf16[8,8,1024]{2,1,0:T(8,128)(2,1)S(1)} %join.1), channel_id=1, replica_groups=mesh['inst'=4,'batch'=8,'tensor'=8] {'batch'}, dimensions={0} | all-to-all | bytes 262144 | tf_op jit(solution)/shard_map/all_to_all | solution.py:292
  46.8 0.0 copy-done.1
  46.8 0.0 copy-done.2
  46.8 0.0 copy-done.3
  46.8 0.0 copy-done.9
  46.8 0.9 %project.1 = bf16[64,1024]{1,0:T(8,128)(2,1)S(1)} custom-call(bf16[64,1024]{1,0:T(8,128)(2,1)S(1)} %bitcast.4, s32[1,64]{1,0:T(1,128)S(1)} %bitcast.7, bf16[1024,1024]{1,0:T(8,128)(2,1)S(1)} %copy-done.1, bf16[1024,512]{1,0:T(8,128)(2,1)S(1)} %copy-done.2, bf16[512,1024]{1,0:T(8,128)(2,1)S(1)} %copy-done.3), custom_call_target="tpu_custom_call" | custom-call | tf_op jit(solution)/shard_map/project/pallas_call | solution.py:293
  47.7 13.7 %all_to_all.23 = bf16[8,8,1024]{2,1,0:T(8,128)(2,1)S(1)} all-to-all(bf16[8,8,1024]{2,1,0:T(8,128)(2,1)S(1)} %bitcast.5), channel_id=1, replica_groups=mesh['inst'=4,'batch'=8,'tensor'=8] {'tensor'}, dimensions={0} | all-to-all | bytes 262144 | tf_op jit(solution)/shard_map/all_to_all | solution.py:301
  61.4 0.0 copy-done.10
  61.4 0.6 add_convert_fusion
  (2 shorter events, 0.0 us)
Async XLA Ops:
  0.0 0.7 %copy-start.5 = (s32[8,8]{1,0:T(8,128)S(1)}, s32[8,8]{1,0:T(8,128)}, u32[]{:S(2)}) copy-start(s32[8,8]{1,0:T(8,128)} %pages_ref.3) | copy-start | bytes 772
  0.0 0.7 %copy-start.4 = (bf16[8,1024]{1,0:T(8,128)(2,1)S(1)}, bf16[8,1024]{1,0:T(8,128)(2,1)}, u32[]{:S(2)}) copy-start(bf16[8,1024]{1,0:T(8,128)(2,1)} %q_ref.3) | copy-start | bytes 49156
  0.7 21.1 %copy-start = (bf16[64,128,256]{2,1,0:T(8,128)(2,1)S(1)}, bf16[64,128,256]{2,1,0:T(8,128)(2,1)}, u32[]{:S(2)}) copy-start(bf16[64,128,256]{2,1,0:T(8,128)(2,1)} %pool_ref.3) | copy-start | bytes 12582916
  0.7 21.1 %copy-start.7 = (s32[1,32]{1,0:T(1,128)S(1)}, s32[1,32]{1,0:T(1,128)}, u32[]{:S(2)}) copy-start(s32[1,32]{1,0:T(1,128)} %listed_ref.1) | copy-start | bytes 388
  0.9 34.2 %copy-start.6 = (bf16[8,256]{1,0:T(8,128)(2,1)S(1)}, bf16[8,256]{1,0:T(8,128)(2,1)}, u32[]{:S(2)}) copy-start(bf16[8,256]{1,0:T(8,128)(2,1)} %fresh_ref.1) | copy-start | bytes 12292
  0.9 34.2 %copy-start.8 = (s32[8]{0:T(128)S(1)}, s32[8]{0:T(128)}, u32[]{:S(2)}) copy-start(s32[8]{0:T(128)} %param.16) | copy-start | bytes 100
  21.9 24.9 %copy-start.1 = (bf16[1024,1024]{1,0:T(8,128)(2,1)S(1)}, bf16[1024,1024]{1,0:T(8,128)(2,1)}, u32[]{:S(2)}) copy-start(bf16[1024,1024]{1,0:T(8,128)(2,1)} %wo_ref.1) | copy-start | bytes 6291460
  21.9 24.9 %copy-start.2 = (bf16[1024,512]{1,0:T(8,128)(2,1)S(1)}, bf16[1024,512]{1,0:T(8,128)(2,1)}, u32[]{:S(2)}) copy-start(bf16[1024,512]{1,0:T(8,128)(2,1)} %down_ref.1) | copy-start | bytes 3145732
  21.9 24.9 %copy-start.3 = (bf16[512,1024]{1,0:T(8,128)(2,1)S(1)}, bf16[512,1024]{1,0:T(8,128)(2,1)}, u32[]{:S(2)}) copy-start(bf16[512,1024]{1,0:T(8,128)(2,1)} %up_ref.1) | copy-start | bytes 3145732
  21.9 24.9 %copy-start.9 = (s32[64]{0:T(128)S(1)}, s32[64]{0:T(128)}, u32[]{:S(2)}) copy-start(s32[64]{0:T(128)} %param.17) | copy-start | bytes 772
  35.1 26.4 %copy-start.10 = (bf16[8,1024]{1,0:T(8,128)(2,1)S(1)}, bf16[8,1024]{1,0:T(8,128)(2,1)}, u32[]{:S(2)}) copy-start(bf16[8,1024]{1,0:T(8,128)(2,1)} %param.18) | copy-start | bytes 49156
